TPU v7x, 32 devices: a whole 2x2x4 slice. The times are simulated.
32 devices in a mesh: snap: 8 (over z, y), rows: 4 (over x, core).
Axes of the slice: x: 2, y: 2, z: 4, core: 2. Of those that a mesh axis runs over, the one named last changes fastest.
Arguments:
- snapshots: bfloat16 [32, 128, 64, 128], P('snap', 'rows'), may hold values from -6 to 6
- cotangent: bfloat16 [32, 128, 64, 128], P('snap', 'rows'), may hold values from -6 to 6
- lengths: int32 [8], P('snap'), may hold values from 1 to 4, as said below
- slot_mask: int32 [32], P('snap'), may hold values from 0 to 1, as said below
- encoder_kernel: float32 [5, 5, 64, 128], replicated, may hold values from -0.15625 to 0.15625
- decoder_kernel: float32 [5, 5, 128, 64], replicated, may hold values from -0.21875 to 0.21875
- biases: float32 [192], replicated, may hold values from -1.5 to 1.5
- encoder_mom: float32 [5, 5, 64, 128], replicated, may hold values from -32 to 32
- decoder_mom: float32 [5, 5, 128, 64], replicated, may hold values from -16 to 16
- bias_mom: float32 [192], replicated, may hold values from -64 to 64
- encoder_ema: float32 [5, 5, 64, 128], replicated, may hold values from -0.15625 to 0.15625
- decoder_ema: float32 [5, 5, 128, 64], replicated, may hold values from -0.21875 to 0.21875
- bias_ema: float32 [192], replicated, may hold values from -1.5 to 1.5
Outputs:
- output: bfloat16 [32, 128, 64, 128], P('snap', 'rows')
- input_grad: bfloat16 [32, 128, 64, 128], P('snap', 'rows')
- encoder_grad: float32 [5, 5, 64, 128], replicated
- decoder_grad: float32 [5, 5, 128, 64], replicated
- bias_grad: float32 [192], replicated
- encoder_mom_new: float32 [5, 5, 64, 128], replicated
- decoder_mom_new: float32 [5, 5, 128, 64], replicated
- bias_mom_new: float32 [192], replicated
- encoder_ema_new: float32 [5, 5, 64, 128], replicated
- decoder_ema_new: float32 [5, 5, 128, 64], replicated
- bias_ema_new: float32 [192], replicated
- encoder_new: float32 [5, 5, 64, 128], replicated
- decoder_new: float32 [5, 5, 128, 64], replicated
- bias_new: float32 [192], replicated
- encoder_copy: bfloat16 [5, 5, 64, 128], replicated
- decoder_copy: bfloat16 [5, 5, 128, 64], replicated
- bias_copy: bfloat16 [192], replicated
Inputs may be any that keep to these rules, and one draw needn't show every extreme that they name: `slot_mask`: the first slot of every window is valid. `lengths`: every fourth window, starting with the first, is full.
All inputs are finite; a program needn't handle non-finite values.
Results may differ from a plain program's by a relative error of at most 0.0075.
Values may be sent and summed in bfloat16 or wider, within the bound.
No kernel may reach another device: no remote copies, remote signals or barrier semaphores. Data moves between devices by JAX's collectives and lax.ppermute only.
A program may use at most 128 MiB of HBM per device.

v0:
```python
import functools

import jax
import jax.numpy as jnp
from jax import lax
from jax.experimental import pallas as pl
from jax.experimental.pallas import tpu as pltpu
from jax.sharding import Mesh, PartitionSpec as P

MOMENTUM = 0.5
EMA_DECAY = 0.5
LEARN_RATE = 0.01
F32, BF16 = jnp.float32, jnp.bfloat16
XU, XD, CU, CD = 8, 7, 4, 3
NT = (((1,), (1,)), ((), ()))
KERNEL_ROWS = 1600
HALF_ROWS = 1792
BIAS_ROW, COUNT_ROW = 1600, 1601


def dot(a, b):
    return jnp.dot(a, b, preferred_element_type=F32)


def chunked(lo, hi, size, step):
    whole = (hi - lo) // size
    if whole == 1:
        step(lo, size)
    elif whole:
        pl.loop(0, whole)(lambda n: step(lo + n * size, size))
    rest = (hi - lo) % size
    if rest:
        step(hi - rest, rest)


def split_matrix():
    row = lax.broadcasted_iota(jnp.int32, (256, 256), 0)
    col = lax.broadcasted_iota(jnp.int32, (256, 256), 1)
    want = (col // 64 % 2) * 128 + (col % 64) * 2 + col // 128
    return jnp.where(row == want, 1.0, 0.0).astype(BF16)


def merge_matrix():
    row = lax.broadcasted_iota(jnp.int32, (256, 256), 0)
    col = lax.broadcasted_iota(jnp.int32, (256, 256), 1)
    want = (row // 64 % 2) * 128 + (row % 64) * 2 + row // 128
    return jnp.where(col == want, 1.0, 0.0).astype(BF16)


def column_before(v):
    return shifted(v, 1, 0)


def column_after(v):
    return shifted(v, 127, 63)


def shifted(v, by, edge):
    parts = []
    for h in range(v.shape[1] // 128):
        part = v[:, h * 128 : (h + 1) * 128]
        lane = lax.broadcasted_iota(jnp.int32, part.shape, 1) % 64
        parts.append(jnp.where(lane == edge, 0.0, pltpu.roll(part, by, axis=1)))
    return parts[0] if len(parts) == 1 else jnp.concatenate(parts, axis=1)


def split_rows(ref, rows, split):
    pieces = [
        jnp.concatenate([ref[2 * h, r], ref[2 * h + 1, r]], axis=1) for r in rows for h in range(2)
    ]
    y = dot(jnp.concatenate(pieces, axis=0), split)
    out = []
    for n in range(len(rows)):
        a, b = y[n * 128 : n * 128 + 64], y[n * 128 + 64 : n * 128 + 128]
        out.append([jnp.concatenate([a[:, p * 128 : p * 128 + 128], b[:, p * 128 : p * 128 + 128]], axis=1) for p in range(2)])
    return out


def merge_rows(v, merge):
    pieces = [
        jnp.concatenate([v[rho * 128 : rho * 128 + 64, h * 128 : h * 128 + 128], v[rho * 128 + 64 : rho * 128 + 128, h * 128 : h * 128 + 128]], axis=1)
        for rho in range(2)
        for h in range(2)
    ]
    y = dot(jnp.concatenate(pieces, axis=0), merge).astype(BF16)
    return [
        [y[(rho * 2 + n // 2) * 64 : (rho * 2 + n // 2) * 64 + 64, (n % 2) * 128 : (n % 2) * 128 + 128] for n in range(4)]
        for rho in range(2)
    ]


def up_weights(dest, taps, sign):
    for rho in range(2):
        for pi in range(2):
            for di in range(-1, 2):
                for dj in range(-1, 2):
                    a, b = 2 + sign * (2 * di - rho), 2 + sign * (2 * dj - pi)
                    inside = 0 <= a <= 4 and 0 <= b <= 4
                    block = taps[a, b].astype(BF16) if inside else jnp.zeros((64, 128), BF16)
                    r, c = (rho * 2 + pi) * 64, ((di + 1) * 3 + dj + 1) * 128
                    dest[r : r + 64, c : c + 128] = block


def lane_sums(v):
    ones = jnp.ones((8, v.shape[1]), F32)
    return lax.dot_general(ones, v, NT, precision=lax.Precision.HIGHEST, preferred_element_type=F32)[:1]


def step_kernel(
    R, U, x_hbm, c_hbm, hu, hd, we, wdt, bias, lens, mask,
    out, e_out, pay,
    xv, cv, xb, l3, slope, d5, we2, wd2, wb, dsum, esum, acc0, acc1, split_ref, merge_ref, sems,
):
    I = R // 2
    row_at = lax.axis_index("x") * 2 + lax.axis_index("core")
    row_last = lax.axis_size("x") * 2 - 1
    core = lax.axis_index("core")
    first, last = row_at == 0, row_at == row_last
    copies = [
        pltpu.make_async_copy(x_hbm, xv.at[:, XU : XU + R], sems.at[0]),
        pltpu.make_async_copy(hu.at[:, :XU], xv.at[:, :XU], sems.at[1]),
        pltpu.make_async_copy(hd.at[:, :XD], xv.at[:, XU + R : XU + R + XD], sems.at[2]),
        pltpu.make_async_copy(c_hbm, cv.at[:, CU : CU + R], sems.at[3]),
        pltpu.make_async_copy(hu.at[:, XU:], cv.at[:, :CU], sems.at[4]),
        pltpu.make_async_copy(hd.at[:, XD:], cv.at[:, CU + R : CU + R + CD], sems.at[5]),
    ]
    for c in copies:
        c.start()
    cv[:, CU + R + CD] = jnp.zeros((4, 64, 128), BF16)
    split_ref[...] = split_matrix()
    merge_ref[...] = merge_matrix()
    we2[...] = we[...].reshape(KERNEL_ROWS, 128).T.astype(BF16)
    wb[...] = jnp.concatenate([wdt[4 - q].reshape(320, 128) for q in range(5)], axis=0).T.astype(BF16)
    up_weights(wd2, wdt, 1)
    dsum[...] = jnp.zeros_like(dsum)
    esum[...] = jnp.zeros_like(esum)
    slot = lax.broadcasted_iota(jnp.int32, (1, 256), 1) // 64
    live_lane = jnp.zeros((1, 256), F32)
    count = jnp.float32(0)
    for n in range(4):
        valid = jnp.where((n < lens[0]) & (mask[n] > 0), 1.0, 0.0)
        count = count + valid
        live_lane = jnp.where(slot == n, valid, live_lane)
    for c in copies[:3]:
        c.wait()

    def columns(t, count):
        for n, (even, odd) in enumerate(split_rows(xv, [t + m for m in range(count)], split_ref[...])):
            for b, v in enumerate([column_before(even), column_before(odd), even, odd, column_after(even)]):
                xb[t + n, b * 64 : b * 64 + 64] = v.astype(BF16)

    chunked(0, XU + R + XD, 2 * U, columns)

    bias_enc = jnp.concatenate([bias[:128]] * 2, axis=1)

    def encode(u, count):
        for n in range(count):
            pre = dot(we2[...], xb[pl.ds(2 * (u + n), 5)].reshape(KERNEL_ROWS, 256)) + bias_enc
            grow = jnp.exp(jnp.minimum(pre, 0.0))
            lat = jnp.maximum(pre, 0.0) + (grow - 1.0)
            if isinstance(u, int):
                if u + n < 3:
                    lat = jnp.where(first, 0.0, lat)
                if u + n >= I + 3:
                    lat = jnp.where(last, 0.0, lat)
                if 2 <= u + n < I + 4:
                    slope[u + n - 2] = grow
            else:
                slope[u + n - 2] = grow
            l3[u + n, :128] = column_before(lat).astype(BF16)
            l3[u + n, 128:256] = lat.astype(BF16)
            l3[u + n, 256:] = column_after(lat).astype(BF16)

    chunked(0, 3, 3, encode)
    chunked(3, I + 3, U, encode)
    chunked(I + 3, I + 6, 3, encode)

    for c in copies[3:]:
        c.wait()
    bias_dec = jnp.concatenate([jnp.concatenate([bias[128:]] * 4, axis=0)] * 2, axis=1)

    def decode(w, count, own):
        for n in range(count):
            pre = dot(wd2[...], l3[pl.ds(w + n, 3)].reshape(9 * 128, 256)) + bias_dec
            grow = jnp.exp(jnp.minimum(pre, 0.0))
            if own:
                value = (jnp.maximum(pre, 0.0) + (grow - 1.0)).astype(BF16)
                for rho, slots in enumerate(merge_rows(value, merge_ref[...])):
                    for s, v in enumerate(slots):
                        out[s, 2 * (w + n - 2) + rho] = v
            total = jnp.zeros((64, 256), F32)
            for rho, halves in enumerate(split_rows(cv, [2 * (w + n), 2 * (w + n) + 1], split_ref[...])):
                even, odd = [
                    (halves[pi] * live_lane * grow[(rho * 2 + pi) * 64 : (rho * 2 + pi) * 64 + 64]).astype(BF16).astype(F32)
                    for pi in range(2)
                ]
                total = total + even + odd
                for b, v in enumerate([column_after(even), odd, even, column_before(odd), column_before(even)]):
                    d5[2 * (w + n) + rho, b * 64 : b * 64 + 64] = v.astype(BF16)
            if own:
                dsum[...] += total

    chunked(0, 2, 2, functools.partial(decode, own=False))
    chunked(2, I + 2, U, functools.partial(decode, own=True))
    chunked(I + 2, I + 4, 2, functools.partial(decode, own=False))

    def back(e, count, own):
        for n in range(count):
            v = (dot(wb[...], d5[pl.ds(2 * (e + n), 5)].reshape(KERNEL_ROWS, 256)) * slope[e + n]).astype(BF16)
            if own:
                esum[...] += v.astype(F32)
            elif e == 0:
                v = jnp.where(first, jnp.zeros_like(v), v)
            else:
                v = jnp.where(last, jnp.zeros_like(v), v)
            e_out[e + n] = v

    def kernel_grad(cols, cols_at, latent, latent_at, half, taps):
        def add(s, count):
            rows = [s + n for n in range(count)]
            lhs = jnp.concatenate([cols[cols_at + 2 * r] for r in rows], axis=1)
            rhs = jnp.concatenate([jnp.concatenate([latent(latent_at + r + d) for d in range(3)], axis=0) for r in rows], axis=1)
            even = lax.dot_general(lhs, rhs, NT, preferred_element_type=F32)
            lhs = jnp.concatenate([cols[cols_at + 2 * r + 1] for r in rows], axis=1)
            odd = lax.dot_general(lhs, rhs[128:], NT, preferred_element_type=F32)
            if isinstance(s, int) and s == 0:
                acc0[...] = even
                acc1[...] = odd
            else:
                acc0[...] += even
                acc1[...] += odd

        size = 2 * U
        add(0, size)
        chunked(size, I, size, add)
        for d in range(3):
            a = taps[0][d]
            pay[half, a * 320 : a * 320 + 320] = acc0[:, d * 128 : d * 128 + 128].astype(BF16)
        for d in range(2):
            a = taps[1][d]
            pay[half, a * 320 : a * 320 + 320] = acc1[:, d * 128 : d * 128 + 128].astype(BF16)

    enc_half, dec_half = core, 1 - core
    kernel_grad(d5, CU, lambda u: l3[u, 128:256], 2, dec_half, ((0, 2, 4), (1, 3)))
    chunked(0, 1, 1, functools.partial(back, own=False))
    chunked(1, I + 1, U, functools.partial(back, own=True))
    chunked(I + 1, I + 2, 1, functools.partial(back, own=False))
    kernel_grad(xb, XU, lambda e: e_out[e], 0, enc_half, ((4, 2, 0), (3, 1)))

    count = jnp.where(row_at == 0, count, 0.0)
    count_row = jnp.broadcast_to(count, (1, 128))
    dec_row = jnp.concatenate([lane_sums(dsum[...]), jnp.zeros((1, 64), F32)], axis=1)
    for half, row in ((enc_half, lane_sums(esum[...])), (dec_half, dec_row)):
        tail = jnp.concatenate([row, count_row, jnp.zeros((14, 128), F32)], axis=0)
        pay[half, KERNEL_ROWS : KERNEL_ROWS + 16] = tail.astype(BF16)
        pay[half, KERNEL_ROWS + 16 :] = jnp.zeros((HALF_ROWS - KERNEL_ROWS - 16, 128), BF16)


def input_grad_kernel(R, U, e_ref, we, tail, ig, e3, we3, merge_ref):
    I = R // 2
    merge_ref[...] = merge_matrix()
    up_weights(we3, we, -1)
    scale = 1.0 / tail[...].astype(F32)[1:2]
    scale = jnp.concatenate([scale] * 2, axis=1)

    def widen(e, count):
        for n in range(count):
            v = e_ref[e + n].astype(F32)
            e3[e + n, :128] = column_before(v).astype(BF16)
            e3[e + n, 128:256] = e_ref[e + n]
            e3[e + n, 256:] = column_after(v).astype(BF16)

    chunked(0, I + 2, U, widen)

    def scatter(s, count):
        for n in range(count):
            v = dot(we3[...], e3[pl.ds(s + n, 3)].reshape(9 * 128, 256)) * scale
            for rho, slots in enumerate(merge_rows(v.astype(BF16), merge_ref[...])):
                for k, piece in enumerate(slots):
                    ig[k, 2 * (s + n) + rho] = piece

    chunked(0, I, U, scatter)


def update_kernel(mine, other, tail, *refs):
    core = lax.axis_index("core")
    scale = 1.0 / tail[...].astype(F32)[1:2]
    a, b = mine[...].astype(F32), other[...].astype(F32)
    own_first = core == 0
    for n in range(2):
        grad = jnp.where(own_first, a if n == 0 else b, b if n == 0 else a) * scale
        weight, moment, average = [r[...] for r in refs[3 * n : 3 * n + 3]]
        grad_out, mom_out, ema_out, new_out, copy_out = refs[6 + 5 * n : 11 + 5 * n]
        mom = MOMENTUM * moment + grad
        new = weight - LEARN_RATE * (grad + MOMENTUM * mom)
        grad_out[...] = grad
        mom_out[...] = mom
        ema_out[...] = EMA_DECAY * average + (1.0 - EMA_DECAY) * new
        new_out[...] = new
        copy_out[...] = new.astype(BF16)


def advance(grad, weight, moment, average):
    moment_new = MOMENTUM * moment + grad
    weight_new = weight - LEARN_RATE * (grad + MOMENTUM * moment_new)
    average_new = EMA_DECAY * average + (1.0 - EMA_DECAY) * weight_new
    return (moment_new, average_new, weight_new)


def whole(shape, memory_space=pltpu.VMEM):
    return pl.BlockSpec(memory_space=memory_space)


def on_device(
    snapshots, cotangent, lengths, slot_mask, encoder_kernel, decoder_kernel, biases,
    encoder_mom, decoder_mom, bias_mom, encoder_ema, decoder_ema, bias_ema,
):
    slots, R, C, W = snapshots.shape
    I, U = R // 2, 4
    nx = lax.axis_size("x")
    peers = lax.axis_size("snap") * nx
    flat = ("x", "core")
    count = 2 * nx
    down = [(n, n + 1) for n in range(count - 1)]
    up = [(n + 1, n) for n in range(count - 1)]
    hu = lax.ppermute(jnp.concatenate([snapshots[:, R - XU :], cotangent[:, R - CU :]], axis=1), flat, down)
    hd = lax.ppermute(jnp.concatenate([snapshots[:, :XD], cotangent[:, :CD]], axis=1), flat, up)
    bias_wide = jnp.broadcast_to(biases[:, None], (192, 128))
    decoder_t = jnp.swapaxes(decoder_kernel, 2, 3)
    vmem, smem, anyspace = (pl.BlockSpec(memory_space=m) for m in (pltpu.VMEM, pltpu.SMEM, pl.ANY))
    params = pltpu.CompilerParams(vmem_limit_bytes=60 * 2**20)
    field = jax.ShapeDtypeStruct(snapshots.shape, BF16)
    output, e_rows, pay = pl.pallas_call(
        functools.partial(step_kernel, R, U),
        out_shape=[field, jax.ShapeDtypeStruct((I + 2, 128, 256), BF16), jax.ShapeDtypeStruct((2, HALF_ROWS, 128), BF16)],
        in_specs=[anyspace] * 4 + [vmem] * 3 + [smem] * 2,
        out_specs=[vmem] * 3,
        scratch_shapes=[
            pltpu.VMEM((4, XU + R + 8, 64, 128), BF16),
            pltpu.VMEM((4, CU + R + 4, 64, 128), BF16),
            pltpu.VMEM((XU + R + 8, 320, 256), BF16),
            pltpu.VMEM((I + 6, 384, 256), BF16),
            pltpu.VMEM((I + 2, 128, 256), F32),
            pltpu.VMEM((R + 8, 320, 256), BF16),
            pltpu.VMEM((128, KERNEL_ROWS), BF16),
            pltpu.VMEM((256, 1152), BF16),
            pltpu.VMEM((128, KERNEL_ROWS), BF16),
            pltpu.VMEM((64, 256), F32),
            pltpu.VMEM((128, 256), F32),
            pltpu.VMEM((320, 384), F32),
            pltpu.VMEM((320, 256), F32),
            pltpu.VMEM((256, 256), BF16),
            pltpu.VMEM((256, 256), BF16),
            pltpu.SemaphoreType.DMA((6,)),
        ],
        compiler_params=params,
        name="step",
    )(snapshots, cotangent, hu, hd, encoder_kernel, decoder_t, bias_wide, lengths, slot_mask)

    swap = [(0, 1), (1, 0)]
    recv = lax.ppermute(pay[1], "core", swap)
    part = (pay[0].astype(F32) + recv.astype(F32)).astype(BF16).reshape(peers, HALF_ROWS // peers, 128)
    parts = lax.all_to_all(part, ("snap", "x"), 0, 0, tiled=True)
    total = jnp.sum(parts.astype(F32), axis=0).astype(BF16)
    mine = lax.all_to_all(jnp.broadcast_to(total[None], part.shape), ("snap", "x"), 0, 0, tiled=True)
    mine = mine.reshape(HALF_ROWS, 128)
    other = lax.ppermute(mine, "core", swap)
    tail = mine[KERNEL_ROWS : KERNEL_ROWS + 16]
    input_grad = pl.pallas_call(
        functools.partial(input_grad_kernel, R, U),
        out_shape=field,
        in_specs=[vmem] * 3,
        out_specs=vmem,
        scratch_shapes=[
            pltpu.VMEM((I + 2, 384, 256), BF16),
            pltpu.VMEM((256, 1152), BF16),
            pltpu.VMEM((256, 256), BF16),
        ],
        compiler_params=params,
        cost_estimate=pl.CostEstimate(flops=2 * 4096 * 204800, bytes_accessed=4 << 20, transcendentals=0),
        name="input_grad",
    )(e_rows, encoder_kernel, tail)

    def rows(v):
        return v.reshape(KERNEL_ROWS, 128)

    def trows(v):
        return jnp.swapaxes(v, 2, 3).reshape(KERNEL_ROWS, 128)

    block = pl.BlockSpec((320, 128), lambda a: (a, 0))
    fixed = pl.BlockSpec((16, 128), lambda a: (0, 0))
    shape32 = jax.ShapeDtypeStruct((KERNEL_ROWS, 128), F32)
    shape16 = jax.ShapeDtypeStruct((KERNEL_ROWS, 128), BF16)
    results = pl.pallas_call(
        update_kernel,
        grid=(5,),
        out_shape=[shape32, shape32, shape32, shape32, shape16] * 2,
        in_specs=[block, block, fixed] + [block] * 6,
        out_specs=[block] * 10,
        compiler_params=params,
        name="update",
    )(
        mine, other, tail,
        rows(encoder_kernel), rows(encoder_mom), rows(encoder_ema),
        trows(decoder_kernel), trows(decoder_mom), trows(decoder_ema),
    )
    enc_grad, enc_mom, enc_ema, enc_new, enc_copy = [v.reshape(encoder_kernel.shape) for v in results[:5]]
    dec_grad, dec_mom, dec_ema, dec_new, dec_copy = [jnp.swapaxes(v.reshape(decoder_t.shape), 2, 3) for v in results[5:]]
    own_first = lax.axis_index("core") == 0
    mine_row, other_row = mine[BIAS_ROW].astype(F32), other[BIAS_ROW].astype(F32)
    enc_row, dec_row = jnp.where(own_first, mine_row, other_row), jnp.where(own_first, other_row, mine_row)
    bias_grad = jnp.concatenate([enc_row, dec_row[:C]]) / mine[COUNT_ROW, 0].astype(F32)
    bia_mom, bia_ema, bia_new = advance(bias_grad, biases, bias_mom, bias_ema)
    return (
        output, input_grad, enc_grad, dec_grad, bias_grad, enc_mom, dec_mom, bia_mom,
        enc_ema, dec_ema, bia_ema, enc_new, dec_new, bia_new, enc_copy, dec_copy, bia_new.astype(BF16),
    )


def solution(mesh):
    snap, rows = mesh.devices.shape
    split = Mesh(mesh.devices.reshape(snap, rows // 2, 2), ("snap", "x", "core"))
    field = P("snap", ("x", "core"), None, None)
    return jax.shard_map(
        on_device,
        mesh=split,
        in_specs=(field, field, P("snap"), P("snap")) + (P(),) * 9,
        out_specs=(field, field) + (P(),) * 15,
        check_vma=False,
    )
```

profile of v0, /device:TPU:1, one launch (start us, length us, event | category | flops | bytes accessed | tf_op | source)
XLA Modules:
  0.0 113.9 jit_solution(10530302898165721375)
XLA Ops:
  0.7 1.0 slice.37
  1.6 0.0 slice-start
  1.6 0.0 slice-start.1
  1.7 1.1 %slice.36 = bf16[4,8,64,128]{3,2,1,0:T(8,128)(2,1)S(1)} slice(bf16[4,32,64,128]{3,2,1,0:T(8,128)(2,1)} %x_hbm.1), slice={[0:4], [24:32], [0:64], [0:128]} | slice | bytes 1048576 | tf_op jit(solution)/shard_map/slice | solution.py:326
  2.8 0.0 copy-start.4
  2.8 0.1 pad_maximum_fusion
  2.9 4.5 %collective-permute-start = (bf16[4,12,64,128]{3,2,1,0:T(8,128)(2,1)S(1)}, bf16[4,12,64,128]{3,2,1,0:T(8,128)(2,1)S(1)}, u32[]{:S(2)}, u32[]{:S(2)}) collective-permute-start(bf16[4,12,64,128]{3,2,1,0:T(8,128)(2,1)S(1)} %pad_maximum_fusion), channel_id=1, source_target_pairs={{0,1},{1,2},{2,3},{4,5},{5,6},{6,7},{8,9},{9,10},{10,11},{12,13},{... | collective-permute-start | bytes 2359304 | tf_op jit(solution)/shard_map/ppermute | solution.py:326
  7.4 0.1 pad_maximum_fusion.1
  7.5 1.9 %collective-permute-start.1 = (bf16[4,10,64,128]{3,2,1,0:T(8,128)(2,1)S(1)}, bf16[4,10,64,128]{3,2,1,0:T(8,128)(2,1)S(1)}, u32[]{:S(2)}, u32[]{:S(2)}) collective-permute-start(bf16[4,10,64,128]{3,2,1,0:T(8,128)(2,1)S(1)} %pad_maximum_fusion.1), channel_id=1, source_target_pairs={{1,0},{2,1},{3,2},{5,4},{6,5},{7,6},{9,8},{10,9},{11,10},{13,12},{... | collective-permute-start | bytes 1966088 | tf_op jit(solution)/shard_map/ppermute | solution.py:327
  10.1 9.3 %collective-permute-done.1.hd = bf16[4,10,64,128]{3,2,1,0:T(8,128)(2,1)S(1)} collective-permute-done((bf16[4,10,64,128]{3,2,1,0:T(8,128)(2,1)S(1)}, bf16[4,10,64,128]{3,2,1,0:T(8,128)(2,1)S(1)}, u32[]{:S(2)}, u32[]{:S(2)}) %collective-permute-start.1) | collective-permute-done | bytes 655392 | tf_op jit(solution)/shard_map/ppermute | solution.py:327
  19.4 0.0 collective-permute-done.hu
  19.4 0.9 broadcast_in_dim.4.bias
  20.3 0.2 copy-done.1
  20.5 29.6 %step.1 = (bf16[4,32,64,128]{3,2,1,0:T(8,128)(2,1)}, bf16[18,128,256]{2,1,0:T(8,128)(2,1)}, bf16[2,1792,128]{2,1,0:T(8,128)(2,1)}) custom-call(bf16[4,32,64,128]{3,2,1,0:T(8,128)(2,1)} %x_hbm.1, bf16[4,32,64,128]{3,2,1,0:T(8,128)(2,1)} %c_hbm.1, bf16[4,12,64,128]{3,2,1,0:T(8,128)(2,1)} %copy-done.1, bf16[4,10,64,128]{3,2,1,0:T(8,128)(2,1)} %copy-done.2, ...), custom_call_target="tpu_custom_call" | custom-call | tf_op jit(solution)/shard_map/step/pallas_call | solution.py:333
  50.1 1.1 slice_bitcast_fusion
  51.2 0.1 collective-permute-start.2
  51.2 1.8 %collective-permute-done.2 = bf16[1792,128]{1,0:T(8,128)(2,1)S(1)} collective-permute-done((bf16[1792,128]{1,0:T(8,128)(2,1)S(1)}, bf16[1792,128]{1,0:T(8,128)(2,1)S(1)}, u32[]{:S(2)}, u32[]{:S(2)}) %collective-permute-start.2) | collective-permute-done | bytes 458784 | tf_op jit(solution)/shard_map/ppermute | solution.py:361
  53.1 1.1 %fusion = bf16[1792,128]{1,0:T(8,128)(2,1)S(1)} fusion(bf16[1792,128]{1,0:T(8,128)(2,1)S(1)} %collective-permute-done.2, bf16[2,1792,128]{2,1,0:T(8,128)(2,1)} %get-tuple-element.32), kind=kLoop, calls=%fused_computation.1 | loop fusion | flops 917504 | bytes 1376256 | tf_op jit(solution)/shard_map/convert_element_type | solution.py:362
  54.2 17.2 %all_to_all.10 = bf16[16,112,128]{2,1,0:T(8,128)(2,1)S(1)} all-to-all(bf16[16,112,128]{2,1,0:T(8,128)(2,1)S(1)} %bitcast.53), channel_id=1, replica_groups=mesh['snap'=8,'x'=2,'core'=2] {'snap','x'}, dimensions={0} | all-to-all | bytes 917504 | tf_op jit(solution)/shard_map/all_to_all | solution.py:363
  71.4 0.1 reduce_sum.12
  71.5 0.1 broadcast_in_dim.5
  71.6 15.7 %all_to_all.11 = bf16[16,112,128]{2,1,0:T(8,128)(2,1)S(1)} all-to-all(bf16[16,112,128]{2,1,0:T(8,128)(2,1)S(1)} %broadcast_in_dim.5), channel_id=1, replica_groups=mesh['snap'=8,'x'=2,'core'=2] {'snap','x'}, dimensions={0} | all-to-all | bytes 917504 | tf_op jit(solution)/shard_map/all_to_all | solution.py:365
  87.2 4.2 %collective-permute-start.3 = (bf16[1792,128]{1,0:T(8,128)(2,1)S(1)}, bf16[1792,128]{1,0:T(8,128)(2,1)S(1)}, u32[]{:S(2)}, u32[]{:S(2)}) collective-permute-start(bf16[1792,128]{1,0:T(8,128)(2,1)S(1)} %bitcast.48), channel_id=1, source_target_pairs={{0,1},{1,0},{2,3},{3,2},{4,5},{5,4},{6,7},{7,6},{8,9},{9,8},{10,11... | collective-permute-start | bytes 1376264 | tf_op jit(solution)/shard_map/ppermute | solution.py:367
  91.5 0.6 slice.48.tail
  92.0 0.5 slice.51
  93.2 0.0 copy-start.6
  93.2 0.0 copy-start.7
  93.2 12.2 %input_grad.1 = bf16[4,32,64,128]{3,2,1,0:T(8,128)(2,1)} custom-call(bf16[18,128,256]{2,1,0:T(8,128)(2,1)} %get-tuple-element.31.e_ref, f32[5,5,64,128]{3,2,1,0:T(8,128)} %we.3, bf16[16,128]{1,0:T(8,128)(2,1)} %slice.48.tail), custom_call_target="tpu_custom_call" | custom-call | flops 1677721600 | bytes 4194304 | tf_op jit(solution)/shard_map/input_grad/pallas_call | solution.py:369
  105.4 0.0 collective-permute-done.3.other
  105.4 0.7 fusion.2
  106.1 0.6 add_multiply_fusion
  106.7 7.2 %update.1 = (f32[1600,128]{1,0:T(8,128)}, f32[1600,128]{1,0:T(8,128)}, f32[1600,128]{1,0:T(8,128)}, f32[1600,128]{1,0:T(8,128)}, bf16[1600,128]{1,0:T(8,128)(2,1...) custom-call(bf16[1792,128]{1,0:T(8,128)(2,1)} %bitcast.52, ...), custom_call_target="tpu_custom_call" | custom-call | tf_op jit(solution)/shard_map/update/pallas_call | solution.py:394
  (16 shorter events, 0.0 us)
Async XLA Ops:
  1.6 5.8 %slice-start = ((bf16[4,32,64,128]{3,2,1,0:T(8,128)(2,1)}), bf16[4,7,64,128]{3,2,1,0:T(8,128)(2,1)S(1)}, s32[]{:S(2)}) async-start(bf16[4,32,64,128]{3,2,1,0:T(8,128)(2,1)} %x_hbm.1), calls=%async_computation.2 | async-start | bytes 917504 | tf_op jit(solution)/shard_map/slice | solution.py:327
  1.6 5.8 %slice-start.1 = ((bf16[4,32,64,128]{3,2,1,0:T(8,128)(2,1)}), bf16[4,3,64,128]{3,2,1,0:T(8,128)(2,1)S(1)}, s32[]{:S(2)}) async-start(bf16[4,32,64,128]{3,2,1,0:T(8,128)(2,1)} %c_hbm.1), calls=%async_computation.3 | async-start | bytes 393216 | tf_op jit(solution)/shard_map/slice | solution.py:327
  2.8 16.6 %copy-start.4 = (f32[192]{0:T(256)S(1)}, f32[192]{0:T(256)}, u32[]{:S(2)}) copy-start(f32[192]{0:T(256)} %param.19) | copy-start | bytes 2308
  2.9 16.5 %collective-permute-start = (bf16[4,12,64,128]{3,2,1,0:T(8,128)(2,1)S(1)}, bf16[4,12,64,128]{3,2,1,0:T(8,128)(2,1)S(1)}, u32[]{:S(2)}, u32[]{:S(2)}) collective-permute-start(bf16[4,12,64,128]{3,2,1,0:T(8,128)(2,1)S(1)} %pad_maximum_fusion), channel_id=1, source_target_pairs={{0,1},{1,2},{2,3},{4,5},{5,6},{6,7},{8,9},{9,10},{10,11},{12,13},{... | collective-permute-start | bytes 2359304 | tf_op jit(solution)/shard_map/ppermute | solution.py:326
  7.5 11.9 %collective-permute-start.1 = (bf16[4,10,64,128]{3,2,1,0:T(8,128)(2,1)S(1)}, bf16[4,10,64,128]{3,2,1,0:T(8,128)(2,1)S(1)}, u32[]{:S(2)}, u32[]{:S(2)}) collective-permute-start(bf16[4,10,64,128]{3,2,1,0:T(8,128)(2,1)S(1)} %pad_maximum_fusion.1), channel_id=1, source_target_pairs={{1,0},{2,1},{3,2},{5,4},{6,5},{7,6},{9,8},{10,9},{11,10},{13,12},{... | collective-permute-start | bytes 1966088 | tf_op jit(solution)/shard_map/ppermute | solution.py:327
  19.4 0.9 copy-start.2
  19.4 1.1 copy-start.1
  51.2 1.9 %collective-permute-start.2 = (bf16[1792,128]{1,0:T(8,128)(2,1)S(1)}, bf16[1792,128]{1,0:T(8,128)(2,1)S(1)}, u32[]{:S(2)}, u32[]{:S(2)}) collective-permute-start(bf16[1792,128]{1,0:T(8,128)(2,1)S(1)} %slice_bitcast_fusion), channel_id=1, source_target_pairs={{0,1},{1,0},{2,3},{3,2},{4,5},{5,4},{6,7},{7,6},{8,9},{9,8},{10,11... | collective-permute-start | bytes 1376264 | tf_op jit(solution)/shard_map/ppermute | solution.py:361
  87.2 18.2 %copy-start = (bf16[16,112,128]{2,1,0:T(8,128)(2,1)}, bf16[16,112,128]{2,1,0:T(8,128)(2,1)S(1)}, u32[]{:S(2)}) copy-start(bf16[16,112,128]{2,1,0:T(8,128)(2,1)S(1)} %all_to_all.11) | copy-start | bytes 1376260
  87.2 18.2 %collective-permute-start.3 = (bf16[1792,128]{1,0:T(8,128)(2,1)S(1)}, bf16[1792,128]{1,0:T(8,128)(2,1)S(1)}, u32[]{:S(2)}, u32[]{:S(2)}) collective-permute-start(bf16[1792,128]{1,0:T(8,128)(2,1)S(1)} %bitcast.48), channel_id=1, source_target_pairs={{0,1},{1,0},{2,3},{3,2},{4,5},{5,4},{6,7},{7,6},{8,9},{9,8},{10,11... | collective-permute-start | bytes 1376264 | tf_op jit(solution)/shard_map/ppermute | solution.py:367
  93.2 12.2 %copy-start.6 = (f32[192]{0:T(256)S(1)}, f32[192]{0:T(256)}, u32[]{:S(2)}) copy-start(f32[192]{0:T(256)} %param.22) | copy-start | bytes 2308
  93.2 12.9 %copy-start.7 = (f32[192]{0:T(256)S(1)}, f32[192]{0:T(256)}, u32[]{:S(2)}) copy-start(f32[192]{0:T(256)} %param.25) | copy-start | bytes 2308
  105.4 1.3 %copy-start.3 = (bf16[1792,128]{1,0:T(8,128)(2,1)}, bf16[1792,128]{1,0:T(8,128)(2,1)S(1)}, u32[]{:S(2)}) copy-start(bf16[1792,128]{1,0:T(8,128)(2,1)S(1)} %collective-permute-done.3.other) | copy-start | bytes 1376260
  106.1 7.8 %copy-start.5 = (f32[192]{0:T(256)}, f32[192]{0:T(256)S(1)}, u32[]{:S(2)}) copy-start(f32[192]{0:T(256)S(1)} %get-tuple-element.44) | copy-start | bytes 2308
where the time goes:
time: 115 us; the launch traced here: 114 us
  Pallas kernels  49 us (43%)
  blocking collectives  32.9 us (29%)
  waiting for transfers between devices  11.1 us (10%)
  starting transfers between devices  10.7 us (9%)
  local copies, waits for them, and re-layouts  5.49 us (5%)
  other arithmetic  2.57 us (2%)
  between operations  2.13 us (2%)
    pallas_call x1, Pallas kernels, on_device(): pl.pallas_call(functools.partial(step_kernel, R, U), out_shape=[field, ja...  29.6 us
    all_to_all x1, blocking collectives, on_device(): parts = lax.all_to_all(part, ('snap', 'x'), 0, 0, tiled=True)  17.2 us
    all_to_all x1, blocking collectives, on_device(): lax.all_to_all(jnp.broadcast_to(total[None], part.shape), ('snap', 'x'),...  15.7 us
    pallas_call x1, Pallas kernels, on_device(): pl.pallas_call(functools.partial(input_grad_kernel, R, U), out_shape=fiel...  12.2 us
    ppermute x1, waiting for transfers between devices, on_device(): lax.ppermute(jnp.concatenate([snapshots[:, :XD], cotangent[:, :CD]], axis...  9.33 us
    pallas_call x1, Pallas kernels, on_device(): pl.pallas_call(update_kernel, grid=(5,), out_shape=[shape32, shape32, sha...  7.23 us
    ppermute x1, starting transfers between devices, on_device(): lax.ppermute(jnp.concatenate([snapshots[:, R - XU:], cotangent[:, R - CU:...  4.51 us
    ppermute x1, starting transfers between devices, on_device(): other = lax.ppermute(mine, 'core', swap)  4.21 us
  transfers between devices with their start and end apart: 4, of which 2 were waited for; matrix products, arithmetic and copies ran while one was open for 1% of the time, Pallas kernels for 11%

commit v1 on v0

v1 whole, which is shorter than its diff:
```python
import functools

import jax
import jax.numpy as jnp
from jax import lax
from jax.experimental import pallas as pl
from jax.experimental.pallas import tpu as pltpu
from jax.sharding import Mesh, PartitionSpec as P

MOMENTUM = 0.5
EMA_DECAY = 0.5
LEARN_RATE = 0.01
F32, BF16 = jnp.float32, jnp.bfloat16
XH, CH = 8, 4
XU, XD = 8, 7
NT = (((1,), (1,)), ((), ()))
KERNEL_ROWS = 1600
INNER_MB, OUTER_MB, FIELD_MB, UPDATE_MB = 16, 16, 12, 12


GROUPS = KERNEL_ROWS // 16


def chunk_groups(peers):
    return -(-(GROUPS + peers // 2) // peers)


def headless(peers, half):
    n = max(0, peers - (peers * chunk_groups(peers) - GROUPS))
    return peers - n * (1 + half), peers - n * half


def chunk_runs(peers, half):
    size, at, runs = chunk_groups(peers), 0, []
    lo, hi = headless(peers, half)
    for p in range(peers):
        first = 0 if lo <= p < hi else 1
        count = min(size - first, GROUPS - at)
        runs.append((first * 16, at * 16, (at + count) * 16))
        at += count
    assert at == GROUPS
    return runs


def dot(a, b):
    return jnp.dot(a, b, preferred_element_type=F32)


def chunked(lo, hi, size, step):
    whole = (hi - lo) // size
    if whole == 1:
        step(lo, size)
    elif whole:
        pl.loop(0, whole)(lambda n: step(lo + n * size, size))
    rest = (hi - lo) % size
    if rest:
        step(hi - rest, rest)


def split_matrix():
    row = lax.broadcasted_iota(jnp.int32, (256, 256), 0)
    col = lax.broadcasted_iota(jnp.int32, (256, 256), 1)
    want = (col // 64 % 2) * 128 + (col % 64) * 2 + col // 128
    return jnp.where(row == want, 1.0, 0.0).astype(BF16)


def merge_matrix():
    row = lax.broadcasted_iota(jnp.int32, (256, 256), 0)
    col = lax.broadcasted_iota(jnp.int32, (256, 256), 1)
    want = (row // 64 % 2) * 128 + (row % 64) * 2 + row // 128
    return jnp.where(col == want, 1.0, 0.0).astype(BF16)


def column_before(v):
    return shifted(v, 1, 0)


def column_after(v):
    return shifted(v, 127, 63)


def shifted(v, by, edge):
    parts = []
    for h in range(v.shape[1] // 128):
        part = v[:, h * 128 : (h + 1) * 128]
        lane = lax.broadcasted_iota(jnp.int32, part.shape, 1) % 64
        parts.append(jnp.where(lane == edge, jnp.zeros_like(part), pltpu.roll(part, by, axis=1)))
    return parts[0] if len(parts) == 1 else jnp.concatenate(parts, axis=1)


def split_rows(rows, split):
    pieces = [jnp.concatenate([row(2 * h), row(2 * h + 1)], axis=1) for row in rows for h in range(2)]
    y = dot(jnp.concatenate(pieces, axis=0), split)
    out = []
    for n in range(len(rows)):
        a, b = y[n * 128 : n * 128 + 64], y[n * 128 + 64 : n * 128 + 128]
        out.append([jnp.concatenate([a[:, p * 128 : p * 128 + 128], b[:, p * 128 : p * 128 + 128]], axis=1) for p in range(2)])
    return out


def merge_rows(v, merge):
    pieces = [
        jnp.concatenate([v[rho * 128 : rho * 128 + 64, h * 128 : h * 128 + 128], v[rho * 128 + 64 : rho * 128 + 128, h * 128 : h * 128 + 128]], axis=1)
        for rho in range(2)
        for h in range(2)
    ]
    y = dot(jnp.concatenate(pieces, axis=0), merge).astype(BF16)
    return [
        [y[(rho * 2 + n // 2) * 64 : (rho * 2 + n // 2) * 64 + 64, (n % 2) * 128 : (n % 2) * 128 + 128] for n in range(4)]
        for rho in range(2)
    ]


def up_weights(dest, taps, sign):
    for rho in range(2):
        for pi in range(2):
            for di in range(-1, 2):
                for dj in range(-1, 2):
                    a, b = 2 + sign * (2 * di - rho), 2 + sign * (2 * dj - pi)
                    inside = 0 <= a <= 4 and 0 <= b <= 4
                    block = taps[a, b].astype(BF16) if inside else jnp.zeros((64, 128), BF16)
                    r, c = (rho * 2 + pi) * 64, ((di + 1) * 3 + dj + 1) * 128
                    dest[r : r + 64, c : c + 128] = block


def lane_sums(v):
    ones = jnp.ones((8, v.shape[1]), F32)
    return lax.dot_general(ones, v, NT, precision=lax.Precision.HIGHEST, preferred_element_type=F32)[:1]


def store_columns(xb, at, halves):
    even, odd = [v.astype(BF16) for v in halves]
    for b, v in enumerate([column_before(even), column_before(odd), even, odd, column_after(even)]):
        xb[at, b * 64 : b * 64 + 64] = v


def store_split(seeds, at, pair, live_lane):
    for rho, halves in enumerate(pair):
        for pi, v in enumerate(halves):
            row = (rho * 2 + pi) * 64
            seeds[at, row : row + 64] = (v * live_lane).astype(BF16)


def up(weights, rows, at):
    even = dot(weights[:128], rows[pl.ds(at, 3)].reshape(9 * 128, 256))
    odd = dot(weights[128:, 384:], rows[pl.ds(at + 1, 2)].reshape(6 * 128, 256))
    return jnp.concatenate([even, odd], axis=0)


def encode_row(u, I, ends, we2, bias, xb, l3, slope):
    pre = dot(we2[...], xb[pl.ds(2 * u, 5)].reshape(KERNEL_ROWS, 256)) + bias
    grow = jnp.exp(jnp.minimum(pre, 0.0))
    lat = jnp.maximum(pre, grow - 1.0)
    if ends is not None:
        if u < 3:
            lat = jnp.where(ends[0], 0.0, lat)
        if u >= I + 3:
            lat = jnp.where(ends[1], 0.0, lat)
    if ends is None or 2 <= u < I + 4:
        slope[u - 2] = grow
    lat = lat.astype(BF16)
    l3[u, :128] = column_before(lat)
    l3[u, 128:256] = lat
    l3[u, 256:] = column_after(lat)


def decode_row(w, own, wd2, bias, seeds, l3, d5, value, dsum):
    pre = up(wd2, l3, w) + bias
    grow = jnp.exp(jnp.minimum(pre, 0.0))
    if own:
        value[w - 2] = jnp.maximum(pre, grow - 1.0).astype(BF16)
    full = seeds[w].astype(F32) * grow
    if own:
        dsum[...] += (full[:64] + full[64:128]) + (full[128:192] + full[192:])
    back = full.astype(BF16)
    for rho in range(2):
        even, odd = [back[(rho * 2 + pi) * 64 : (rho * 2 + pi) * 64 + 64] for pi in range(2)]
        for b, v in enumerate([column_after(even), odd, even, column_before(odd), column_before(even)]):
            d5[2 * w + rho, b * 64 : b * 64 + 64] = v


def live_lanes(lens, mask):
    slot = lax.broadcasted_iota(jnp.int32, (1, 256), 1) // 64
    lanes, count = jnp.zeros((1, 256), F32), jnp.float32(0)
    for n in range(4):
        valid = jnp.where((n < lens[0]) & (mask[n] > 0), 1.0, 0.0)
        count = count + valid
        lanes = jnp.where(slot == n, valid, lanes)
    return lanes, count


def bias_tiles(bias):
    def column(row):
        count = row.shape[1]
        at = lax.broadcasted_iota(jnp.int32, (count, count), 0)
        to = lax.broadcasted_iota(jnp.int32, (count, count), 1)
        return jnp.sum(jnp.where(at == to, jnp.broadcast_to(row, (count, count)), 0.0), axis=1, keepdims=True)

    enc = column(bias[:, :128])
    dec = column(bias[:, 128:])
    return jnp.broadcast_to(enc, (128, 256)), jnp.broadcast_to(jnp.concatenate([dec] * 4, axis=0), (256, 256))


def halo_kernel(R, x_hbm, c_hbm, near, far, sems):
    core = lax.axis_index("core")
    copies = []
    for n, (dest, low) in enumerate(((near, core == 0), (far, core == 1))):
        for m, (src, rows, at) in enumerate(((x_hbm, XH, 0), (c_hbm, CH, XH))):
            start = jnp.where(low, R - rows, 0)
            copies.append(pltpu.make_async_copy(src.at[:, pl.ds(start, rows)], dest.at[:, at : at + rows], sems.at[2 * n + m]))
    for c in copies:
        c.start()
    for c in copies:
        c.wait()


def kernel_grad(rows, cols, cols_at, latent, latent_at):
    rhs = jnp.concatenate(
        [jnp.concatenate([latent(latent_at + s + d) for d in range(3)], axis=0) for s in rows], axis=1
    )
    even, odd = [jnp.concatenate([cols[cols_at + 2 * s + rho] for s in rows], axis=1) for rho in range(2)]
    return (
        lax.dot_general(even, rhs, NT, preferred_element_type=F32),
        lax.dot_general(odd, rhs[128:], NT, preferred_element_type=F32),
    )


def inner_kernel(
    R, U, x_hbm, c_hbm, we_hbm, wdt_hbm, bias, lens, mask,
    xb, l3, slope, d5, value, seeds, dsum, acc0, acc1, we2, wd2, wb, xv, cv, we, wdt, split_ref, sems,
):
    I = R // 2
    parts = 2
    step = R // parts
    x_copies = [
        pltpu.make_async_copy(x_hbm.at[:, n * step : n * step + step], xv.at[:, n * step : n * step + step], sems.at[n])
        for n in range(parts)
    ]
    c_copy = pltpu.make_async_copy(c_hbm, cv, sems.at[parts])
    w_copies = [
        pltpu.make_async_copy(we_hbm, we, sems.at[parts + 1]),
        pltpu.make_async_copy(wdt_hbm, wdt, sems.at[parts + 2]),
    ]
    for c in w_copies[:1] + x_copies + w_copies[1:] + [c_copy]:
        c.start()
    split_ref[...] = split_matrix()
    dsum[...] = jnp.zeros_like(dsum)
    live_lane, _ = live_lanes(lens, mask)
    bias_enc, bias_dec = bias_tiles(bias[...])

    def columns(t, count):
        rows = [lambda s, r=t + m: xv[s, r] for m in range(count)]
        for n, halves in enumerate(split_rows(rows, split_ref[...])):
            store_columns(xb, XU + t + n, halves)

    def cotangent(s, count):
        rows = [lambda k, r=2 * s + m: cv[k, r] for m in range(2 * count)]
        halves = split_rows(rows, split_ref[...])
        for n in range(count):
            store_split(seeds, s + n + 2, halves[2 * n : 2 * n + 2], live_lane)

    def encode(u, count):
        for n in range(count):
            encode_row(u + n, I, None, we2, bias_enc, xb, l3, slope)

    def decode(w, count):
        for n in range(count):
            decode_row(w + n, True, wd2, bias_dec, seeds, l3, d5, value, dsum)

    w_copies[0].wait()
    we2[...] = we[...].reshape(KERNEL_ROWS, 128).T.astype(BF16)
    for n, c in enumerate(x_copies):
        c.wait()
        chunked(n * step, n * step + step, U, columns)
    chunked(4, I + 2, U, encode)
    w_copies[1].wait()
    up_weights(wd2, wdt, 1)
    c_copy.wait()
    chunked(0, I, U, cotangent)
    chunked(4, I, U, decode)
    acc0[...], acc1[...] = kernel_grad(range(2, I - 2), d5, CH, lambda u: l3[u, 128:256], 2)
    wb[...] = jnp.concatenate([wdt[4 - q].reshape(320, 128) for q in range(5)], axis=0).T.astype(BF16)


def outer_kernel(
    R, U, near, far, bias, lens, mask, we2, wd2, wb,
    xb_in, l3_in, slope_in, d5_in, value_in, seeds_in, dsum_in, acc0_in, acc1_in,
    e_out, keep, send, xb, l3, slope, d5, value, seeds, dsum, acc0, acc1,
    e_rows, esum, split_ref, sem,
):
    I = R // 2
    core = lax.axis_index("core")
    row_at = lax.axis_index("x") * 2 + core
    ends = row_at == 0, row_at == lax.axis_size("x") * 2 - 1
    split_ref[...] = split_matrix()
    esum[...] = jnp.zeros_like(esum)
    live_lane, count = live_lanes(lens, mask)
    bias_enc, bias_dec = bias_tiles(bias[...])
    upper = core == 0

    def above(r):
        return lambda s: jnp.where(upper, far[s, r], near[s, r])

    def below(r):
        return lambda s: jnp.where(upper, near[s, r], far[s, r])

    rows = [above(r) for r in range(XU)] + [below(r) for r in range(XD)]
    for n, halves in enumerate(split_rows(rows, split_ref[...])):
        store_columns(xb, n if n < XU else R + n, halves)
    halves = split_rows([above(XH + r) for r in range(CH)] + [below(XH + r) for r in range(CH)], split_ref[...])
    for n, w in enumerate((0, 1, I + 2, I + 3)):
        store_split(seeds, w, halves[2 * n : 2 * n + 2], live_lane)
    for u in list(range(4)) + list(range(I + 2, I + 6)):
        encode_row(u, I, ends, we2, bias_enc, xb, l3, slope)
    for w in list(range(4)) + list(range(I, I + 4)):
        decode_row(w, 2 <= w < I + 2, wd2, bias_dec, seeds, l3, d5, value, dsum)

    def back(e, count, own):
        for n in range(count):
            v = dot(wb[...], d5[pl.ds(2 * (e + n), 5)].reshape(KERNEL_ROWS, 256)) * slope[e + n]
            if own:
                esum[...] += v
            else:
                v = jnp.where(ends[0] if e == 0 else ends[1], 0.0, v)
            e_rows[e + n] = v.astype(BF16)

    chunks, chunk_rows = keep.shape[:2]

    def put(half, even_taps, odd_taps):
        blocks = {a: (acc0, d) for d, a in enumerate(even_taps)} | {a: (acc1, d) for d, a in enumerate(odd_taps)}

        def into(dest):
            for a, (acc, d) in blocks.items():
                block = acc[:, d * 128 : d * 128 + 128].astype(BF16)
                for p, (first, lo, hi) in enumerate(chunk_runs(chunks, half)):
                    lo, hi, start = max(lo, a * 320), min(hi, a * 320 + 320), lo
                    if lo < hi:
                        dest[p, first + lo - start : first + hi - start] = block[lo - a * 320 : hi - a * 320]

        pl.when(core == half)(lambda: into(keep))
        pl.when(core != half)(lambda: into(send))

    even, odd = kernel_grad([0, 1, I - 2, I - 1], d5, CH, lambda u: l3[u, 128:256], 2)
    acc0[...] += even
    acc1[...] += odd
    put(1, (0, 2, 4), (1, 3))
    back(0, 1, False)
    chunked(1, I + 1, U, functools.partial(back, own=True))
    back(I + 1, 1, False)
    e_copy = pltpu.make_async_copy(e_rows, e_out, sem)
    e_copy.start()
    acc0[...], acc1[...] = kernel_grad(range(I), xb, XU, lambda e: e_rows[e], 0)
    put(0, (4, 2, 0), (3, 1))

    count_row = jnp.broadcast_to(jnp.where(row_at == 0, count, 0.0), (1, 128))
    dec_row = jnp.concatenate([lane_sums(dsum[...]), jnp.zeros((1, 64), F32)], axis=1)
    head = jnp.concatenate([count_row, lane_sums(esum[...]), dec_row, jnp.zeros((13, 128), F32)], axis=0).astype(BF16)
    other_head = jnp.concatenate([count_row, jnp.zeros((15, 128), F32)], axis=0).astype(BF16)

    def finish(half, dest):
        for p, (first, lo, hi) in enumerate(chunk_runs(chunks, half)):
            if first:
                dest[p, :16] = other_head if p else head
            end = first + hi - lo
            if end < chunk_rows:
                dest[p, end:] = jnp.zeros((chunk_rows - end, 128), BF16)

    for half in range(2):
        pl.when(core == half)(functools.partial(finish, half, keep))
        pl.when(core != half)(functools.partial(finish, half, send))
    e_copy.wait()


def field_copies(R, field, out, sems):
    step = R // 4
    return [pltpu.make_async_copy(field.at[:, n * step : n * step + step], out.at[:, n * step : n * step + step], sems.at[n]) for n in range(4)]


def merge_field(R, value, merge, field, out, sems):
    I = R // 2
    copies = field_copies(R, field, out, sems)
    for n, c in enumerate(copies):
        for s in range(n * I // 4, (n + 1) * I // 4):
            for rho, slots in enumerate(merge_rows(value[s], merge)):
                for k, piece in enumerate(slots):
                    field[k, 2 * s + rho] = piece
        c.start()
    return copies


def output_kernel(R, value, out, field, merge_ref, sems):
    merge_ref[...] = merge_matrix()
    for c in merge_field(R, value, merge_ref[...], field, out, sems):
        c.wait()


def input_grad_kernel(R, U, e_hbm, we_hbm, count, count_other, ig, e_rows, we, e3, we3, grads, field, merge_ref, sems):
    I = R // 2
    fetch = [pltpu.make_async_copy(we_hbm, we, sems.at[4]), pltpu.make_async_copy(e_hbm, e_rows, sems.at[5])]
    for c in fetch:
        c.start()
    merge_ref[...] = merge_matrix()
    scale = 1.0 / jnp.maximum(count[:1], count_other[:1])
    scale = jnp.concatenate([scale] * 2, axis=1)
    fetch[0].wait()
    up_weights(we3, we, -1)
    fetch[1].wait()

    def widen(e, count):
        for n in range(count):
            v = e_rows[e + n]
            e3[e + n, :128] = column_before(v)
            e3[e + n, 128:256] = v
            e3[e + n, 256:] = column_after(v)

    def scatter(s, count):
        for n in range(count):
            grads[s + n] = (up(we3, e3, s + n) * scale).astype(BF16)

    chunked(0, I + 2, I + 2, widen)
    chunked(0, I, U, scatter)
    for c in merge_field(R, grads, merge_ref[...], field, ig, sems):
        c.wait()


def total_kernel(parts, count, wide, total, sems):
    peers = parts.shape[0]
    total[...] = sum(parts[p].astype(F32) for p in range(peers)).astype(BF16)
    copies = [pltpu.make_async_copy(total, wide.at[p], sems.at[p]) for p in range(peers)]
    for c in copies:
        c.start()
    me = lax.axis_index("snap") * lax.axis_size("x") + lax.axis_index("x")
    core = lax.axis_index("core")
    lo, hi = [jnp.where(core == 0, a, b) for a, b in zip(headless(peers, 0), headless(peers, 1), strict=True)]
    row = jnp.where((lo <= me) & (me < hi), 0.0, total[:16].astype(F32)[:1])
    count[...] = jnp.broadcast_to(row, (8, 128))
    for c in copies:
        c.wait()


PARTS = 4


def update_rows(n, totals, scale, weights, staged, results, sems, before):
    copies, sent = [], 0
    for p, (first, lo, hi) in enumerate(chunk_runs(totals.shape[0], n)):
        if lo == hi:
            break
        before(hi)
        grad = totals[p, first : first + hi - lo].astype(F32) * scale
        mom, ema, new = advance(grad, *[r[lo:hi] for r in weights])
        for ref, v in zip(staged, (grad, mom, ema, new, new.astype(BF16)), strict=True):
            ref[lo:hi] = v
        if hi == KERNEL_ROWS or hi - sent >= KERNEL_ROWS // PARTS:
            for m in range(5):
                c = pltpu.make_async_copy(staged[m].at[sent:hi], results[5 * n + m].at[sent:hi], sems.at[len(copies)])
                c.start()
                copies.append(c)
            sent = hi
    for c in copies:
        c.wait()


def own_update_kernel(totals, *refs):
    sources, small, results, bias_out = refs[:6], refs[6:9], refs[9:19], refs[19:24]
    ahead, weights, staged, sems, out_sems = refs[24:27], refs[27:30], refs[30:35], refs[35], refs[36]
    head = totals[0, 0:16].astype(F32)
    scale = 1.0 / head[0:1]
    core = lax.axis_index("core")
    step = KERNEL_ROWS // PARTS

    def half(n):
        own = [
            [
                pltpu.make_async_copy(sources[3 * n + m].at[p * step : p * step + step], weights[m].at[p * step : p * step + step], sems.at[3 * p + m])
                for m in range(3)
            ]
            for p in range(PARTS)
        ]
        later = [pltpu.make_async_copy(sources[3 * (1 - n) + m], ahead[m], sems.at[3 * PARTS + m]) for m in range(3)]
        for c in sum(own, []) + later:
            c.start()
        waited = [0]

        def before(hi):
            while waited[0] * step < hi:
                for c in own[waited[0]]:
                    c.wait()
                waited[0] += 1

        update_rows(n, totals, scale, weights, staged, results, out_sems, before)
        for c in later:
            c.wait()

    pl.when(core == 0)(lambda: half(0))
    pl.when(core != 0)(lambda: half(1))
    grad = jnp.concatenate([head[1:2], head[2:3, :64]], axis=1) * scale[:, :1]
    mom, ema, new = advance(grad, *[r[...] for r in small])
    for ref, v in zip(bias_out, (grad, mom, ema, new, new.astype(BF16)), strict=True):
        ref[...] = v


def other_update_kernel(totals, *refs):
    weights, results, staged, out_sems = refs[:3], refs[13:23], refs[23:28], refs[28]
    scale = 1.0 / totals[0, 0:16].astype(F32)[0:1]
    core = lax.axis_index("core")

    def half(n):
        update_rows(n, totals, scale, weights, staged, results, out_sems, lambda hi: None)

    pl.when(core == 0)(lambda: half(1))
    pl.when(core != 0)(lambda: half(0))


def advance(grad, weight, moment, average):
    moment_new = MOMENTUM * moment + grad
    weight_new = weight - LEARN_RATE * (grad + MOMENTUM * moment_new)
    average_new = EMA_DECAY * average + (1.0 - EMA_DECAY) * weight_new
    return (moment_new, average_new, weight_new)


def on_device(
    snapshots, cotangent, lengths, slot_mask, encoder_kernel, decoder_kernel, biases,
    encoder_mom, decoder_mom, bias_mom, encoder_ema, decoder_ema, bias_ema,
):
    slots, R, C, W = snapshots.shape
    latent_ch = encoder_kernel.shape[3]
    I, U = R // 2, 16
    nx = lax.axis_size("x")
    peers = lax.axis_size("snap") * nx
    swap = [(0, 1), (1, 0)]
    decoder_t = jnp.swapaxes(decoder_kernel, 2, 3)
    vmem, smem, hbm = (pl.BlockSpec(memory_space=m) for m in (pltpu.VMEM, pltpu.SMEM, pltpu.HBM))

    def call(kernel, name, megabytes, flops, **kw):
        return pl.pallas_call(
            kernel,
            name=name,
            compiler_params=pltpu.CompilerParams(vmem_limit_bytes=megabytes * 2**20),
            cost_estimate=pl.CostEstimate(flops=flops, bytes_accessed=4 << 20, transcendentals=0),
            **kw,
        )

    def sds(*shape, dtype=BF16):
        return jax.ShapeDtypeStruct(shape, dtype)

    def in_vmem(v):
        return pltpu.with_memory_space_constraint(v, pltpu.VMEM)

    def in_hbm(v):
        return pltpu.with_memory_space_constraint(v, pltpu.HBM)

    conv = 2 * 4096 * 204800
    halo = sds(slots, XH + CH, C, W)
    near, far = call(
        functools.partial(halo_kernel, R), "halo", 4, 0,
        out_shape=[halo, halo],
        in_specs=[hbm] * 2,
        out_specs=[vmem] * 2,
        scratch_shapes=[pltpu.SemaphoreType.DMA((4,))],
    )(in_hbm(snapshots), in_hbm(cotangent))
    far = lax.ppermute(far, ("x", "core"), [pair for n in range(nx - 1) for pair in ((2 * n + 1, 2 * n + 2), (2 * n + 2, 2 * n + 1))])
    near = lax.ppermute(near, "core", swap)
    bias_row = biases.reshape(1, -1)

    field = pltpu.HBM(snapshots.shape, BF16)
    state = [
        sds(XU + R + 8, 320, 256), sds(I + 6, 384, 256), sds(I + 2, 128, 256, dtype=F32), sds(R + 8, 320, 256),
        sds(I, 256, 256), sds(I + 4, 256, 256), sds(64, 256, dtype=F32), sds(320, 384, dtype=F32), sds(320, 256, dtype=F32),
    ]
    *mid, we2, wd2, wb = call(
        functools.partial(inner_kernel, R, U), "inner", INNER_MB, 2 * conv,
        out_shape=state + [sds(128, KERNEL_ROWS), sds(256, 1152), sds(128, KERNEL_ROWS)],
        in_specs=[hbm] * 4 + [vmem] + [smem] * 2,
        out_specs=[vmem] * 12,
        scratch_shapes=[
            pltpu.VMEM(snapshots.shape, BF16),
            pltpu.VMEM(snapshots.shape, BF16),
            pltpu.VMEM(encoder_kernel.shape, F32),
            pltpu.VMEM(encoder_kernel.shape, F32),
            pltpu.VMEM((256, 256), BF16),
            pltpu.SemaphoreType.DMA((5,)),
        ],
    )(in_hbm(snapshots), in_hbm(cotangent), in_hbm(encoder_kernel), in_hbm(decoder_t), bias_row, lengths, slot_mask)
    chunk = sds(peers, 16 * chunk_groups(peers), 128)
    e_rows, keep, send, _, _, _, _, value, *_ = call(
        functools.partial(outer_kernel, R, U), "outer", OUTER_MB, 4 * conv,
        out_shape=[pltpu.HBM((I + 2, 128, 256), BF16), chunk, chunk] + state,
        in_specs=[vmem] * 3 + [smem] * 2 + [vmem] * 12,
        out_specs=[hbm] + [vmem] * 11,
        input_output_aliases={8 + n: 3 + n for n in range(9)},
        scratch_shapes=[
            pltpu.VMEM((I + 2, 128, 256), BF16),
            pltpu.VMEM((128, 256), F32),
            pltpu.VMEM((256, 256), BF16),
            pltpu.SemaphoreType.DMA,
        ],
    )(near, far, bias_row, lengths, slot_mask, we2, wd2, wb, *mid)

    recv = lax.ppermute(send, "core", swap)
    output = call(
        functools.partial(output_kernel, R), "output", FIELD_MB, conv // 4,
        out_shape=field,
        in_specs=[vmem],
        out_specs=hbm,
        scratch_shapes=[pltpu.VMEM(snapshots.shape, BF16), pltpu.VMEM((256, 256), BF16), pltpu.SemaphoreType.DMA((4,))],
    )(value)
    part = (keep.astype(F32) + recv.astype(F32)).astype(BF16)
    part, output = lax.optimization_barrier((part, output))
    parts = lax.all_to_all(part, ("snap", "x"), 0, 0, tiled=True)
    live, wide = call(
        total_kernel, "total", 4, 0,
        out_shape=[sds(8, 128, dtype=F32), pltpu.HBM(part.shape, BF16)],
        in_specs=[vmem],
        out_specs=[vmem, hbm],
        scratch_shapes=[pltpu.VMEM(part.shape[1:], BF16), pltpu.SemaphoreType.DMA((peers,))],
    )(parts)
    live_other = lax.ppermute(live, "core", swap)
    mine = lax.all_to_all(wide, ("snap", "x"), 0, 0, tiled=True)
    input_grad = call(
        functools.partial(input_grad_kernel, R, U), "input_grad", FIELD_MB, 4 * conv,
        out_shape=field,
        in_specs=[hbm, hbm, vmem, vmem],
        out_specs=hbm,
        scratch_shapes=[
            pltpu.VMEM((I + 2, 128, 256), BF16),
            pltpu.VMEM(encoder_kernel.shape, F32),
            pltpu.VMEM((I + 2, 384, 256), BF16),
            pltpu.VMEM((256, 1152), BF16),
            pltpu.VMEM((I, 256, 256), BF16),
            pltpu.VMEM(snapshots.shape, BF16),
            pltpu.VMEM((256, 256), BF16),
            pltpu.SemaphoreType.DMA((6,)),
        ],
    )(in_hbm(e_rows), in_hbm(encoder_kernel), live, live_other)
    mine, input_grad = lax.optimization_barrier((mine, input_grad))
    other = lax.ppermute(mine, "core", swap)

    def rows(v):
        return v.reshape(KERNEL_ROWS, 128)

    def trows(v):
        return jnp.swapaxes(v, 2, 3).reshape(KERNEL_ROWS, 128)

    params = [
        rows(encoder_kernel), rows(encoder_mom), rows(encoder_ema),
        trows(decoder_kernel), trows(decoder_mom), trows(decoder_ema),
    ]
    shape = (KERNEL_ROWS, 128)
    five = [pltpu.HBM(shape, F32)] * 4 + [pltpu.HBM(shape, BF16)]
    staged = [pltpu.VMEM(v.shape, v.dtype) for v in five]
    bias_shape = [sds(1, latent_ch + C, dtype=F32)] * 4 + [sds(1, latent_ch + C)]
    begun = call(
        own_update_kernel, "update_own", UPDATE_MB, 1 << 20,
        out_shape=five * 2 + bias_shape + [pltpu.VMEM(shape, F32)] * 3,
        in_specs=[vmem] + [hbm] * 6 + [vmem] * 3,
        out_specs=[hbm] * 10 + [vmem] * 8,
        scratch_shapes=[pltpu.VMEM(shape, F32)] * 3
        + staged
        + [pltpu.SemaphoreType.DMA((3 * PARTS + 3,)), pltpu.SemaphoreType.DMA((5 * PARTS,))],
    )(mine, *[in_hbm(v) for v in params], bias_row, bias_mom.reshape(1, -1), bias_ema.reshape(1, -1))
    bias_grad, bia_mom, bia_ema, bia_new, bia_copy = [v.reshape(biases.shape) for v in begun[10:15]]
    results = call(
        other_update_kernel, "update_other", UPDATE_MB, 1 << 20,
        out_shape=five * 2,
        in_specs=[vmem] * 4 + [hbm] * 10,
        out_specs=[hbm] * 10,
        input_output_aliases={4 + n: n for n in range(10)},
        scratch_shapes=staged + [pltpu.SemaphoreType.DMA((5 * PARTS,))],
    )(other, *[in_vmem(v) for v in begun[15:]], *[in_hbm(v) for v in begun[:10]])
    enc_grad, enc_mom, enc_ema, enc_new, enc_copy = [v.reshape(encoder_kernel.shape) for v in results[:5]]
    dec_grad, dec_mom, dec_ema, dec_new, dec_copy = [jnp.swapaxes(v.reshape(decoder_t.shape), 2, 3) for v in results[5:]]
    return (
        output, input_grad, enc_grad, dec_grad, bias_grad, enc_mom, dec_mom, bia_mom,
        enc_ema, dec_ema, bia_ema, enc_new, dec_new, bia_new, enc_copy, dec_copy, bia_copy,
    )


def solution(mesh):
    snap, rows = mesh.devices.shape
    split = Mesh(mesh.devices.reshape(snap, rows // 2, 2), ("snap", "x", "core"))
    field = P("snap", ("x", "core"), None, None)
    return jax.shard_map(
        on_device,
        mesh=split,
        in_specs=(field, field, P("snap"), P("snap")) + (P(),) * 9,
        out_specs=(field, field) + (P(),) * 15,
        check_vma=False,
    )
```

time: 115 us -> 75.5 us (0.66)
  blocking collectives: 32.9 us -> 17.5 us
  Pallas kernels: 49 us -> 35.9 us
  waiting for transfers between devices: 11.1 us -> 3.62 us
  local copies, waits for them, and re-layouts: 5.49 us -> 0.02 us
  starting transfers between devices: 10.7 us -> 15.8 us
  other arithmetic: 2.57 us -> 0.65 us
    all_to_all x1 -> x0, blocking collectives: 15.7 us -> none  [on_device(): lax.all_to_all(jnp.broadcast_to(total[None], part.shape), ('snap', 'x'),...]
    pallas_call x3 -> x8, Pallas kernels: 49 us -> 35.9 us  [the longest x1 10.2 us: on_device(): call(functools.partial(inner_kernel, R, U), 'inner', INNER_MB, 2 * conv,...]
    ppermute x3 -> x4, waiting for transfers between devices: 11.1 us -> 0.95 us  [the longest x1 0.82 us: on_device(): live_other = lax.ppermute(live, 'core', swap)]
    all_to_all x0 -> x1, starting transfers between devices: none -> 5.22 us  [on_device(): mine = lax.all_to_all(wide, ('snap', 'x'), 0, 0, tiled=True)]
    slice x9 -> x0, local copies, waits for them, and re-layouts: 3.23 us -> none  [the longest x1 1.14 us: on_device(): snapshots[:, R - XU:]]
    all_to_all x0 -> x1, waiting for transfers between devices: none -> 2.67 us  [on_device(): mine = lax.all_to_all(wide, ('snap', 'x'), 0, 0, tiled=True)]
    convert_element_type x2 -> x1, other arithmetic: 1.79 us -> 0.12 us  [on_device(): part = (keep.astype(F32) + recv.astype(F32)).astype(BF16)]
    ppermute x3 -> x4, starting transfers between devices: 6.5 us -> 6.32 us  [the longest x1 4.47 us: on_device(): lax.ppermute(far, ('x', 'core'), [pair for n in range(nx - 1) for pair in...]
  transfers between devices with their start and end apart: 4 -> 6, of which waited for: 2 -> 3; matrix products, arithmetic and copies ran while one was open for 1% -> 1% of each run, Pallas kernels for 11% -> 29%
where the time goes in v1:
time: 75.5 us; the launch traced here: 75.1 us
  Pallas kernels  35.9 us (48%)
  blocking collectives  17.5 us (23%)
  starting transfers between devices  15.8 us (21%)
  waiting for transfers between devices  3.62 us (5%)
  between operations  1.6 us (2%)
    all_to_all x1, blocking collectives, on_device(): parts = lax.all_to_all(part, ('snap', 'x'), 0, 0, tiled=True)  17.5 us
    pallas_call x1, Pallas kernels, on_device(): call(functools.partial(inner_kernel, R, U), 'inner', INNER_MB, 2 * conv,...  10.2 us
    pallas_call x1, Pallas kernels, on_device(): call(functools.partial(outer_kernel, R, U), 'outer', OUTER_MB, 4 * conv,...  10.1 us
    pallas_call x1, Pallas kernels, on_device(): call(functools.partial(input_grad_kernel, R, U), 'input_grad', FIELD_MB,...  5.48 us
    all_to_all x1, starting transfers between devices, on_device(): mine = lax.all_to_all(wide, ('snap', 'x'), 0, 0, tiled=True)  5.22 us
    ppermute x1, starting transfers between devices, on_device(): lax.ppermute(far, ('x', 'core'), [pair for n in range(nx - 1) for pair in...  4.47 us
    ppermute x1, starting transfers between devices, on_device(): other = lax.ppermute(mine, 'core', swap)  4.21 us
    pallas_call x1, Pallas kernels, on_device(): call(own_update_kernel, 'update_own', UPDATE_MB, 1 << 20, out_shape=five...  4.16 us
  transfers between devices with their start and end apart: 6, of which 3 were waited for; matrix products, arithmetic and copies ran while one was open for 1% of the time, Pallas kernels for 29%

profile of v1, /device:TPU:1, one launch (start us, length us, event | category | flops | bytes accessed | tf_op | source)
XLA Modules:
  0.0 75.1 jit_solution(8770585413668972592)
XLA Ops:
  0.7 0.0 copy-start.3
  0.7 0.0 copy-start
  0.7 1.4 %halo.1 = (bf16[4,12,64,128]{3,2,1,0:T(8,128)(2,1)S(1)}, bf16[4,12,64,128]{3,2,1,0:T(8,128)(2,1)S(1)}) custom-call(bf16[4,32,64,128]{3,2,1,0:T(8,128)(2,1)} %x_hbm.3, bf16[4,32,64,128]{3,2,1,0:T(8,128)(2,1)} %c_hbm.3), custom_call_target="tpu_custom_call" | custom-call | bytes 4194304 | tf_op jit(solution)/shard_map/halo/pallas_call | solution.py:555
  2.1 0.1 collective-permute-start
  2.2 4.5 %collective-permute-start.1 = (bf16[4,12,64,128]{3,2,1,0:T(8,128)(2,1)S(1)}, bf16[4,12,64,128]{3,2,1,0:T(8,128)(2,1)S(1)}, u32[]{:S(2)}, u32[]{:S(2)}) collective-permute-start(bf16[4,12,64,128]{3,2,1,0:T(8,128)(2,1)S(1)} %get-tuple-element.70), channel_id=1, source_target_pairs={{1,2},{2,1},{5,6},{6,5},{9,10},{10,9},{13,14},{14,13},{17,18},{18,... | collective-permute-start | bytes 2359304 | tf_op jit(solution)/shard_map/ppermute | solution.py:562
  7.3 0.0 copy-done.3
  7.3 0.0 copy-done
  7.3 10.2 %inner.1 = (bf16[48,320,256]{2,1,0:T(8,128)(2,1)S(1)}, bf16[22,384,256]{2,1,0:T(8,128)(2,1)S(1)}, f32[18,128,256]{2,1,0:T(8,128)S(1)}, bf16[40,320,256]{2,1,0:T(...) custom-call(bf16[4,32,64,128]{3,2,1,0:T(8,128)(2,1)} %x_hbm.3, ...), custom_call_target="tpu_custom_call" | custom-call | flops 3355443200 | bytes 4194304 | tf_op jit(solution)/shard_map/inner/pallas_call | solution.py:571
  17.5 0.0 collective-permute-done.near
  17.6 0.0 collective-permute-done.1.far
  17.6 10.1 %outer.1 = (bf16[18,128,256]{2,1,0:T(8,128)(2,1)}, bf16[16,112,128]{2,1,0:T(8,128)(2,1)S(1)}, bf16[16,112,128]{2,1,0:T(8,128)(2,1)S(1)}, bf16[48,320,256]{2,1,0:...) custom-call(bf16[4,12,64,128]{3,2,1,0:T(8,128)(2,1)S(1)} %collective, ...), custom_call_target="tpu_custom_call", output_to_operand_aliasing={{3}: (8, {}), {4}: (9, {}), {5}: (10, {}), {6}: (11, {}), {... | custom-call | flops 6710886400 | bytes 4194304 | tf_op jit(solution)/shard_map/outer/pallas_call | solution.py:586
  27.6 0.1 collective-permute-start.2
  27.7 1.7 %output.1 = bf16[4,32,64,128]{3,2,1,0:T(8,128)(2,1)} custom-call(bf16[16,256,256]{2,1,0:T(8,128)(2,1)S(1)} %get-tuple-element.85.value), custom_call_target="tpu_custom_call" | custom-call | flops 419430400 | bytes 4194304 | tf_op jit(solution)/shard_map/output/pallas_call | solution.py:601
  29.4 0.1 collective-permute-done.2
  29.5 0.1 add_convert_fusion
  29.6 17.5 %all_to_all.10.parts = bf16[16,112,128]{2,1,0:T(8,128)(2,1)S(1)} all-to-all(bf16[16,112,128]{2,1,0:T(8,128)(2,1)S(1)} %add_convert_fusion), channel_id=1, replica_groups=mesh['snap'=8,'x'=2,'core'=2] {'snap','x'}, dimensions={0} | all-to-all | bytes 917504 | tf_op jit(solution)/shard_map/all_to_all | solution.py:610
  47.2 0.9 %total.1 = (f32[8,128]{1,0:T(8,128)S(1)}, bf16[16,112,128]{2,1,0:T(8,128)(2,1)}) custom-call(bf16[16,112,128]{2,1,0:T(8,128)(2,1)S(1)} %all_to_all.10.parts), custom_call_target="tpu_custom_call" | custom-call | bytes 4194304 | tf_op jit(solution)/shard_map/total/pallas_call | solution.py:611
  48.1 5.2 %all-to-all-start.1 = ((bf16[16,112,128]{2,1,0:T(8,128)(2,1)}), bf16[16,112,128]{2,1,0:T(8,128)(2,1)S(1)}, u32[]{:S(2)}, u32[]{:S(2)}) async-start(bf16[16,112,128]{2,1,0:T(8,128)(2,1)} %get-tuple-element.88), calls=%async_computation.1 | async-start | bytes 917504 | tf_op jit(solution)/shard_map/all_to_all | solution.py:619
  53.4 1.7 %collective-permute-start.3 = (f32[8,128]{1,0:T(8,128)S(1)}, f32[8,128]{1,0:T(8,128)S(1)}, u32[]{:S(2)}, u32[]{:S(2)}) collective-permute-start(f32[8,128]{1,0:T(8,128)S(1)} %get-tuple-element.90.count), channel_id=1, source_target_pairs={{0,1},{1,0},{2,3},{3,2},{4,5},{5,4},{6,7},{7,6},{8,9},{9,8},{10,11... | collective-permute-start | bytes 12296 | tf_op jit(solution)/shard_map/ppermute | solution.py:618
  55.0 0.8 %collective-permute-done.3.count_other = f32[8,128]{1,0:T(8,128)S(1)} collective-permute-done((f32[8,128]{1,0:T(8,128)S(1)}, f32[8,128]{1,0:T(8,128)S(1)}, u32[]{:S(2)}, u32[]{:S(2)}) %collective-permute-start.3) | collective-permute-done | bytes 4128 | tf_op jit(solution)/shard_map/ppermute | solution.py:618
  55.8 0.0 copy-start.1
  55.9 0.0 copy-start.2
  55.9 5.5 %input_grad.1 = bf16[4,32,64,128]{3,2,1,0:T(8,128)(2,1)} custom-call(bf16[18,128,256]{2,1,0:T(8,128)(2,1)} %get-tuple-element.89.e_hbm, f32[5,5,64,128]{3,2,1,0:T(8,128)} %we_hbm.3, f32[8,128]{1,0:T(8,128)S(1)} %get-tuple-element.90.count, f32[8,128]{1,0:T(8,128)S(1)} %collective-permute-done.3.count_other), custom_call_target="tpu_custom_call" | custom-call | flops 6710886400 | bytes 4194304 | tf_op jit(solution)/shard_map/input_grad/pallas_call | solution.py:620
  61.3 2.7 %all-to-all-done.1.totals = bf16[16,112,128]{2,1,0:T(8,128)(2,1)S(1)} async-done(((bf16[16,112,128]{2,1,0:T(8,128)(2,1)}), bf16[16,112,128]{2,1,0:T(8,128)(2,1)S(1)}, u32[]{:S(2)}, u32[]{:S(2)}) %all-to-all-start.1) | async-done | bytes 458784 | tf_op jit(solution)/shard_map/all_to_all | solution.py:619
  64.0 4.2 %collective-permute-start.4 = (bf16[16,112,128]{2,1,0:T(8,128)(2,1)S(1)}, bf16[16,112,128]{2,1,0:T(8,128)(2,1)S(1)}, u32[]{:S(2)}, u32[]{:S(2)}) collective-permute-start(bf16[16,112,128]{2,1,0:T(8,128)(2,1)S(1)} %all-to-all-done.1.totals), channel_id=1, source_target_pairs={{0,1},{1,0},{2,3},{3,2},{4,5},{5,4},{6,7},{7,6},{8,9},{9,8},{10,11... | collective-permute-start | bytes 1376264 | tf_op jit(solution)/shard_map/ppermute | solution.py:637
  68.2 0.0 copy-done.1
  68.2 0.0 copy-done.2
  68.2 4.2 %update_own.1 = (f32[1600,128]{1,0:T(8,128)}, f32[1600,128]{1,0:T(8,128)}, f32[1600,128]{1,0:T(8,128)}, f32[1600,128]{1,0:T(8,128)}, bf16[1600,128]{1,0:T(8,128)...) custom-call(bf16[16,112,128]{2,1,0:T(8,128)(2,1)S(1)} %all-to-all-do, ...), custom_call_target="tpu_custom_call" | custom-call | flops 1048576 | bytes 4194304 | tf_op jit(solution)/shard_map/update_own/pallas_call | solution.py:653
  72.4 0.5 reduce
  72.9 0.0 collective-permute-done.4.totals
  72.9 2.0 %update_other.1 = (f32[1600,128]{1,0:T(8,128)}, f32[1600,128]{1,0:T(8,128)}, f32[1600,128]{1,0:T(8,128)}, f32[1600,128]{1,0:T(8,128)}, bf16[1600,128]{1,0:T(8,12...) custom-call(bf16[16,112,128]{2,1,0:T(8,128)(2,1)S(1)} %collective-pe, ...), custom_call_target="tpu_custom_call", output_to_operand_aliasing={{0}: (4, {}), {1}: (5, {}), {2}: (6, {}), {3}: (7, {}), {4}... | custom-call | flops 1048576 | bytes 4194304 | tf_op jit(solution)/shard_map/update_other/pallas_call | solution.py:663
Async XLA Ops:
  0.7 6.7 %copy-start.3 = (s32[4]{0:T(128)S(1)}, s32[4]{0:T(128)}, u32[]{:S(2)}) copy-start(s32[4]{0:T(128)} %mask.3) | copy-start | bytes 52
  0.7 6.7 %copy-start = (f32[192]{0:T(256)S(1)}, f32[192]{0:T(256)}, u32[]{:S(2)}) copy-start(f32[192]{0:T(256)} %param.19) | copy-start | bytes 2308
  2.1 15.5 %collective-permute-start = (bf16[4,12,64,128]{3,2,1,0:T(8,128)(2,1)S(1)}, bf16[4,12,64,128]{3,2,1,0:T(8,128)(2,1)S(1)}, u32[]{:S(2)}, u32[]{:S(2)}) collective-permute-start(bf16[4,12,64,128]{3,2,1,0:T(8,128)(2,1)S(1)} %get-tuple-element.69), channel_id=1, source_target_pairs={{0,1},{1,0},{2,3},{3,2},{4,5},{5,4},{6,7},{7,6},{8,9},{9,8},{10,11... | collective-permute-start | bytes 2359304 | tf_op jit(solution)/shard_map/ppermute | solution.py:563
  2.2 15.4 %collective-permute-start.1 = (bf16[4,12,64,128]{3,2,1,0:T(8,128)(2,1)S(1)}, bf16[4,12,64,128]{3,2,1,0:T(8,128)(2,1)S(1)}, u32[]{:S(2)}, u32[]{:S(2)}) collective-permute-start(bf16[4,12,64,128]{3,2,1,0:T(8,128)(2,1)S(1)} %get-tuple-element.70), channel_id=1, source_target_pairs={{1,2},{2,1},{5,6},{6,5},{9,10},{10,9},{13,14},{14,13},{17,18},{18,... | collective-permute-start | bytes 2359304 | tf_op jit(solution)/shard_map/ppermute | solution.py:562
  27.6 1.9 %collective-permute-start.2 = (bf16[16,112,128]{2,1,0:T(8,128)(2,1)S(1)}, bf16[16,112,128]{2,1,0:T(8,128)(2,1)S(1)}, u32[]{:S(2)}, u32[]{:S(2)}) collective-permute-start(bf16[16,112,128]{2,1,0:T(8,128)(2,1)S(1)} %get-tuple-element.84), channel_id=1, source_target_pairs={{0,1},{1,0},{2,3},{3,2},{4,5},{5,4},{6,7},{7,6},{8,9},{9,8},{10,11... | collective-permute-start | bytes 1376264 | tf_op jit(solution)/shard_map/ppermute | solution.py:600
  48.1 15.9 %all-to-all-start.1 = ((bf16[16,112,128]{2,1,0:T(8,128)(2,1)}), bf16[16,112,128]{2,1,0:T(8,128)(2,1)S(1)}, u32[]{:S(2)}, u32[]{:S(2)}) async-start(bf16[16,112,128]{2,1,0:T(8,128)(2,1)} %get-tuple-element.88), calls=%async_computation.1 | async-start | bytes 917504 | tf_op jit(solution)/shard_map/all_to_all | solution.py:619
  53.4 2.5 %collective-permute-start.3 = (f32[8,128]{1,0:T(8,128)S(1)}, f32[8,128]{1,0:T(8,128)S(1)}, u32[]{:S(2)}, u32[]{:S(2)}) collective-permute-start(f32[8,128]{1,0:T(8,128)S(1)} %get-tuple-element.90.count), channel_id=1, source_target_pairs={{0,1},{1,0},{2,3},{3,2},{4,5},{5,4},{6,7},{7,6},{8,9},{9,8},{10,11... | collective-permute-start | bytes 12296 | tf_op jit(solution)/shard_map/ppermute | solution.py:618
  55.8 12.4 %copy-start.1 = (f32[192]{0:T(256)S(1)}, f32[192]{0:T(256)}, u32[]{:S(2)}) copy-start(f32[192]{0:T(256)} %param.22) | copy-start | bytes 2308
  55.9 12.4 %copy-start.2 = (f32[192]{0:T(256)S(1)}, f32[192]{0:T(256)}, u32[]{:S(2)}) copy-start(f32[192]{0:T(256)} %param.25) | copy-start | bytes 2308
  64.0 8.9 %collective-permute-start.4 = (bf16[16,112,128]{2,1,0:T(8,128)(2,1)S(1)}, bf16[16,112,128]{2,1,0:T(8,128)(2,1)S(1)}, u32[]{:S(2)}, u32[]{:S(2)}) collective-permute-start(bf16[16,112,128]{2,1,0:T(8,128)(2,1)S(1)} %all-to-all-done.1.totals), channel_id=1, source_target_pairs={{0,1},{1,0},{2,3},{3,2},{4,5},{5,4},{6,7},{7,6},{8,9},{9,8},{10,11... | collective-permute-start | bytes 1376264 | tf_op jit(solution)/shard_map/ppermute | solution.py:637

commit v2 on v1

--- a/solution.py
+++ b/solution.py
@@ -15,31 +15,19 @@
 XU, XD = 8, 7
 NT = (((1,), (1,)), ((), ()))
 KERNEL_ROWS = 1600
-INNER_MB, OUTER_MB, FIELD_MB, UPDATE_MB = 16, 16, 12, 12
-
-
-GROUPS = KERNEL_ROWS // 16
-
-
-def chunk_groups(peers):
-    return -(-(GROUPS + peers // 2) // peers)
-
-
-def headless(peers, half):
-    n = max(0, peers - (peers * chunk_groups(peers) - GROUPS))
-    return peers - n * (1 + half), peers - n * half
-
-
-def chunk_runs(peers, half):
-    size, at, runs = chunk_groups(peers), 0, []
-    lo, hi = headless(peers, half)
-    for p in range(peers):
-        first = 0 if lo <= p < hi else 1
-        count = min(size - first, GROUPS - at)
-        runs.append((first * 16, at * 16, (at + count) * 16))
-        at += count
-    assert at == GROUPS
-    return runs
+INNER_MB, OUTER_MB, FIELD_MB, UPDATE_MB = 8, 8, 12, 12
+
+
+HEAD = 8
+
+
+def chunk_span(peers):
+    return -(-KERNEL_ROWS // (8 * peers)) * 8
+
+
+def chunk_runs(peers):
+    span = chunk_span(peers)
+    return [(min(KERNEL_ROWS, p * span), min(KERNEL_ROWS, (p + 1) * span)) for p in range(peers)]
 
 
 def dot(a, b):
@@ -179,6 +167,15 @@
             d5[2 * w + rho, b * 64 : b * 64 + 64] = v
 
 
+def back_row(e, own, wb, d5, slope, e_rows, esum, outside=None):
+    v = dot(wb[...], d5[pl.ds(2 * e, 5)].reshape(KERNEL_ROWS, 256)) * slope[e]
+    if own:
+        esum[...] += v
+    else:
+        v = jnp.where(outside, 0.0, v)
+    e_rows[e] = v.astype(BF16)
+
+
 def live_lanes(lens, mask):
     slot = lax.broadcasted_iota(jnp.int32, (1, 256), 1) // 64
     lanes, count = jnp.zeros((1, 256), F32), jnp.float32(0)
@@ -226,27 +223,18 @@
 
 
 def inner_kernel(
-    R, U, x_hbm, c_hbm, we_hbm, wdt_hbm, bias, lens, mask,
-    xb, l3, slope, d5, value, seeds, dsum, acc0, acc1, we2, wd2, wb, xv, cv, we, wdt, split_ref, sems,
+    R, U, xv, cv, we_hbm, wdt_hbm, bias, lens, mask,
+    xb, l3, slope, d5, value, seeds, dsum, acc0, acc1, e_rows, esum, we2, wd2, wb, bias_enc, bias_dec, split_ref, we, wdt, sems,
 ):
     I = R // 2
-    parts = 2
-    step = R // parts
-    x_copies = [
-        pltpu.make_async_copy(x_hbm.at[:, n * step : n * step + step], xv.at[:, n * step : n * step + step], sems.at[n])
-        for n in range(parts)
-    ]
-    c_copy = pltpu.make_async_copy(c_hbm, cv, sems.at[parts])
-    w_copies = [
-        pltpu.make_async_copy(we_hbm, we, sems.at[parts + 1]),
-        pltpu.make_async_copy(wdt_hbm, wdt, sems.at[parts + 2]),
-    ]
-    for c in w_copies[:1] + x_copies + w_copies[1:] + [c_copy]:
+    copies = [pltpu.make_async_copy(a, b, sems.at[n]) for n, (a, b) in enumerate(((we_hbm, we), (wdt_hbm, wdt)))]
+    for c in copies:
         c.start()
     split_ref[...] = split_matrix()
     dsum[...] = jnp.zeros_like(dsum)
     live_lane, _ = live_lanes(lens, mask)
-    bias_enc, bias_dec = bias_tiles(bias[...])
+    bias_enc[...], bias_dec[...] = bias_tiles(bias[...])
+    esum[...] = jnp.zeros_like(esum)
 
     def columns(t, count):
         rows = [lambda s, r=t + m: xv[s, r] for m in range(count)]
@@ -261,41 +249,37 @@
 
     def encode(u, count):
         for n in range(count):
-            encode_row(u + n, I, None, we2, bias_enc, xb, l3, slope)
+            encode_row(u + n, I, None, we2, bias_enc[...], xb, l3, slope)
 
     def decode(w, count):
         for n in range(count):
-            decode_row(w + n, True, wd2, bias_dec, seeds, l3, d5, value, dsum)
-
-    w_copies[0].wait()
+            decode_row(w + n, True, wd2, bias_dec[...], seeds, l3, d5, value, dsum)
+
+    chunked(0, R, U, columns)
+    copies[0].wait()
     we2[...] = we[...].reshape(KERNEL_ROWS, 128).T.astype(BF16)
-    for n, c in enumerate(x_copies):
-        c.wait()
-        chunked(n * step, n * step + step, U, columns)
     chunked(4, I + 2, U, encode)
-    w_copies[1].wait()
+    copies[1].wait()
     up_weights(wd2, wdt, 1)
-    c_copy.wait()
     chunked(0, I, U, cotangent)
     chunked(4, I, U, decode)
+    wb[...] = jnp.concatenate([wdt[4 - q].reshape(320, 128) for q in range(5)], axis=0).T.astype(BF16)
     acc0[...], acc1[...] = kernel_grad(range(2, I - 2), d5, CH, lambda u: l3[u, 128:256], 2)
-    wb[...] = jnp.concatenate([wdt[4 - q].reshape(320, 128) for q in range(5)], axis=0).T.astype(BF16)
+    for e in range(4, I - 2):
+        back_row(e, True, wb, d5, slope, e_rows, esum)
 
 
 def outer_kernel(
-    R, U, near, far, bias, lens, mask, we2, wd2, wb,
-    xb_in, l3_in, slope_in, d5_in, value_in, seeds_in, dsum_in, acc0_in, acc1_in,
-    e_out, keep, send, xb, l3, slope, d5, value, seeds, dsum, acc0, acc1,
-    e_rows, esum, split_ref, sem,
+    R, far, near, lens, mask, we2, wd2, wb, bias_enc, bias_dec, split_ref,
+    xb_in, l3_in, slope_in, d5_in, value_in, seeds_in, dsum_in, dec0_in, dec1_in, e_rows_in, esum_in,
+    e_out, keep, send, xb, l3, slope, d5, value, seeds, dsum, dec0, dec1, e_rows, esum,
+    enc0, enc1, sem,
 ):
     I = R // 2
     core = lax.axis_index("core")
     row_at = lax.axis_index("x") * 2 + core
     ends = row_at == 0, row_at == lax.axis_size("x") * 2 - 1
-    split_ref[...] = split_matrix()
-    esum[...] = jnp.zeros_like(esum)
     live_lane, count = live_lanes(lens, mask)
-    bias_enc, bias_dec = bias_tiles(bias[...])
     upper = core == 0
 
     def above(r):
@@ -303,6 +287,9 @@
 
     def below(r):
         return lambda s: jnp.where(upper, near[s, r], far[s, r])
+
+    def encoder_grad(rows):
+        return kernel_grad(rows, xb, XU, lambda e: e_rows[e], 0)
 
     rows = [above(r) for r in range(XU)] + [below(r) for r in range(XD)]
     for n, halves in enumerate(split_rows(rows, split_ref[...])):
@@ -311,63 +298,52 @@
     for n, w in enumerate((0, 1, I + 2, I + 3)):
         store_split(seeds, w, halves[2 * n : 2 * n + 2], live_lane)
     for u in list(range(4)) + list(range(I + 2, I + 6)):
-        encode_row(u, I, ends, we2, bias_enc, xb, l3, slope)
+        encode_row(u, I, ends, we2, bias_enc[...], xb, l3, slope)
+    ready = range(4, I - 4)
+    if ready:
+        enc0[...], enc1[...] = encoder_grad(ready)
     for w in list(range(4)) + list(range(I, I + 4)):
-        decode_row(w, 2 <= w < I + 2, wd2, bias_dec, seeds, l3, d5, value, dsum)
-
-    def back(e, count, own):
-        for n in range(count):
-            v = dot(wb[...], d5[pl.ds(2 * (e + n), 5)].reshape(KERNEL_ROWS, 256)) * slope[e + n]
-            if own:
-                esum[...] += v
-            else:
-                v = jnp.where(ends[0] if e == 0 else ends[1], 0.0, v)
-            e_rows[e + n] = v.astype(BF16)
-
-    chunks, chunk_rows = keep.shape[:2]
-
-    def put(half, even_taps, odd_taps):
-        blocks = {a: (acc0, d) for d, a in enumerate(even_taps)} | {a: (acc1, d) for d, a in enumerate(odd_taps)}
-
-        def into(dest):
-            for a, (acc, d) in blocks.items():
-                block = acc[:, d * 128 : d * 128 + 128].astype(BF16)
-                for p, (first, lo, hi) in enumerate(chunk_runs(chunks, half)):
-                    lo, hi, start = max(lo, a * 320), min(hi, a * 320 + 320), lo
-                    if lo < hi:
-                        dest[p, first + lo - start : first + hi - start] = block[lo - a * 320 : hi - a * 320]
-
-        pl.when(core == half)(lambda: into(keep))
-        pl.when(core != half)(lambda: into(send))
-
+        decode_row(w, 2 <= w < I + 2, wd2, bias_dec[...], seeds, l3, d5, value, dsum)
     even, odd = kernel_grad([0, 1, I - 2, I - 1], d5, CH, lambda u: l3[u, 128:256], 2)
-    acc0[...] += even
-    acc1[...] += odd
-    put(1, (0, 2, 4), (1, 3))
-    back(0, 1, False)
-    chunked(1, I + 1, U, functools.partial(back, own=True))
-    back(I + 1, 1, False)
+    dec0[...] += even
+    dec1[...] += odd
+    for e in list(range(4)) + list(range(I - 2, I + 2)):
+        back_row(e, 1 <= e < I + 1, wb, d5, slope, e_rows, esum, ends[0] if e == 0 else ends[1])
     e_copy = pltpu.make_async_copy(e_rows, e_out, sem)
     e_copy.start()
-    acc0[...], acc1[...] = kernel_grad(range(I), xb, XU, lambda e: e_rows[e], 0)
-    put(0, (4, 2, 0), (3, 1))
+    even, odd = encoder_grad([s for s in range(I) if s not in ready])
+    if ready:
+        enc0[...] += even
+        enc1[...] += odd
+    else:
+        enc0[...], enc1[...] = even, odd
 
     count_row = jnp.broadcast_to(jnp.where(row_at == 0, count, 0.0), (1, 128))
     dec_row = jnp.concatenate([lane_sums(dsum[...]), jnp.zeros((1, 64), F32)], axis=1)
-    head = jnp.concatenate([count_row, lane_sums(esum[...]), dec_row, jnp.zeros((13, 128), F32)], axis=0).astype(BF16)
-    other_head = jnp.concatenate([count_row, jnp.zeros((15, 128), F32)], axis=0).astype(BF16)
-
-    def finish(half, dest):
-        for p, (first, lo, hi) in enumerate(chunk_runs(chunks, half)):
-            if first:
-                dest[p, :16] = other_head if p else head
-            end = first + hi - lo
-            if end < chunk_rows:
-                dest[p, end:] = jnp.zeros((chunk_rows - end, 128), BF16)
-
-    for half in range(2):
-        pl.when(core == half)(functools.partial(finish, half, keep))
-        pl.when(core != half)(functools.partial(finish, half, send))
+    head = jnp.concatenate([count_row, lane_sums(esum[...]), dec_row, jnp.zeros((HEAD - 3, 128), F32)], axis=0).astype(BF16)
+    other_head = jnp.concatenate([count_row, jnp.zeros((HEAD - 1, 128), F32)], axis=0).astype(BF16)
+    chunks, chunk_rows = keep.shape[:2]
+
+    def fill(dest, even_acc, odd_acc, even_taps, odd_taps):
+        blocks = [(a, even_acc, d) for d, a in enumerate(even_taps)] + [(a, odd_acc, d) for d, a in enumerate(odd_taps)]
+        runs = chunk_runs(chunks)
+        for a, acc, d in blocks:
+            block = acc[:, d * 128 : d * 128 + 128]
+            for p, (start, end) in enumerate(runs):
+                lo, hi = max(start, a * 320), min(end, a * 320 + 320)
+                if lo < hi:
+                    dest[p, HEAD + lo - start : HEAD + hi - start] = block[lo - a * 320 : hi - a * 320].astype(BF16)
+        for p, (start, end) in enumerate(runs):
+            dest[p, :HEAD] = other_head if p else head
+            if HEAD + end - start < chunk_rows:
+                dest[p, HEAD + end - start :] = jnp.zeros((chunk_rows - HEAD - end + start, 128), BF16)
+
+    def fill_both(enc_dest, dec_dest):
+        fill(enc_dest, enc0, enc1, (4, 2, 0), (3, 1))
+        fill(dec_dest, dec0, dec1, (0, 2, 4), (1, 3))
+
+    pl.when(core == 0)(lambda: fill_both(keep, send))
+    pl.when(core != 0)(lambda: fill_both(send, keep))
     e_copy.wait()
 
 
@@ -394,13 +370,13 @@
         c.wait()
 
 
-def input_grad_kernel(R, U, e_hbm, we_hbm, count, count_other, ig, e_rows, we, e3, we3, grads, field, merge_ref, sems):
+def input_grad_kernel(R, U, e_hbm, we_hbm, count, ig, e_rows, we, e3, we3, grads, field, merge_ref, sems):
     I = R // 2
     fetch = [pltpu.make_async_copy(we_hbm, we, sems.at[4]), pltpu.make_async_copy(e_hbm, e_rows, sems.at[5])]
     for c in fetch:
         c.start()
     merge_ref[...] = merge_matrix()
-    scale = 1.0 / jnp.maximum(count[:1], count_other[:1])
+    scale = 1.0 / count[:1]
     scale = jnp.concatenate([scale] * 2, axis=1)
     fetch[0].wait()
     up_weights(we3, we, -1)
@@ -423,17 +399,17 @@
         c.wait()
 
 
-def total_kernel(parts, count, wide, total, sems):
-    peers = parts.shape[0]
-    total[...] = sum(parts[p].astype(F32) for p in range(peers)).astype(BF16)
-    copies = [pltpu.make_async_copy(total, wide.at[p], sems.at[p]) for p in range(peers)]
+def partial_kernel(parts, partial):
+    partial[...] = sum(parts[p].astype(F32) for p in range(parts.shape[0])).astype(BF16)
+
+
+def total_kernel(own, other, count, wide, total, sems):
+    both = own[...].astype(F32) + other[...].astype(F32)
+    total[...] = both.astype(BF16)
+    copies = [pltpu.make_async_copy(total, wide.at[p], sems.at[p]) for p in range(wide.shape[0])]
     for c in copies:
         c.start()
-    me = lax.axis_index("snap") * lax.axis_size("x") + lax.axis_index("x")
-    core = lax.axis_index("core")
-    lo, hi = [jnp.where(core == 0, a, b) for a, b in zip(headless(peers, 0), headless(peers, 1), strict=True)]
-    row = jnp.where((lo <= me) & (me < hi), 0.0, total[:16].astype(F32)[:1])
-    count[...] = jnp.broadcast_to(row, (8, 128))
+    count[...] = jnp.broadcast_to(both[:1], (8, 128))
     for c in copies:
         c.wait()
 
@@ -443,15 +419,15 @@
 
 def update_rows(n, totals, scale, weights, staged, results, sems, before):
     copies, sent = [], 0
-    for p, (first, lo, hi) in enumerate(chunk_runs(totals.shape[0], n)):
+    for p, (lo, hi) in enumerate(chunk_runs(totals.shape[0])):
         if lo == hi:
             break
         before(hi)
-        grad = totals[p, first : first + hi - lo].astype(F32) * scale
+        grad = totals[p, HEAD : HEAD + hi - lo].astype(F32) * scale
         mom, ema, new = advance(grad, *[r[lo:hi] for r in weights])
         for ref, v in zip(staged, (grad, mom, ema, new, new.astype(BF16)), strict=True):
             ref[lo:hi] = v
-        if hi == KERNEL_ROWS or hi - sent >= KERNEL_ROWS // PARTS:
+        if hi == KERNEL_ROWS or (hi - sent >= KERNEL_ROWS // PARTS and hi % 16 == 0):
             for m in range(5):
                 c = pltpu.make_async_copy(staged[m].at[sent:hi], results[5 * n + m].at[sent:hi], sems.at[len(copies)])
                 c.start()
@@ -464,9 +440,9 @@
 def own_update_kernel(totals, *refs):
     sources, small, results, bias_out = refs[:6], refs[6:9], refs[9:19], refs[19:24]
     ahead, weights, staged, sems, out_sems = refs[24:27], refs[27:30], refs[30:35], refs[35], refs[36]
-    head = totals[0, 0:16].astype(F32)
+    core = lax.axis_index("core")
+    head = totals[0, :16].astype(F32)
     scale = 1.0 / head[0:1]
-    core = lax.axis_index("core")
     step = KERNEL_ROWS // PARTS
 
     def half(n):
@@ -496,14 +472,14 @@
     pl.when(core != 0)(lambda: half(1))
     grad = jnp.concatenate([head[1:2], head[2:3, :64]], axis=1) * scale[:, :1]
     mom, ema, new = advance(grad, *[r[...] for r in small])
-    for ref, v in zip(bias_out, (grad, mom, ema, new, new.astype(BF16)), strict=True):
+    for ref, v in zip(bias_out, (grad, mom, ema, new, new.astype(BF16).reshape(-1)), strict=True):
         ref[...] = v
 
 
 def other_update_kernel(totals, *refs):
     weights, results, staged, out_sems = refs[:3], refs[13:23], refs[23:28], refs[28]
-    scale = 1.0 / totals[0, 0:16].astype(F32)[0:1]
     core = lax.axis_index("core")
+    scale = 1.0 / totals[0, :16].astype(F32)[:1]
 
     def half(n):
         update_rows(n, totals, scale, weights, staged, results, out_sems, lambda hi: None)
@@ -567,35 +543,31 @@
     state = [
         sds(XU + R + 8, 320, 256), sds(I + 6, 384, 256), sds(I + 2, 128, 256, dtype=F32), sds(R + 8, 320, 256),
         sds(I, 256, 256), sds(I + 4, 256, 256), sds(64, 256, dtype=F32), sds(320, 384, dtype=F32), sds(320, 256, dtype=F32),
+        sds(I + 2, 128, 256), sds(128, 256, dtype=F32),
     ]
-    *mid, we2, wd2, wb = call(
+    shared = [
+        sds(128, KERNEL_ROWS), sds(256, 1152), sds(128, KERNEL_ROWS), sds(128, 256, dtype=F32), sds(256, 256, dtype=F32), sds(256, 256),
+    ]
+    parts = call(
         functools.partial(inner_kernel, R, U), "inner", INNER_MB, 2 * conv,
-        out_shape=state + [sds(128, KERNEL_ROWS), sds(256, 1152), sds(128, KERNEL_ROWS)],
-        in_specs=[hbm] * 4 + [vmem] + [smem] * 2,
-        out_specs=[vmem] * 12,
+        out_shape=state + shared,
+        in_specs=[vmem] * 2 + [hbm] * 2 + [vmem] + [smem] * 2,
+        out_specs=[vmem] * 17,
         scratch_shapes=[
-            pltpu.VMEM(snapshots.shape, BF16),
-            pltpu.VMEM(snapshots.shape, BF16),
             pltpu.VMEM(encoder_kernel.shape, F32),
             pltpu.VMEM(encoder_kernel.shape, F32),
-            pltpu.VMEM((256, 256), BF16),
-            pltpu.SemaphoreType.DMA((5,)),
+            pltpu.SemaphoreType.DMA((2,)),
         ],
-    )(in_hbm(snapshots), in_hbm(cotangent), in_hbm(encoder_kernel), in_hbm(decoder_t), bias_row, lengths, slot_mask)
-    chunk = sds(peers, 16 * chunk_groups(peers), 128)
+    )(in_vmem(snapshots), in_vmem(cotangent), in_hbm(encoder_kernel), in_hbm(decoder_t), bias_row, lengths, slot_mask)
+    chunk = sds(peers, HEAD + chunk_span(peers), 128)
     e_rows, keep, send, _, _, _, _, value, *_ = call(
-        functools.partial(outer_kernel, R, U), "outer", OUTER_MB, 4 * conv,
+        functools.partial(outer_kernel, R), "outer", OUTER_MB, 4 * conv,
         out_shape=[pltpu.HBM((I + 2, 128, 256), BF16), chunk, chunk] + state,
-        in_specs=[vmem] * 3 + [smem] * 2 + [vmem] * 12,
-        out_specs=[hbm] + [vmem] * 11,
-        input_output_aliases={8 + n: 3 + n for n in range(9)},
-        scratch_shapes=[
-            pltpu.VMEM((I + 2, 128, 256), BF16),
-            pltpu.VMEM((128, 256), F32),
-            pltpu.VMEM((256, 256), BF16),
-            pltpu.SemaphoreType.DMA,
-        ],
-    )(near, far, bias_row, lengths, slot_mask, we2, wd2, wb, *mid)
+        in_specs=[vmem] * 2 + [smem] * 2 + [vmem] * 17,
+        out_specs=[hbm] + [vmem] * 13,
+        input_output_aliases={10 + n: 3 + n for n in range(11)},
+        scratch_shapes=[pltpu.VMEM((320, 384), F32), pltpu.VMEM((320, 256), F32), pltpu.SemaphoreType.DMA],
+    )(far, near, lengths, slot_mask, *parts[11:], *parts[:11])
 
     recv = lax.ppermute(send, "core", swap)
     output = call(
@@ -608,19 +580,20 @@
     part = (keep.astype(F32) + recv.astype(F32)).astype(BF16)
     part, output = lax.optimization_barrier((part, output))
     parts = lax.all_to_all(part, ("snap", "x"), 0, 0, tiled=True)
+    own_side = call(partial_kernel, "partial", 4, 0, out_shape=sds(*part.shape[1:]), in_specs=[vmem], out_specs=vmem)(parts)
+    other_side = lax.ppermute(own_side, "side", swap)
     live, wide = call(
         total_kernel, "total", 4, 0,
         out_shape=[sds(8, 128, dtype=F32), pltpu.HBM(part.shape, BF16)],
-        in_specs=[vmem],
+        in_specs=[vmem] * 2,
         out_specs=[vmem, hbm],
         scratch_shapes=[pltpu.VMEM(part.shape[1:], BF16), pltpu.SemaphoreType.DMA((peers,))],
-    )(parts)
-    live_other = lax.ppermute(live, "core", swap)
+    )(own_side, other_side)
     mine = lax.all_to_all(wide, ("snap", "x"), 0, 0, tiled=True)
     input_grad = call(
         functools.partial(input_grad_kernel, R, U), "input_grad", FIELD_MB, 4 * conv,
         out_shape=field,
-        in_specs=[hbm, hbm, vmem, vmem],
+        in_specs=[hbm, hbm, vmem],
         out_specs=hbm,
         scratch_shapes=[
             pltpu.VMEM((I + 2, 128, 256), BF16),
@@ -632,7 +605,7 @@
             pltpu.VMEM((256, 256), BF16),
             pltpu.SemaphoreType.DMA((6,)),
         ],
-    )(in_hbm(e_rows), in_hbm(encoder_kernel), live, live_other)
+    )(in_hbm(e_rows), in_hbm(encoder_kernel), live)
     mine, input_grad = lax.optimization_barrier((mine, input_grad))
     other = lax.ppermute(mine, "core", swap)
 
@@ -649,7 +622,7 @@
     shape = (KERNEL_ROWS, 128)
     five = [pltpu.HBM(shape, F32)] * 4 + [pltpu.HBM(shape, BF16)]
     staged = [pltpu.VMEM(v.shape, v.dtype) for v in five]
-    bias_shape = [sds(1, latent_ch + C, dtype=F32)] * 4 + [sds(1, latent_ch + C)]
+    bias_shape = [sds(1, latent_ch + C, dtype=F32)] * 4 + [sds(latent_ch + C)]
     begun = call(
         own_update_kernel, "update_own", UPDATE_MB, 1 << 20,
         out_shape=five * 2 + bias_shape + [pltpu.VMEM(shape, F32)] * 3,
@@ -678,12 +651,13 @@
 
 def solution(mesh):
     snap, rows = mesh.devices.shape
-    split = Mesh(mesh.devices.reshape(snap, rows // 2, 2), ("snap", "x", "core"))
-    field = P("snap", ("x", "core"), None, None)
+    split = Mesh(mesh.devices.reshape(2, snap // 2, rows // 2, 2), ("side", "snap", "x", "core"))
+    slots = ("side", "snap")
+    field = P(slots, ("x", "core"), None, None)
     return jax.shard_map(
         on_device,
         mesh=split,
-        in_specs=(field, field, P("snap"), P("snap")) + (P(),) * 9,
+        in_specs=(field, field, P(slots), P(slots)) + (P(),) * 9,
         out_specs=(field, field) + (P(),) * 15,
         check_vma=False,
     )

time: 75.5 us -> 65.5 us (0.87)
  blocking collectives: 17.5 us -> 11.3 us
  Pallas kernels: 35.9 us -> 34.3 us
  waiting for transfers between devices: 3.62 us -> 2.15 us
    all_to_all x1, blocking collectives: 17.5 us -> 11.3 us  [on_device(): parts = lax.all_to_all(part, ('snap', 'x'), 0, 0, tiled=True)]
    all_to_all x1, waiting for transfers between devices: 2.67 us -> 0.57 us  [on_device(): mine = lax.all_to_all(wide, ('snap', 'x'), 0, 0, tiled=True)]
    all_to_all x1, starting transfers between devices: 5.22 us -> 3.48 us  [on_device(): mine = lax.all_to_all(wide, ('snap', 'x'), 0, 0, tiled=True)]
    pallas_call x1 -> x2, Pallas kernels: 10.1 us -> 8.46 us  [the longest x1 8.41 us: on_device(): call(functools.partial(outer_kernel, R), 'outer', OUTER_MB, 4 * conv, out...]
  transfers between devices with their start and end apart: 6 -> 6, of which waited for: 3 -> 2; matrix products, arithmetic and copies ran while one was open for 1% -> 0% of each run, Pallas kernels for 29% -> 33%
where the time goes in v2:
time: 65.5 us; the launch traced here: 65.2 us
  Pallas kernels  34.3 us (52%)
  starting transfers between devices  15.6 us (24%)
  blocking collectives  11.3 us (17%)
  waiting for transfers between devices  2.15 us (3%)
  between operations  1.67 us (3%)
    all_to_all x1, blocking collectives, on_device(): parts = lax.all_to_all(part, ('snap', 'x'), 0, 0, tiled=True)  11.3 us
    pallas_call x1, Pallas kernels, on_device(): call(functools.partial(inner_kernel, R, U), 'inner', INNER_MB, 2 * conv,...  9.77 us
    pallas_call x1, Pallas kernels, on_device(): call(functools.partial(outer_kernel, R), 'outer', OUTER_MB, 4 * conv, out...  8.41 us
    pallas_call x1, Pallas kernels, on_device(): call(functools.partial(input_grad_kernel, R, U), 'input_grad', FIELD_MB,...  5.47 us
    ppermute x1, starting transfers between devices, on_device(): lax.ppermute(far, ('x', 'core'), [pair for n in range(nx - 1) for pair in...  4.64 us
    pallas_call x1, Pallas kernels, on_device(): call(own_update_kernel, 'update_own', UPDATE_MB, 1 << 20, out_shape=five...  4.55 us
    ppermute x1, starting transfers between devices, on_device(): other = lax.ppermute(mine, 'core', swap)  4.46 us
    all_to_all x1, starting transfers between devices, on_device(): mine = lax.all_to_all(wide, ('snap', 'x'), 0, 0, tiled=True)  3.48 us
  transfers between devices with their start and end apart: 6, of which 2 were waited for; matrix products, arithmetic and copies ran while one was open for 0% of the time, Pallas kernels for 33%

profile of v2, /device:TPU:1, one launch (start us, length us, event | category | flops | bytes accessed | tf_op | source)
XLA Modules:
  0.0 65.2 jit_solution(10288378584876796900)
XLA Ops:
  0.7 0.0 copy-start.1
  0.7 0.0 copy-start
  0.7 0.0 copy-start.5
  0.7 0.0 copy-start.2
  0.7 1.5 %halo.1 = (bf16[4,12,64,128]{3,2,1,0:T(8,128)(2,1)S(1)}, bf16[4,12,64,128]{3,2,1,0:T(8,128)(2,1)S(1)}) custom-call(bf16[4,32,64,128]{3,2,1,0:T(8,128)(2,1)} %xv.1, bf16[4,32,64,128]{3,2,1,0:T(8,128)(2,1)} %cv.1), custom_call_target="tpu_custom_call" | custom-call | bytes 4194304 | tf_op jit(solution)/shard_map/halo/pallas_call | solution.py:531
  2.2 4.6 %collective-permute-start = (bf16[4,12,64,128]{3,2,1,0:T(8,128)(2,1)S(1)}, bf16[4,12,64,128]{3,2,1,0:T(8,128)(2,1)S(1)}, u32[]{:S(2)}, u32[]{:S(2)}) collective-permute-start(bf16[4,12,64,128]{3,2,1,0:T(8,128)(2,1)S(1)} %get-tuple-element.74), channel_id=1, source_target_pairs={{1,2},{2,1},{5,6},{6,5},{9,10},{10,9},{13,14},{14,13},{17,18},{18,... | collective-permute-start | bytes 2359304 | tf_op jit(solution)/shard_map/ppermute | solution.py:538
  6.9 0.1 collective-permute-start.1
  7.6 0.0 copy-done.1
  7.6 0.0 copy-done
  7.7 9.8 %inner.1 = (bf16[48,320,256]{2,1,0:T(8,128)(2,1)S(1)}, bf16[22,384,256]{2,1,0:T(8,128)(2,1)S(1)}, f32[18,128,256]{2,1,0:T(8,128)S(1)}, bf16[40,320,256]{2,1,0:T(...) custom-call(bf16[4,32,64,128]{3,2,1,0:T(8,128)(2,1)S(1)} %copy-done,, ...), custom_call_target="tpu_custom_call" | custom-call | flops 3355443200 | bytes 4194304 | tf_op jit(solution)/shard_map/inner/pallas_call | solution.py:551
  17.4 0.0 collective-permute-done.far
  17.4 0.0 collective-permute-done.1.near
  17.5 8.4 %outer.1 = (bf16[18,128,256]{2,1,0:T(8,128)(2,1)}, bf16[8,208,128]{2,1,0:T(8,128)(2,1)S(1)}, bf16[8,208,128]{2,1,0:T(8,128)(2,1)S(1)}, bf16[48,320,256]{2,1,0:T(...) custom-call(bf16[4,12,64,128]{3,2,1,0:T(8,128)(2,1)S(1)} %collective, ...), custom_call_target="tpu_custom_call", output_to_operand_aliasing={{3}: (10, {}), {4}: (11, {}), {5}: (12, {}), {6}: (13, {}),... | custom-call | flops 6710886400 | bytes 4194304 | tf_op jit(solution)/shard_map/outer/pallas_call | solution.py:563
  25.9 0.6 collective-permute-start.2
  26.5 1.7 %output.1 = bf16[4,32,64,128]{3,2,1,0:T(8,128)(2,1)} custom-call(bf16[16,256,256]{2,1,0:T(8,128)(2,1)S(1)} %get-tuple-element.95.value), custom_call_target="tpu_custom_call" | custom-call | flops 419430400 | bytes 4194304 | tf_op jit(solution)/shard_map/output/pallas_call | solution.py:573
  28.1 0.0 collective-permute-done.2
  28.1 0.1 add_convert_fusion
  28.3 11.3 %all_to_all.10.parts = bf16[8,208,128]{2,1,0:T(8,128)(2,1)S(1)} all-to-all(bf16[8,208,128]{2,1,0:T(8,128)(2,1)S(1)} %add_convert_fusion), channel_id=1, replica_groups=mesh['side'=2,'snap'=4,'x'=2,'core'=2] {'snap','x'}, dimensions={0} | all-to-all | bytes 851968 | tf_op jit(solution)/shard_map/all_to_all | solution.py:582
  39.6 0.1 partial.1.own
  39.6 2.4 %collective-permute-start.3 = (bf16[208,128]{1,0:T(8,128)(2,1)S(1)}, bf16[208,128]{1,0:T(8,128)(2,1)S(1)}, u32[]{:S(2)}, u32[]{:S(2)}) collective-permute-start(bf16[208,128]{1,0:T(8,128)(2,1)S(1)} %partial.1.own), channel_id=1, source_target_pairs={{0,16},{16,0},{1,17},{17,1},{2,18},{18,2},{3,19},{19,3},{4,20},{20... | collective-permute-start | bytes 159752 | tf_op jit(solution)/shard_map/ppermute | solution.py:584
  42.0 1.6 %collective-permute-done.3.other = bf16[208,128]{1,0:T(8,128)(2,1)S(1)} collective-permute-done((bf16[208,128]{1,0:T(8,128)(2,1)S(1)}, bf16[208,128]{1,0:T(8,128)(2,1)S(1)}, u32[]{:S(2)}, u32[]{:S(2)}) %collective-permute-start.3) | collective-permute-done | bytes 53280 | tf_op jit(solution)/shard_map/ppermute | solution.py:584
  43.6 0.8 %total.1 = (f32[8,128]{1,0:T(8,128)S(1)}, bf16[8,208,128]{2,1,0:T(8,128)(2,1)}) custom-call(bf16[208,128]{1,0:T(8,128)(2,1)S(1)} %partial.1.own, bf16[208,128]{1,0:T(8,128)(2,1)S(1)} %collective-permute-done.3.other), custom_call_target="tpu_custom_call" | custom-call | bytes 4194304 | tf_op jit(solution)/shard_map/total/pallas_call | solution.py:585
  44.4 3.5 %all-to-all-start.1 = ((bf16[8,208,128]{2,1,0:T(8,128)(2,1)}), bf16[8,208,128]{2,1,0:T(8,128)(2,1)S(1)}, u32[]{:S(2)}, u32[]{:S(2)}) async-start(bf16[8,208,128]{2,1,0:T(8,128)(2,1)} %get-tuple-element.98), calls=%async_computation.1 | async-start | bytes 851968 | tf_op jit(solution)/shard_map/all_to_all | solution.py:592
  47.9 0.0 copy-start.3
  47.9 0.0 copy-start.4
  47.9 5.5 %input_grad.1 = bf16[4,32,64,128]{3,2,1,0:T(8,128)(2,1)} custom-call(bf16[18,128,256]{2,1,0:T(8,128)(2,1)} %get-tuple-element.99.e_hbm, f32[5,5,64,128]{3,2,1,0:T(8,128)} %we_hbm.3, f32[8,128]{1,0:T(8,128)S(1)} %get-tuple-element.100.count), custom_call_target="tpu_custom_call" | custom-call | flops 6710886400 | bytes 4194304 | tf_op jit(solution)/shard_map/input_grad/pallas_call | solution.py:593
  53.4 0.6 all-to-all-done.1.totals
  54.0 4.5 %collective-permute-start.4 = (bf16[8,208,128]{2,1,0:T(8,128)(2,1)S(1)}, bf16[8,208,128]{2,1,0:T(8,128)(2,1)S(1)}, u32[]{:S(2)}, u32[]{:S(2)}) collective-permute-start(bf16[8,208,128]{2,1,0:T(8,128)(2,1)S(1)} %all-to-all-done.1.totals), channel_id=1, source_target_pairs={{0,1},{1,0},{2,3},{3,2},{4,5},{5,4},{6,7},{7,6},{8,9},{9,8},{10,11... | collective-permute-start | bytes 1277960 | tf_op jit(solution)/shard_map/ppermute | solution.py:610
  58.4 0.0 copy-done.4
  58.4 4.5 %update_own.1 = (f32[1600,128]{1,0:T(8,128)}, f32[1600,128]{1,0:T(8,128)}, f32[1600,128]{1,0:T(8,128)}, f32[1600,128]{1,0:T(8,128)}, bf16[1600,128]{1,0:T(8,128)...) custom-call(bf16[8,208,128]{2,1,0:T(8,128)(2,1)S(1)} %all-to-all-don, ...), custom_call_target="tpu_custom_call" | custom-call | flops 1048576 | bytes 4194304 | tf_op jit(solution)/shard_map/update_own/pallas_call | solution.py:626
  63.0 0.0 collective-permute-done.4.totals
  63.0 2.0 %update_other.1 = (f32[1600,128]{1,0:T(8,128)}, f32[1600,128]{1,0:T(8,128)}, f32[1600,128]{1,0:T(8,128)}, f32[1600,128]{1,0:T(8,128)}, bf16[1600,128]{1,0:T(8,12...) custom-call(bf16[8,208,128]{2,1,0:T(8,128)(2,1)S(1)} %collective-per, ...), custom_call_target="tpu_custom_call", output_to_operand_aliasing={{0}: (4, {}), {1}: (5, {}), {2}: (6, {}), {3}: (7, {}), {4}... | custom-call | flops 1048576 | bytes 4194304 | tf_op jit(solution)/shard_map/update_other/pallas_call | solution.py:636
  (3 shorter events, 0.0 us)
Async XLA Ops:
  0.7 7.0 %copy-start.1 = (bf16[4,32,64,128]{3,2,1,0:T(8,128)(2,1)S(1)}, bf16[4,32,64,128]{3,2,1,0:T(8,128)(2,1)}, u32[]{:S(2)}) copy-start(bf16[4,32,64,128]{3,2,1,0:T(8,128)(2,1)} %cv.1) | copy-start | bytes 6291460
  0.7 7.0 %copy-start = (bf16[4,32,64,128]{3,2,1,0:T(8,128)(2,1)S(1)}, bf16[4,32,64,128]{3,2,1,0:T(8,128)(2,1)}, u32[]{:S(2)}) copy-start(bf16[4,32,64,128]{3,2,1,0:T(8,128)(2,1)} %xv.1) | copy-start | bytes 6291460
  0.7 7.0 %copy-start.5 = (s32[4]{0:T(128)S(1)}, s32[4]{0:T(128)}, u32[]{:S(2)}) copy-start(s32[4]{0:T(128)} %mask.3) | copy-start | bytes 52
  0.7 7.0 %copy-start.2 = (f32[192]{0:T(256)S(1)}, f32[192]{0:T(256)}, u32[]{:S(2)}) copy-start(f32[192]{0:T(256)} %param.19) | copy-start | bytes 2308
  2.2 15.2 %collective-permute-start = (bf16[4,12,64,128]{3,2,1,0:T(8,128)(2,1)S(1)}, bf16[4,12,64,128]{3,2,1,0:T(8,128)(2,1)S(1)}, u32[]{:S(2)}, u32[]{:S(2)}) collective-permute-start(bf16[4,12,64,128]{3,2,1,0:T(8,128)(2,1)S(1)} %get-tuple-element.74), channel_id=1, source_target_pairs={{1,2},{2,1},{5,6},{6,5},{9,10},{10,9},{13,14},{14,13},{17,18},{18,... | collective-permute-start | bytes 2359304 | tf_op jit(solution)/shard_map/ppermute | solution.py:538
  6.9 10.6 %collective-permute-start.1 = (bf16[4,12,64,128]{3,2,1,0:T(8,128)(2,1)S(1)}, bf16[4,12,64,128]{3,2,1,0:T(8,128)(2,1)S(1)}, u32[]{:S(2)}, u32[]{:S(2)}) collective-permute-start(bf16[4,12,64,128]{3,2,1,0:T(8,128)(2,1)S(1)} %get-tuple-element.75), channel_id=1, source_target_pairs={{0,1},{1,0},{2,3},{3,2},{4,5},{5,4},{6,7},{7,6},{8,9},{9,8},{10,11... | collective-permute-start | bytes 2359304 | tf_op jit(solution)/shard_map/ppermute | solution.py:539
  25.9 2.3 %collective-permute-start.2 = (bf16[8,208,128]{2,1,0:T(8,128)(2,1)S(1)}, bf16[8,208,128]{2,1,0:T(8,128)(2,1)S(1)}, u32[]{:S(2)}, u32[]{:S(2)}) collective-permute-start(bf16[8,208,128]{2,1,0:T(8,128)(2,1)S(1)} %get-tuple-element.94), channel_id=1, source_target_pairs={{0,1},{1,0},{2,3},{3,2},{4,5},{5,4},{6,7},{7,6},{8,9},{9,8},{10,11... | collective-permute-start | bytes 1277960 | tf_op jit(solution)/shard_map/ppermute | solution.py:572
  39.6 3.9 %collective-permute-start.3 = (bf16[208,128]{1,0:T(8,128)(2,1)S(1)}, bf16[208,128]{1,0:T(8,128)(2,1)S(1)}, u32[]{:S(2)}, u32[]{:S(2)}) collective-permute-start(bf16[208,128]{1,0:T(8,128)(2,1)S(1)} %partial.1.own), channel_id=1, source_target_pairs={{0,16},{16,0},{1,17},{17,1},{2,18},{18,2},{3,19},{19,3},{4,20},{20... | collective-permute-start | bytes 159752 | tf_op jit(solution)/shard_map/ppermute | solution.py:584
  44.4 9.6 %all-to-all-start.1 = ((bf16[8,208,128]{2,1,0:T(8,128)(2,1)}), bf16[8,208,128]{2,1,0:T(8,128)(2,1)S(1)}, u32[]{:S(2)}, u32[]{:S(2)}) async-start(bf16[8,208,128]{2,1,0:T(8,128)(2,1)} %get-tuple-element.98), calls=%async_computation.1 | async-start | bytes 851968 | tf_op jit(solution)/shard_map/all_to_all | solution.py:592
  47.9 10.5 %copy-start.3 = (f32[192]{0:T(256)S(1)}, f32[192]{0:T(256)}, u32[]{:S(2)}) copy-start(f32[192]{0:T(256)} %param.22) | copy-start | bytes 2308
  47.9 10.5 %copy-start.4 = (f32[192]{0:T(256)S(1)}, f32[192]{0:T(256)}, u32[]{:S(2)}) copy-start(f32[192]{0:T(256)} %param.25) | copy-start | bytes 2308
  54.0 9.0 %collective-permute-start.4 = (bf16[8,208,128]{2,1,0:T(8,128)(2,1)S(1)}, bf16[8,208,128]{2,1,0:T(8,128)(2,1)S(1)}, u32[]{:S(2)}, u32[]{:S(2)}) collective-permute-start(bf16[8,208,128]{2,1,0:T(8,128)(2,1)S(1)} %all-to-all-done.1.totals), channel_id=1, source_target_pairs={{0,1},{1,0},{2,3},{3,2},{4,5},{5,4},{6,7},{7,6},{8,9},{9,8},{10,11... | collective-permute-start | bytes 1277960 | tf_op jit(solution)/shard_map/ppermute | solution.py:610

commit v3 on v2

--- a/solution.py
+++ b/solution.py
@@ -15,7 +15,7 @@
 XU, XD = 8, 7
 NT = (((1,), (1,)), ((), ()))
 KERNEL_ROWS = 1600
-INNER_MB, OUTER_MB, FIELD_MB, UPDATE_MB = 8, 8, 12, 12
+INNER_MB, OUTER_MB, FIELD_MB, UPDATE_MB = 8, 8, 12, 16
 
 
 HEAD = 8
@@ -198,6 +198,19 @@
     return jnp.broadcast_to(enc, (128, 256)), jnp.broadcast_to(jnp.concatenate([dec] * 4, axis=0), (256, 256))
 
 
+def far_pairs(groups, nx):
+    pairs = []
+    for g in range(groups):
+        base = g * 2 * nx
+        for n in range(nx - 1):
+            a, b = base + 2 * n + 1, base + 2 * n + 2
+            pairs += [(a, b), (b, a)]
+        other = g ^ 1
+        if other < groups:
+            pairs += [(base, other * 2 * nx), (base + 2 * nx - 1, (other + 1) * 2 * nx - 1)]
+    return pairs
+
+
 def halo_kernel(R, x_hbm, c_hbm, near, far, sems):
     core = lax.axis_index("core")
     copies = []
@@ -272,8 +285,7 @@
 def outer_kernel(
     R, far, near, lens, mask, we2, wd2, wb, bias_enc, bias_dec, split_ref,
     xb_in, l3_in, slope_in, d5_in, value_in, seeds_in, dsum_in, dec0_in, dec1_in, e_rows_in, esum_in,
-    e_out, keep, send, xb, l3, slope, d5, value, seeds, dsum, dec0, dec1, e_rows, esum,
-    enc0, enc1, sem,
+    keep, send, xb, l3, slope, d5, value, seeds, dsum, dec0, dec1, e_rows, esum, enc0, enc1,
 ):
     I = R // 2
     core = lax.axis_index("core")
@@ -283,10 +295,10 @@
     upper = core == 0
 
     def above(r):
-        return lambda s: jnp.where(upper, far[s, r], near[s, r])
+        return lambda s: jnp.where(ends[0], jnp.zeros((64, 128), BF16), jnp.where(upper, far[s, r], near[s, r]))
 
     def below(r):
-        return lambda s: jnp.where(upper, near[s, r], far[s, r])
+        return lambda s: jnp.where(ends[1], jnp.zeros((64, 128), BF16), jnp.where(upper, near[s, r], far[s, r]))
 
     def encoder_grad(rows):
         return kernel_grad(rows, xb, XU, lambda e: e_rows[e], 0)
@@ -309,8 +321,6 @@
     dec1[...] += odd
     for e in list(range(4)) + list(range(I - 2, I + 2)):
         back_row(e, 1 <= e < I + 1, wb, d5, slope, e_rows, esum, ends[0] if e == 0 else ends[1])
-    e_copy = pltpu.make_async_copy(e_rows, e_out, sem)
-    e_copy.start()
     even, odd = encoder_grad([s for s in range(I) if s not in ready])
     if ready:
         enc0[...] += even
@@ -344,7 +354,6 @@
 
     pl.when(core == 0)(lambda: fill_both(keep, send))
     pl.when(core != 0)(lambda: fill_both(send, keep))
-    e_copy.wait()
 
 
 def field_copies(R, field, out, sems):
@@ -357,7 +366,7 @@
     copies = field_copies(R, field, out, sems)
     for n, c in enumerate(copies):
         for s in range(n * I // 4, (n + 1) * I // 4):
-            for rho, slots in enumerate(merge_rows(value[s], merge)):
+            for rho, slots in enumerate(merge_rows(value(s), merge)):
                 for k, piece in enumerate(slots):
                     field[k, 2 * s + rho] = piece
         c.start()
@@ -366,21 +375,17 @@
 
 def output_kernel(R, value, out, field, merge_ref, sems):
     merge_ref[...] = merge_matrix()
-    for c in merge_field(R, value, merge_ref[...], field, out, sems):
+    for c in merge_field(R, lambda s: value[s], merge_ref[...], field, out, sems):
         c.wait()
 
 
-def input_grad_kernel(R, U, e_hbm, we_hbm, count, ig, e_rows, we, e3, we3, grads, field, merge_ref, sems):
+def scatter_kernel(R, U, e_rows, we_hbm, *refs):
+    sources, grads, targets, (we, e3, we3, sems) = refs[:6], refs[6], refs[7:13], refs[13:]
     I = R // 2
-    fetch = [pltpu.make_async_copy(we_hbm, we, sems.at[4]), pltpu.make_async_copy(e_hbm, e_rows, sems.at[5])]
+    fetch = [pltpu.make_async_copy(we_hbm, we, sems.at[6])]
+    fetch += [pltpu.make_async_copy(a, b, sems.at[n]) for n, (a, b) in enumerate(zip(sources, targets, strict=True))]
     for c in fetch:
         c.start()
-    merge_ref[...] = merge_matrix()
-    scale = 1.0 / count[:1]
-    scale = jnp.concatenate([scale] * 2, axis=1)
-    fetch[0].wait()
-    up_weights(we3, we, -1)
-    fetch[1].wait()
 
     def widen(e, count):
         for n in range(count):
@@ -391,11 +396,13 @@
 
     def scatter(s, count):
         for n in range(count):
-            grads[s + n] = (up(we3, e3, s + n) * scale).astype(BF16)
+            grads[s + n] = up(we3, e3, s + n)
 
     chunked(0, I + 2, I + 2, widen)
+    fetch[0].wait()
+    up_weights(we3, we, -1)
     chunked(0, I, U, scatter)
-    for c in merge_field(R, grads, merge_ref[...], field, ig, sems):
+    for c in fetch[1:]:
         c.wait()
 
 
@@ -403,89 +410,59 @@
     partial[...] = sum(parts[p].astype(F32) for p in range(parts.shape[0])).astype(BF16)
 
 
-def total_kernel(own, other, count, wide, total, sems):
+def total_kernel(own, other, wide):
     both = own[...].astype(F32) + other[...].astype(F32)
-    total[...] = both.astype(BF16)
-    copies = [pltpu.make_async_copy(total, wide.at[p], sems.at[p]) for p in range(wide.shape[0])]
-    for c in copies:
-        c.start()
-    count[...] = jnp.broadcast_to(both[:1], (8, 128))
-    for c in copies:
-        c.wait()
+    for p in range(wide.shape[0]):
+        wide[p] = both.astype(BF16)
 
 
 PARTS = 4
 
 
-def update_rows(n, totals, scale, weights, staged, results, sems, before):
-    copies, sent = [], 0
-    for p, (lo, hi) in enumerate(chunk_runs(totals.shape[0])):
-        if lo == hi:
-            break
-        before(hi)
-        grad = totals[p, HEAD : HEAD + hi - lo].astype(F32) * scale
-        mom, ema, new = advance(grad, *[r[lo:hi] for r in weights])
-        for ref, v in zip(staged, (grad, mom, ema, new, new.astype(BF16)), strict=True):
-            ref[lo:hi] = v
-        if hi == KERNEL_ROWS or (hi - sent >= KERNEL_ROWS // PARTS and hi % 16 == 0):
-            for m in range(5):
-                c = pltpu.make_async_copy(staged[m].at[sent:hi], results[5 * n + m].at[sent:hi], sems.at[len(copies)])
-                c.start()
-                copies.append(c)
-            sent = hi
-    for c in copies:
-        c.wait()
-
-
-def own_update_kernel(totals, *refs):
-    sources, small, results, bias_out = refs[:6], refs[6:9], refs[9:19], refs[19:24]
-    ahead, weights, staged, sems, out_sems = refs[24:27], refs[27:30], refs[30:35], refs[35], refs[36]
+def update_kernel(owner, totals, *refs):
+    params, results, staged, sems = refs[:6], refs[-16:-6], refs[-6:-1], refs[-1]
+    head = totals[0, :16].astype(F32)
+    scale = 1.0 / head[:1]
+
+    def half(n):
+        copies, sent = [], 0
+        for p, (lo, hi) in enumerate(chunk_runs(totals.shape[0])):
+            if lo == hi:
+                break
+            grad = totals[p, HEAD : HEAD + hi - lo].astype(F32) * scale
+            mom, ema, new = advance(grad, *[r[lo:hi] for r in params[3 * n : 3 * n + 3]])
+            for ref, v in zip(staged, (grad, mom, ema, new, new.astype(BF16)), strict=True):
+                ref[lo:hi] = v
+            if hi == KERNEL_ROWS or (hi - sent >= KERNEL_ROWS // PARTS and hi % 16 == 0):
+                for m in range(5):
+                    c = pltpu.make_async_copy(staged[m].at[sent:hi], results[5 * n + m].at[sent:hi], sems.at[len(copies)])
+                    c.start()
+                    copies.append(c)
+                sent = hi
+        for c in copies:
+            c.wait()
+
     core = lax.axis_index("core")
+    pl.when(core == owner)(lambda: half(0))
+    pl.when(core != owner)(lambda: half(1))
+
+
+def own_update_kernel(R, totals, *refs):
+    params, small, grads, bias_out, ig, rest, (field, merge_ref, sems) = (
+        refs[:6], refs[6:9], refs[9], refs[10:15], refs[15], refs[16:-3], refs[-3:],
+    )
     head = totals[0, :16].astype(F32)
-    scale = 1.0 / head[0:1]
-    step = KERNEL_ROWS // PARTS
-
-    def half(n):
-        own = [
-            [
-                pltpu.make_async_copy(sources[3 * n + m].at[p * step : p * step + step], weights[m].at[p * step : p * step + step], sems.at[3 * p + m])
-                for m in range(3)
-            ]
-            for p in range(PARTS)
-        ]
-        later = [pltpu.make_async_copy(sources[3 * (1 - n) + m], ahead[m], sems.at[3 * PARTS + m]) for m in range(3)]
-        for c in sum(own, []) + later:
-            c.start()
-        waited = [0]
-
-        def before(hi):
-            while waited[0] * step < hi:
-                for c in own[waited[0]]:
-                    c.wait()
-                waited[0] += 1
-
-        update_rows(n, totals, scale, weights, staged, results, out_sems, before)
-        for c in later:
-            c.wait()
-
-    pl.when(core == 0)(lambda: half(0))
-    pl.when(core != 0)(lambda: half(1))
+    scale = 1.0 / head[:1]
+    wide_scale = jnp.concatenate([scale] * 2, axis=1)
+    merge_ref[...] = merge_matrix()
+    copies = merge_field(R, lambda s: (grads[s] * wide_scale).astype(BF16), merge_ref[...], field, ig, sems)
     grad = jnp.concatenate([head[1:2], head[2:3, :64]], axis=1) * scale[:, :1]
     mom, ema, new = advance(grad, *[r[...] for r in small])
     for ref, v in zip(bias_out, (grad, mom, ema, new, new.astype(BF16).reshape(-1)), strict=True):
         ref[...] = v
-
-
-def other_update_kernel(totals, *refs):
-    weights, results, staged, out_sems = refs[:3], refs[13:23], refs[23:28], refs[28]
-    core = lax.axis_index("core")
-    scale = 1.0 / totals[0, :16].astype(F32)[:1]
-
-    def half(n):
-        update_rows(n, totals, scale, weights, staged, results, out_sems, lambda hi: None)
-
-    pl.when(core == 0)(lambda: half(1))
-    pl.when(core != 0)(lambda: half(0))
+    update_kernel(0, totals, *params, *rest)
+    for c in copies:
+        c.wait()
 
 
 def advance(grad, weight, moment, average):
@@ -535,7 +512,7 @@
         out_specs=[vmem] * 2,
         scratch_shapes=[pltpu.SemaphoreType.DMA((4,))],
     )(in_hbm(snapshots), in_hbm(cotangent))
-    far = lax.ppermute(far, ("x", "core"), [pair for n in range(nx - 1) for pair in ((2 * n + 1, 2 * n + 2), (2 * n + 2, 2 * n + 1))])
+    far = lax.ppermute(far, ("snap", "x", "core"), far_pairs(lax.axis_size("snap"), nx))
     near = lax.ppermute(near, "core", swap)
     bias_row = biases.reshape(1, -1)
 
@@ -560,13 +537,13 @@
         ],
     )(in_vmem(snapshots), in_vmem(cotangent), in_hbm(encoder_kernel), in_hbm(decoder_t), bias_row, lengths, slot_mask)
     chunk = sds(peers, HEAD + chunk_span(peers), 128)
-    e_rows, keep, send, _, _, _, _, value, *_ = call(
+    keep, send, _, _, _, _, value, _, _, _, _, e_rows, _ = call(
         functools.partial(outer_kernel, R), "outer", OUTER_MB, 4 * conv,
-        out_shape=[pltpu.HBM((I + 2, 128, 256), BF16), chunk, chunk] + state,
+        out_shape=[chunk, chunk] + state,
         in_specs=[vmem] * 2 + [smem] * 2 + [vmem] * 17,
-        out_specs=[hbm] + [vmem] * 13,
-        input_output_aliases={10 + n: 3 + n for n in range(11)},
-        scratch_shapes=[pltpu.VMEM((320, 384), F32), pltpu.VMEM((320, 256), F32), pltpu.SemaphoreType.DMA],
+        out_specs=[vmem] * 13,
+        input_output_aliases={10 + n: 2 + n for n in range(11)},
+        scratch_shapes=[pltpu.VMEM((320, 384), F32), pltpu.VMEM((320, 256), F32)],
     )(far, near, lengths, slot_mask, *parts[11:], *parts[:11])
 
     recv = lax.ppermute(send, "core", swap)
@@ -580,34 +557,9 @@
     part = (keep.astype(F32) + recv.astype(F32)).astype(BF16)
     part, output = lax.optimization_barrier((part, output))
     parts = lax.all_to_all(part, ("snap", "x"), 0, 0, tiled=True)
+    parts, e_rows = lax.optimization_barrier((parts, e_rows))
     own_side = call(partial_kernel, "partial", 4, 0, out_shape=sds(*part.shape[1:]), in_specs=[vmem], out_specs=vmem)(parts)
     other_side = lax.ppermute(own_side, "side", swap)
-    live, wide = call(
-        total_kernel, "total", 4, 0,
-        out_shape=[sds(8, 128, dtype=F32), pltpu.HBM(part.shape, BF16)],
-        in_specs=[vmem] * 2,
-        out_specs=[vmem, hbm],
-        scratch_shapes=[pltpu.VMEM(part.shape[1:], BF16), pltpu.SemaphoreType.DMA((peers,))],
-    )(own_side, other_side)
-    mine = lax.all_to_all(wide, ("snap", "x"), 0, 0, tiled=True)
-    input_grad = call(
-        functools.partial(input_grad_kernel, R, U), "input_grad", FIELD_MB, 4 * conv,
-        out_shape=field,
-        in_specs=[hbm, hbm, vmem],
-        out_specs=hbm,
-        scratch_shapes=[
-            pltpu.VMEM((I + 2, 128, 256), BF16),
-            pltpu.VMEM(encoder_kernel.shape, F32),
-            pltpu.VMEM((I + 2, 384, 256), BF16),
-            pltpu.VMEM((256, 1152), BF16),
-            pltpu.VMEM((I, 256, 256), BF16),
-            pltpu.VMEM(snapshots.shape, BF16),
-            pltpu.VMEM((256, 256), BF16),
-            pltpu.SemaphoreType.DMA((6,)),
-        ],
-    )(in_hbm(e_rows), in_hbm(encoder_kernel), live)
-    mine, input_grad = lax.optimization_barrier((mine, input_grad))
-    other = lax.ppermute(mine, "core", swap)
 
     def rows(v):
         return v.reshape(KERNEL_ROWS, 128)
@@ -620,27 +572,43 @@
         trows(decoder_kernel), trows(decoder_mom), trows(decoder_ema),
     ]
     shape = (KERNEL_ROWS, 128)
+    grads, *params = call(
+        functools.partial(scatter_kernel, R, U), "scatter", FIELD_MB, conv,
+        out_shape=[sds(I, 256, 256, dtype=F32)] + [sds(*shape, dtype=F32)] * 6,
+        in_specs=[vmem] + [hbm] * 7,
+        out_specs=[vmem] * 7,
+        scratch_shapes=[
+            pltpu.VMEM(encoder_kernel.shape, F32),
+            pltpu.VMEM((I + 2, 384, 256), BF16),
+            pltpu.VMEM((256, 1152), BF16),
+            pltpu.SemaphoreType.DMA((7,)),
+        ],
+    )(e_rows, in_hbm(encoder_kernel), *[in_hbm(v) for v in params])
+    other_side, grads, params = lax.optimization_barrier((other_side, grads, params))
+    wide = call(total_kernel, "total", 4, 0, out_shape=sds(*part.shape), in_specs=[vmem] * 2, out_specs=vmem)(own_side, other_side)
+    mine = lax.all_to_all(wide, ("snap", "x"), 0, 0, tiled=True)
+    mine, grads, params = lax.optimization_barrier((mine, grads, params))
+    other = lax.ppermute(mine, "core", swap)
     five = [pltpu.HBM(shape, F32)] * 4 + [pltpu.HBM(shape, BF16)]
-    staged = [pltpu.VMEM(v.shape, v.dtype) for v in five]
+    staged = [pltpu.VMEM(v.shape, v.dtype) for v in five] + [pltpu.SemaphoreType.DMA((5 * PARTS,))]
     bias_shape = [sds(1, latent_ch + C, dtype=F32)] * 4 + [sds(latent_ch + C)]
-    begun = call(
-        own_update_kernel, "update_own", UPDATE_MB, 1 << 20,
-        out_shape=five * 2 + bias_shape + [pltpu.VMEM(shape, F32)] * 3,
-        in_specs=[vmem] + [hbm] * 6 + [vmem] * 3,
-        out_specs=[hbm] * 10 + [vmem] * 8,
-        scratch_shapes=[pltpu.VMEM(shape, F32)] * 3
-        + staged
-        + [pltpu.SemaphoreType.DMA((3 * PARTS + 3,)), pltpu.SemaphoreType.DMA((5 * PARTS,))],
-    )(mine, *[in_hbm(v) for v in params], bias_row, bias_mom.reshape(1, -1), bias_ema.reshape(1, -1))
-    bias_grad, bia_mom, bia_ema, bia_new, bia_copy = [v.reshape(biases.shape) for v in begun[10:15]]
+    own = call(
+        functools.partial(own_update_kernel, R), "update_own", UPDATE_MB, 1 << 20,
+        out_shape=bias_shape + [field] + five * 2,
+        in_specs=[vmem] * 11,
+        out_specs=[vmem] * 5 + [hbm] * 11,
+        scratch_shapes=staged + [pltpu.VMEM(snapshots.shape, BF16), pltpu.VMEM((256, 256), BF16), pltpu.SemaphoreType.DMA((4,))],
+    )(mine, *params, bias_row, bias_mom.reshape(1, -1), bias_ema.reshape(1, -1), grads)
+    bias_results, input_grad, begun = own[:5], own[5], own[6:]
+    bias_grad, bia_mom, bia_ema, bia_new, bia_copy = [v.reshape(biases.shape) for v in bias_results]
     results = call(
-        other_update_kernel, "update_other", UPDATE_MB, 1 << 20,
+        functools.partial(update_kernel, 1), "update_other", UPDATE_MB, 1 << 20,
         out_shape=five * 2,
-        in_specs=[vmem] * 4 + [hbm] * 10,
+        in_specs=[vmem] * 7 + [hbm] * 10,
         out_specs=[hbm] * 10,
-        input_output_aliases={4 + n: n for n in range(10)},
-        scratch_shapes=staged + [pltpu.SemaphoreType.DMA((5 * PARTS,))],
-    )(other, *[in_vmem(v) for v in begun[15:]], *[in_hbm(v) for v in begun[:10]])
+        input_output_aliases={7 + n: n for n in range(10)},
+        scratch_shapes=staged,
+    )(other, *params, *[in_hbm(v) for v in begun])
     enc_grad, enc_mom, enc_ema, enc_new, enc_copy = [v.reshape(encoder_kernel.shape) for v in results[:5]]
     dec_grad, dec_mom, dec_ema, dec_new, dec_copy = [jnp.swapaxes(v.reshape(decoder_t.shape), 2, 3) for v in results[5:]]
     return (

time: 65.5 us -> 62.3 us (0.951)
  blocking collectives: 11.3 us -> 20.7 us
  starting transfers between devices: 15.6 us -> 8.24 us
  Pallas kernels: 34.3 us -> 31.3 us
  waiting for transfers between devices: 2.15 us -> 0.04 us
    all_to_all x0 -> x1, blocking collectives: none -> 9.5 us  [on_device(): mine = lax.all_to_all(wide, ('snap', 'x'), 0, 0, tiled=True)]
    all_to_all x1 -> x0, starting transfers between devices: 3.48 us -> none  [on_device(): mine = lax.all_to_all(wide, ('snap', 'x'), 0, 0, tiled=True)]
    pallas_call x4, Pallas kernels: 12.9 us -> 9.85 us  [the longest x1 4.17 us: on_device(): call(functools.partial(scatter_kernel, R, U), 'scatter', FIELD_MB, conv,...]
    ppermute x1, starting transfers between devices: 4.64 us -> 2.67 us  [on_device(): lax.ppermute(far, ('snap', 'x', 'core'), far_pairs(lax.axis_size('snap'),...]
    ppermute x1, starting transfers between devices: 4.46 us -> 2.64 us  [on_device(): other = lax.ppermute(mine, 'core', swap)]
    ppermute x1, waiting for transfers between devices: 1.57 us -> 0.01 us  [on_device(): other_side = lax.ppermute(own_side, 'side', swap)]
  transfers between devices with their start and end apart: 6 -> 5, of which waited for: 2 -> 0; matrix products, arithmetic and copies ran while one was open for 0% -> 0% of each run, Pallas kernels for 33% -> 32%
where the time goes in v3:
time: 62.3 us; the launch traced here: 62 us
  Pallas kernels  31.3 us (50%)
  blocking collectives  20.7 us (33%)
  starting transfers between devices  8.24 us (13%)
  between operations  1.63 us (3%)
    all_to_all x1, blocking collectives, on_device(): parts = lax.all_to_all(part, ('snap', 'x'), 0, 0, tiled=True)  11.2 us
    pallas_call x1, Pallas kernels, on_device(): call(functools.partial(inner_kernel, R, U), 'inner', INNER_MB, 2 * conv,...  10.1 us
    all_to_all x1, blocking collectives, on_device(): mine = lax.all_to_all(wide, ('snap', 'x'), 0, 0, tiled=True)  9.5 us
    pallas_call x1, Pallas kernels, on_device(): call(functools.partial(outer_kernel, R), 'outer', OUTER_MB, 4 * conv, out...  8.08 us
    pallas_call x1, Pallas kernels, on_device(): call(functools.partial(scatter_kernel, R, U), 'scatter', FIELD_MB, conv,...  4.17 us
    pallas_call x1, Pallas kernels, on_device(): call(functools.partial(own_update_kernel, R), 'update_own', UPDATE_MB, 1...  3.61 us
    ppermute x1, starting transfers between devices, on_device(): lax.ppermute(far, ('snap', 'x', 'core'), far_pairs(lax.axis_size('snap'),...  2.67 us
    ppermute x1, starting transfers between devices, on_device(): other = lax.ppermute(mine, 'core', swap)  2.64 us
  transfers between devices with their start and end apart: 5, of which 0 were waited for; matrix products, arithmetic and copies ran while one was open for 0% of the time, Pallas kernels for 32%

profile of v3, /device:TPU:1, one launch (start us, length us, event | category | flops | bytes accessed | tf_op | source)
XLA Modules:
  0.0 62.0 jit_solution(14197133836686309613)
XLA Ops:
  0.7 0.0 copy-start.1
  0.7 0.0 copy-start
  0.7 0.0 copy-start.5
  0.7 0.0 copy-start.2
  0.7 1.5 %halo.1 = (bf16[4,12,64,128]{3,2,1,0:T(8,128)(2,1)S(1)}, bf16[4,12,64,128]{3,2,1,0:T(8,128)(2,1)S(1)}) custom-call(bf16[4,32,64,128]{3,2,1,0:T(8,128)(2,1)} %xv.1, bf16[4,32,64,128]{3,2,1,0:T(8,128)(2,1)} %cv.1), custom_call_target="tpu_custom_call" | custom-call | bytes 4194304 | tf_op jit(solution)/shard_map/halo/pallas_call | solution.py:508
  2.2 2.7 %collective-permute-start = (bf16[4,12,64,128]{3,2,1,0:T(8,128)(2,1)S(1)}, bf16[4,12,64,128]{3,2,1,0:T(8,128)(2,1)S(1)}, u32[]{:S(2)}, u32[]{:S(2)}) collective-permute-start(bf16[4,12,64,128]{3,2,1,0:T(8,128)(2,1)S(1)} %get-tuple-element.93), channel_id=1, source_target_pairs={{1,2},{2,1},{0,4},{3,7},{5,6},{6,5},{4,0},{7,3},{9,10},{10,9},{8,1... | collective-permute-start | bytes 2359304 | tf_op jit(solution)/shard_map/ppermute | solution.py:515
  4.9 0.4 collective-permute-start.1
  6.0 0.0 copy-done.1
  6.0 0.0 copy-done
  6.0 0.0 copy-done.5
  6.0 0.0 copy-done.2
  6.0 10.1 %inner.1 = (bf16[48,320,256]{2,1,0:T(8,128)(2,1)S(1)}, bf16[22,384,256]{2,1,0:T(8,128)(2,1)S(1)}, f32[18,128,256]{2,1,0:T(8,128)S(1)}, bf16[40,320,256]{2,1,0:T(...) custom-call(bf16[4,32,64,128]{3,2,1,0:T(8,128)(2,1)S(1)} %copy-done,, ...), custom_call_target="tpu_custom_call" | custom-call | flops 3355443200 | bytes 4194304 | tf_op jit(solution)/shard_map/inner/pallas_call | solution.py:528
  16.1 0.0 collective-permute-done.far
  16.1 0.0 collective-permute-done.1.near
  16.2 8.1 %outer.1 = (bf16[8,208,128]{2,1,0:T(8,128)(2,1)S(1)}, bf16[8,208,128]{2,1,0:T(8,128)(2,1)S(1)}, bf16[48,320,256]{2,1,0:T(8,128)(2,1)S(1)}, bf16[22,384,256]{2,1,...) custom-call(bf16[4,12,64,128]{3,2,1,0:T(8,128)(2,1)S(1)} %collective, ...), custom_call_target="tpu_custom_call", output_to_operand_aliasing={{2}: (10, {}), {3}: (11, {}), {4}: (12, {}), {5}: (13, {}),... | custom-call | flops 6710886400 | bytes 4194304 | tf_op jit(solution)/shard_map/outer/pallas_call | solution.py:540
  24.2 0.1 collective-permute-start.2
  24.4 1.7 %output.1 = bf16[4,32,64,128]{3,2,1,0:T(8,128)(2,1)} custom-call(bf16[16,256,256]{2,1,0:T(8,128)(2,1)S(1)} %get-tuple-element.114.value), custom_call_target="tpu_custom_call" | custom-call | flops 419430400 | bytes 4194304 | tf_op jit(solution)/shard_map/output/pallas_call | solution.py:550
  26.1 0.0 collective-permute-done.2
  26.1 0.1 add_convert_fusion
  26.2 11.2 %all_to_all.10.parts = bf16[8,208,128]{2,1,0:T(8,128)(2,1)S(1)} all-to-all(bf16[8,208,128]{2,1,0:T(8,128)(2,1)S(1)} %add_convert_fusion), channel_id=1, replica_groups=mesh['side'=2,'snap'=4,'x'=2,'core'=2] {'snap','x'}, dimensions={0} | all-to-all | bytes 851968 | tf_op jit(solution)/shard_map/all_to_all | solution.py:559
  37.4 0.1 partial.1.own
  37.4 2.4 %collective-permute-start.3 = (bf16[208,128]{1,0:T(8,128)(2,1)S(1)}, bf16[208,128]{1,0:T(8,128)(2,1)S(1)}, u32[]{:S(2)}, u32[]{:S(2)}) collective-permute-start(bf16[208,128]{1,0:T(8,128)(2,1)S(1)} %partial.1.own), channel_id=1, source_target_pairs={{0,16},{16,0},{1,17},{17,1},{2,18},{18,2},{3,19},{19,3},{4,20},{20... | collective-permute-start | bytes 159752 | tf_op jit(solution)/shard_map/ppermute | solution.py:562
  39.8 0.0 copy-start.3
  39.8 4.2 %scatter.1 = (f32[16,256,256]{2,1,0:T(8,128)S(1)}, f32[1600,128]{1,0:T(8,128)S(1)}, f32[1600,128]{1,0:T(8,128)S(1)}, f32[1600,128]{1,0:T(8,128)S(1)}, f32[1600,1...) custom-call(bf16[18,128,256]{2,1,0:T(8,128)(2,1)S(1)} %get-tuple-element.119.e_rows, ...), custom_call_target="tpu_custom_call" | custom-call | flops 1677721600 | bytes 4194304 | tf_op jit(solution)/shard_map/scatter/pallas_call | solution.py:575
  44.0 0.0 collective-permute-done.3.other
  44.1 9.5 %all_to_all.11.totals = bf16[8,208,128]{2,1,0:T(8,128)(2,1)S(1)} all-to-all(bf16[8,208,128]{2,1,0:T(8,128)(2,1)S(1)} %total.1), channel_id=1, replica_groups=mesh['side'=2,'snap'=4,'x'=2,'core'=2] {'snap','x'}, dimensions={0} | all-to-all | bytes 851968 | tf_op jit(solution)/shard_map/all_to_all | solution.py:589
  53.6 2.6 %collective-permute-start.4 = (bf16[8,208,128]{2,1,0:T(8,128)(2,1)S(1)}, bf16[8,208,128]{2,1,0:T(8,128)(2,1)S(1)}, u32[]{:S(2)}, u32[]{:S(2)}) collective-permute-start(bf16[8,208,128]{2,1,0:T(8,128)(2,1)S(1)} %all_to_all.11.totals), channel_id=1, source_target_pairs={{0,1},{1,0},{2,3},{3,2},{4,5},{5,4},{6,7},{7,6},{8,9},{9,8},{10,11... | collective-permute-start | bytes 1277960 | tf_op jit(solution)/shard_map/ppermute | solution.py:591
  56.2 0.0 copy-done.3
  56.2 0.0 copy-done.4
  56.2 3.6 %update_own.1 = (f32[1,192]{1,0:T(1,128)}, f32[1,192]{1,0:T(1,128)}, f32[1,192]{1,0:T(1,128)}, f32[1,192]{1,0:T(1,128)}, bf16[192]{0:T(256)(128)(2,1)}, /*index=...) custom-call(bf16[8,208,128]{2,1,0:T(8,128)(2,1)S(1)} %all_to_all.11., ...), custom_call_target="tpu_custom_call" | custom-call | flops 1048576 | bytes 4194304 | tf_op jit(solution)/shard_map/update_own/pallas_call | solution.py:595
  59.8 0.0 collective-permute-done.4.totals
  59.8 2.0 %update_other.1 = (f32[1600,128]{1,0:T(8,128)}, f32[1600,128]{1,0:T(8,128)}, f32[1600,128]{1,0:T(8,128)}, f32[1600,128]{1,0:T(8,128)}, bf16[1600,128]{1,0:T(8,12...) custom-call(bf16[8,208,128]{2,1,0:T(8,128)(2,1)S(1)} %collective-per, ...), custom_call_target="tpu_custom_call", output_to_operand_aliasing={{0}: (7, {}), {1}: (8, {}), {2}: (9, {}), {3}: (10, {}), {4... | custom-call | flops 1048576 | bytes 4194304 | tf_op jit(solution)/shard_map/update_other/pallas_call | solution.py:604
  (2 shorter events, 0.0 us)
Async XLA Ops:
  0.7 5.3 %copy-start.1 = (bf16[4,32,64,128]{3,2,1,0:T(8,128)(2,1)S(1)}, bf16[4,32,64,128]{3,2,1,0:T(8,128)(2,1)}, u32[]{:S(2)}) copy-start(bf16[4,32,64,128]{3,2,1,0:T(8,128)(2,1)} %cv.1) | copy-start | bytes 6291460
  0.7 5.3 %copy-start = (bf16[4,32,64,128]{3,2,1,0:T(8,128)(2,1)S(1)}, bf16[4,32,64,128]{3,2,1,0:T(8,128)(2,1)}, u32[]{:S(2)}) copy-start(bf16[4,32,64,128]{3,2,1,0:T(8,128)(2,1)} %xv.1) | copy-start | bytes 6291460
  0.7 5.3 %copy-start.5 = (s32[4]{0:T(128)S(1)}, s32[4]{0:T(128)}, u32[]{:S(2)}) copy-start(s32[4]{0:T(128)} %mask.3) | copy-start | bytes 52
  0.7 5.3 %copy-start.2 = (f32[192]{0:T(256)S(1)}, f32[192]{0:T(256)}, u32[]{:S(2)}) copy-start(f32[192]{0:T(256)} %param.19) | copy-start | bytes 2308
  2.2 13.9 %collective-permute-start = (bf16[4,12,64,128]{3,2,1,0:T(8,128)(2,1)S(1)}, bf16[4,12,64,128]{3,2,1,0:T(8,128)(2,1)S(1)}, u32[]{:S(2)}, u32[]{:S(2)}) collective-permute-start(bf16[4,12,64,128]{3,2,1,0:T(8,128)(2,1)S(1)} %get-tuple-element.93), channel_id=1, source_target_pairs={{1,2},{2,1},{0,4},{3,7},{5,6},{6,5},{4,0},{7,3},{9,10},{10,9},{8,1... | collective-permute-start | bytes 2359304 | tf_op jit(solution)/shard_map/ppermute | solution.py:515
  4.9 11.2 %collective-permute-start.1 = (bf16[4,12,64,128]{3,2,1,0:T(8,128)(2,1)S(1)}, bf16[4,12,64,128]{3,2,1,0:T(8,128)(2,1)S(1)}, u32[]{:S(2)}, u32[]{:S(2)}) collective-permute-start(bf16[4,12,64,128]{3,2,1,0:T(8,128)(2,1)S(1)} %get-tuple-element.94), channel_id=1, source_target_pairs={{0,1},{1,0},{2,3},{3,2},{4,5},{5,4},{6,7},{7,6},{8,9},{9,8},{10,11... | collective-permute-start | bytes 2359304 | tf_op jit(solution)/shard_map/ppermute | solution.py:516
  24.2 1.8 %collective-permute-start.2 = (bf16[8,208,128]{2,1,0:T(8,128)(2,1)S(1)}, bf16[8,208,128]{2,1,0:T(8,128)(2,1)S(1)}, u32[]{:S(2)}, u32[]{:S(2)}) collective-permute-start(bf16[8,208,128]{2,1,0:T(8,128)(2,1)S(1)} %get-tuple-element.113), channel_id=1, source_target_pairs={{0,1},{1,0},{2,3},{3,2},{4,5},{5,4},{6,7},{7,6},{8,9},{9,8},{10,11... | collective-permute-start | bytes 1277960 | tf_op jit(solution)/shard_map/ppermute | solution.py:549
  37.4 6.6 %collective-permute-start.3 = (bf16[208,128]{1,0:T(8,128)(2,1)S(1)}, bf16[208,128]{1,0:T(8,128)(2,1)S(1)}, u32[]{:S(2)}, u32[]{:S(2)}) collective-permute-start(bf16[208,128]{1,0:T(8,128)(2,1)S(1)} %partial.1.own), channel_id=1, source_target_pairs={{0,16},{16,0},{1,17},{17,1},{2,18},{18,2},{3,19},{19,3},{4,20},{20... | collective-permute-start | bytes 159752 | tf_op jit(solution)/shard_map/ppermute | solution.py:562
  39.8 16.4 %copy-start.3 = (f32[192]{0:T(256)S(1)}, f32[192]{0:T(256)}, u32[]{:S(2)}) copy-start(f32[192]{0:T(256)} %param.22) | copy-start | bytes 2308
  39.8 16.4 %copy-start.4 = (f32[192]{0:T(256)S(1)}, f32[192]{0:T(256)}, u32[]{:S(2)}) copy-start(f32[192]{0:T(256)} %param.25) | copy-start | bytes 2308
  53.6 6.3 %collective-permute-start.4 = (bf16[8,208,128]{2,1,0:T(8,128)(2,1)S(1)}, bf16[8,208,128]{2,1,0:T(8,128)(2,1)S(1)}, u32[]{:S(2)}, u32[]{:S(2)}) collective-permute-start(bf16[8,208,128]{2,1,0:T(8,128)(2,1)S(1)} %all_to_all.11.totals), channel_id=1, source_target_pairs={{0,1},{1,0},{2,3},{3,2},{4,5},{5,4},{6,7},{7,6},{8,9},{9,8},{10,11... | collective-permute-start | bytes 1277960 | tf_op jit(solution)/shard_map/ppermute | solution.py:591

commit v4 on v3

--- a/solution.py
+++ b/solution.py
@@ -177,13 +177,11 @@
 
 
 def live_lanes(lens, mask):
-    slot = lax.broadcasted_iota(jnp.int32, (1, 256), 1) // 64
-    lanes, count = jnp.zeros((1, 256), F32), jnp.float32(0)
+    lane = lax.broadcasted_iota(jnp.int32, (1, 256), 1)
+    length, valid = jnp.broadcast_to(lens, (1, 256)), jnp.zeros((1, 256), jnp.int32)
     for n in range(4):
-        valid = jnp.where((n < lens[0]) & (mask[n] > 0), 1.0, 0.0)
-        count = count + valid
-        lanes = jnp.where(slot == n, valid, lanes)
-    return lanes, count
+        valid = jnp.where(lane // 64 == n, jnp.broadcast_to(mask[:, n : n + 1], (1, 256)), valid)
+    return jnp.where((lane // 64 < length) & (valid > 0), 1.0, 0.0)
 
 
 def bias_tiles(bias):
@@ -237,7 +235,7 @@
 
 def inner_kernel(
     R, U, xv, cv, we_hbm, wdt_hbm, bias, lens, mask,
-    xb, l3, slope, d5, value, seeds, dsum, acc0, acc1, e_rows, esum, we2, wd2, wb, bias_enc, bias_dec, split_ref, we, wdt, sems,
+    xb, l3, slope, d5, value, seeds, dsum, acc0, acc1, e_rows, esum, we2, wd2, wb, bias_enc, bias_dec, split_ref, live, we, wdt, sems,
 ):
     I = R // 2
     copies = [pltpu.make_async_copy(a, b, sems.at[n]) for n, (a, b) in enumerate(((we_hbm, we), (wdt_hbm, wdt)))]
@@ -245,7 +243,8 @@
         c.start()
     split_ref[...] = split_matrix()
     dsum[...] = jnp.zeros_like(dsum)
-    live_lane, _ = live_lanes(lens, mask)
+    live_lane = live_lanes(lens[...], mask[...])
+    live[...] = jnp.broadcast_to(live_lane, live.shape)
     bias_enc[...], bias_dec[...] = bias_tiles(bias[...])
     esum[...] = jnp.zeros_like(esum)
 
@@ -283,7 +282,7 @@
 
 
 def outer_kernel(
-    R, far, near, lens, mask, we2, wd2, wb, bias_enc, bias_dec, split_ref,
+    R, far, near, we2, wd2, wb, bias_enc, bias_dec, split_ref, live,
     xb_in, l3_in, slope_in, d5_in, value_in, seeds_in, dsum_in, dec0_in, dec1_in, e_rows_in, esum_in,
     keep, send, xb, l3, slope, d5, value, seeds, dsum, dec0, dec1, e_rows, esum, enc0, enc1,
 ):
@@ -291,7 +290,8 @@
     core = lax.axis_index("core")
     row_at = lax.axis_index("x") * 2 + core
     ends = row_at == 0, row_at == lax.axis_size("x") * 2 - 1
-    live_lane, count = live_lanes(lens, mask)
+    live_lane = live[:1]
+    count = sum(live_lane[:, n * 64 : n * 64 + 1] for n in range(4))
     upper = core == 0
 
     def above(r):
@@ -483,7 +483,7 @@
     peers = lax.axis_size("snap") * nx
     swap = [(0, 1), (1, 0)]
     decoder_t = jnp.swapaxes(decoder_kernel, 2, 3)
-    vmem, smem, hbm = (pl.BlockSpec(memory_space=m) for m in (pltpu.VMEM, pltpu.SMEM, pltpu.HBM))
+    vmem, hbm = (pl.BlockSpec(memory_space=m) for m in (pltpu.VMEM, pltpu.HBM))
 
     def call(kernel, name, megabytes, flops, **kw):
         return pl.pallas_call(
@@ -524,27 +524,28 @@
     ]
     shared = [
         sds(128, KERNEL_ROWS), sds(256, 1152), sds(128, KERNEL_ROWS), sds(128, 256, dtype=F32), sds(256, 256, dtype=F32), sds(256, 256),
+        sds(8, 256, dtype=F32),
     ]
     parts = call(
         functools.partial(inner_kernel, R, U), "inner", INNER_MB, 2 * conv,
         out_shape=state + shared,
-        in_specs=[vmem] * 2 + [hbm] * 2 + [vmem] + [smem] * 2,
-        out_specs=[vmem] * 17,
+        in_specs=[vmem] * 2 + [hbm] * 2 + [vmem] * 3,
+        out_specs=[vmem] * 18,
         scratch_shapes=[
             pltpu.VMEM(encoder_kernel.shape, F32),
             pltpu.VMEM(encoder_kernel.shape, F32),
             pltpu.SemaphoreType.DMA((2,)),
         ],
-    )(in_vmem(snapshots), in_vmem(cotangent), in_hbm(encoder_kernel), in_hbm(decoder_t), bias_row, lengths, slot_mask)
+    )(in_vmem(snapshots), in_vmem(cotangent), in_hbm(encoder_kernel), in_hbm(decoder_t), bias_row, lengths.reshape(1, 1), slot_mask.reshape(1, slots))
     chunk = sds(peers, HEAD + chunk_span(peers), 128)
     keep, send, _, _, _, _, value, _, _, _, _, e_rows, _ = call(
         functools.partial(outer_kernel, R), "outer", OUTER_MB, 4 * conv,
         out_shape=[chunk, chunk] + state,
-        in_specs=[vmem] * 2 + [smem] * 2 + [vmem] * 17,
+        in_specs=[vmem] * 20,
         out_specs=[vmem] * 13,
-        input_output_aliases={10 + n: 2 + n for n in range(11)},
+        input_output_aliases={9 + n: 2 + n for n in range(11)},
         scratch_shapes=[pltpu.VMEM((320, 384), F32), pltpu.VMEM((320, 256), F32)],
-    )(far, near, lengths, slot_mask, *parts[11:], *parts[:11])
+    )(far, near, *parts[11:], *parts[:11])
 
     recv = lax.ppermute(send, "core", swap)
     output = call(

time: 62.3 us -> 61.4 us (0.986)
  Pallas kernels: 31.3 us -> 30 us
    pallas_call x1, Pallas kernels: 8.08 us -> 7.34 us  [on_device(): call(functools.partial(outer_kernel, R), 'outer', OUTER_MB, 4 * conv, out...]
  transfers between devices with their start and end apart: 5 -> 5, of which waited for: 0 -> 0; matrix products, arithmetic and copies ran while one was open for 0% -> 0% of each run, Pallas kernels for 32% -> 31%
where the time goes in v4:
time: 61.4 us; the launch traced here: 61.2 us
  Pallas kernels  30 us (49%)
  blocking collectives  21.1 us (34%)
  starting transfers between devices  8.24 us (13%)
  between operations  1.63 us (3%)
    all_to_all x1, blocking collectives, on_device(): parts = lax.all_to_all(part, ('snap', 'x'), 0, 0, tiled=True)  11.6 us
    pallas_call x1, Pallas kernels, on_device(): call(functools.partial(inner_kernel, R, U), 'inner', INNER_MB, 2 * conv,...  9.53 us
    all_to_all x1, blocking collectives, on_device(): mine = lax.all_to_all(wide, ('snap', 'x'), 0, 0, tiled=True)  9.5 us
    pallas_call x1, Pallas kernels, on_device(): call(functools.partial(outer_kernel, R), 'outer', OUTER_MB, 4 * conv, out...  7.34 us
    pallas_call x1, Pallas kernels, on_device(): call(functools.partial(scatter_kernel, R, U), 'scatter', FIELD_MB, conv,...  4.16 us
    pallas_call x1, Pallas kernels, on_device(): call(functools.partial(own_update_kernel, R), 'update_own', UPDATE_MB, 1...  3.6 us
    ppermute x1, starting transfers between devices, on_device(): lax.ppermute(far, ('snap', 'x', 'core'), far_pairs(lax.axis_size('snap'),...  2.67 us
    ppermute x1, starting transfers between devices, on_device(): other = lax.ppermute(mine, 'core', swap)  2.64 us
  transfers between devices with their start and end apart: 5, of which 0 were waited for; matrix products, arithmetic and copies ran while one was open for 0% of the time, Pallas kernels for 31%

profile of v4, /device:TPU:1, one launch (start us, length us, event | category | flops | bytes accessed | tf_op | source)
XLA Modules:
  0.0 61.2 jit_solution(17860789555740519122)
XLA Ops:
  0.7 0.0 copy-start.1
  0.7 0.0 copy-start
  0.7 0.0 copy-start.2
  0.7 0.0 copy-start.5
  0.7 1.5 %halo.1 = (bf16[4,12,64,128]{3,2,1,0:T(8,128)(2,1)S(1)}, bf16[4,12,64,128]{3,2,1,0:T(8,128)(2,1)S(1)}) custom-call(bf16[4,32,64,128]{3,2,1,0:T(8,128)(2,1)} %xv.1, bf16[4,32,64,128]{3,2,1,0:T(8,128)(2,1)} %cv.1), custom_call_target="tpu_custom_call" | custom-call | bytes 4194304 | tf_op jit(solution)/shard_map/halo/pallas_call | solution.py:508
  2.2 2.7 %collective-permute-start = (bf16[4,12,64,128]{3,2,1,0:T(8,128)(2,1)S(1)}, bf16[4,12,64,128]{3,2,1,0:T(8,128)(2,1)S(1)}, u32[]{:S(2)}, u32[]{:S(2)}) collective-permute-start(bf16[4,12,64,128]{3,2,1,0:T(8,128)(2,1)S(1)} %get-tuple-element.94), channel_id=1, source_target_pairs={{1,2},{2,1},{0,4},{3,7},{5,6},{6,5},{4,0},{7,3},{9,10},{10,9},{8,1... | collective-permute-start | bytes 2359304 | tf_op jit(solution)/shard_map/ppermute | solution.py:515
  4.9 0.4 collective-permute-start.1
  6.0 0.0 copy-done.1
  6.0 0.0 copy-done
  6.0 0.0 copy-done.2
  6.0 0.0 copy-done.5
  6.0 9.5 %inner.1 = (bf16[48,320,256]{2,1,0:T(8,128)(2,1)S(1)}, bf16[22,384,256]{2,1,0:T(8,128)(2,1)S(1)}, f32[18,128,256]{2,1,0:T(8,128)S(1)}, bf16[40,320,256]{2,1,0:T(...) custom-call(bf16[4,32,64,128]{3,2,1,0:T(8,128)(2,1)S(1)} %copy-done,, ...), custom_call_target="tpu_custom_call" | custom-call | flops 3355443200 | bytes 4194304 | tf_op jit(solution)/shard_map/inner/pallas_call | solution.py:529
  15.6 0.0 collective-permute-done.far
  15.6 0.0 collective-permute-done.1.near
  15.6 7.3 %outer.1 = (bf16[8,208,128]{2,1,0:T(8,128)(2,1)S(1)}, bf16[8,208,128]{2,1,0:T(8,128)(2,1)S(1)}, bf16[48,320,256]{2,1,0:T(8,128)(2,1)S(1)}, bf16[22,384,256]{2,1,...) custom-call(bf16[4,12,64,128]{3,2,1,0:T(8,128)(2,1)S(1)} %collective, ...), custom_call_target="tpu_custom_call", output_to_operand_aliasing={{2}: (9, {}), {3}: (10, {}), {4}: (11, {}), {5}: (12, {}), ... | custom-call | flops 6710886400 | bytes 4194304 | tf_op jit(solution)/shard_map/outer/pallas_call | solution.py:541
  22.9 0.1 collective-permute-start.2
  23.1 1.7 %output.1 = bf16[4,32,64,128]{3,2,1,0:T(8,128)(2,1)} custom-call(bf16[16,256,256]{2,1,0:T(8,128)(2,1)S(1)} %get-tuple-element.116.value), custom_call_target="tpu_custom_call" | custom-call | flops 419430400 | bytes 4194304 | tf_op jit(solution)/shard_map/output/pallas_call | solution.py:551
  24.7 0.0 collective-permute-done.2
  24.8 0.1 add_convert_fusion
  24.9 11.6 %all_to_all.10.parts = bf16[8,208,128]{2,1,0:T(8,128)(2,1)S(1)} all-to-all(bf16[8,208,128]{2,1,0:T(8,128)(2,1)S(1)} %add_convert_fusion), channel_id=1, replica_groups=mesh['side'=2,'snap'=4,'x'=2,'core'=2] {'snap','x'}, dimensions={0} | all-to-all | bytes 851968 | tf_op jit(solution)/shard_map/all_to_all | solution.py:560
  36.5 0.1 partial.1.own
  36.6 2.4 %collective-permute-start.3 = (bf16[208,128]{1,0:T(8,128)(2,1)S(1)}, bf16[208,128]{1,0:T(8,128)(2,1)S(1)}, u32[]{:S(2)}, u32[]{:S(2)}) collective-permute-start(bf16[208,128]{1,0:T(8,128)(2,1)S(1)} %partial.1.own), channel_id=1, source_target_pairs={{0,16},{16,0},{1,17},{17,1},{2,18},{18,2},{3,19},{19,3},{4,20},{20... | collective-permute-start | bytes 159752 | tf_op jit(solution)/shard_map/ppermute | solution.py:563
  39.0 0.0 copy-start.3
  39.0 4.2 %scatter.1 = (f32[16,256,256]{2,1,0:T(8,128)S(1)}, f32[1600,128]{1,0:T(8,128)S(1)}, f32[1600,128]{1,0:T(8,128)S(1)}, f32[1600,128]{1,0:T(8,128)S(1)}, f32[1600,1...) custom-call(bf16[18,128,256]{2,1,0:T(8,128)(2,1)S(1)} %get-tuple-element.121.e_rows, ...), custom_call_target="tpu_custom_call" | custom-call | flops 1677721600 | bytes 4194304 | tf_op jit(solution)/shard_map/scatter/pallas_call | solution.py:576
  43.1 0.0 collective-permute-done.3.other
  43.2 9.5 %all_to_all.11.totals = bf16[8,208,128]{2,1,0:T(8,128)(2,1)S(1)} all-to-all(bf16[8,208,128]{2,1,0:T(8,128)(2,1)S(1)} %total.1), channel_id=1, replica_groups=mesh['side'=2,'snap'=4,'x'=2,'core'=2] {'snap','x'}, dimensions={0} | all-to-all | bytes 851968 | tf_op jit(solution)/shard_map/all_to_all | solution.py:590
  52.7 2.6 %collective-permute-start.4 = (bf16[8,208,128]{2,1,0:T(8,128)(2,1)S(1)}, bf16[8,208,128]{2,1,0:T(8,128)(2,1)S(1)}, u32[]{:S(2)}, u32[]{:S(2)}) collective-permute-start(bf16[8,208,128]{2,1,0:T(8,128)(2,1)S(1)} %all_to_all.11.totals), channel_id=1, source_target_pairs={{0,1},{1,0},{2,3},{3,2},{4,5},{5,4},{6,7},{7,6},{8,9},{9,8},{10,11... | collective-permute-start | bytes 1277960 | tf_op jit(solution)/shard_map/ppermute | solution.py:592
  55.3 0.0 copy-done.3
  55.3 0.0 copy-done.4
  55.3 3.6 %update_own.1 = (f32[1,192]{1,0:T(1,128)}, f32[1,192]{1,0:T(1,128)}, f32[1,192]{1,0:T(1,128)}, f32[1,192]{1,0:T(1,128)}, bf16[192]{0:T(256)(128)(2,1)}, /*index=...) custom-call(bf16[8,208,128]{2,1,0:T(8,128)(2,1)S(1)} %all_to_all.11., ...), custom_call_target="tpu_custom_call" | custom-call | flops 1048576 | bytes 4194304 | tf_op jit(solution)/shard_map/update_own/pallas_call | solution.py:596
  59.0 0.0 collective-permute-done.4.totals
  59.0 2.0 %update_other.1 = (f32[1600,128]{1,0:T(8,128)}, f32[1600,128]{1,0:T(8,128)}, f32[1600,128]{1,0:T(8,128)}, f32[1600,128]{1,0:T(8,128)}, bf16[1600,128]{1,0:T(8,12...) custom-call(bf16[8,208,128]{2,1,0:T(8,128)(2,1)S(1)} %collective-per, ...), custom_call_target="tpu_custom_call", output_to_operand_aliasing={{0}: (7, {}), {1}: (8, {}), {2}: (9, {}), {3}: (10, {}), {4... | custom-call | flops 1048576 | bytes 4194304 | tf_op jit(solution)/shard_map/update_other/pallas_call | solution.py:605
  (2 shorter events, 0.0 us)
Async XLA Ops:
  0.7 5.3 %copy-start.1 = (bf16[4,32,64,128]{3,2,1,0:T(8,128)(2,1)S(1)}, bf16[4,32,64,128]{3,2,1,0:T(8,128)(2,1)}, u32[]{:S(2)}) copy-start(bf16[4,32,64,128]{3,2,1,0:T(8,128)(2,1)} %cv.1) | copy-start | bytes 6291460
  0.7 5.3 %copy-start = (bf16[4,32,64,128]{3,2,1,0:T(8,128)(2,1)S(1)}, bf16[4,32,64,128]{3,2,1,0:T(8,128)(2,1)}, u32[]{:S(2)}) copy-start(bf16[4,32,64,128]{3,2,1,0:T(8,128)(2,1)} %xv.1) | copy-start | bytes 6291460
  0.7 5.3 %copy-start.2 = (f32[192]{0:T(256)S(1)}, f32[192]{0:T(256)}, u32[]{:S(2)}) copy-start(f32[192]{0:T(256)} %param.19) | copy-start | bytes 2308
  0.7 5.3 %copy-start.5 = (s32[4]{0:T(128)S(1)}, s32[4]{0:T(128)}, u32[]{:S(2)}) copy-start(s32[4]{0:T(128)} %param.16) | copy-start | bytes 52
  2.2 13.3 %collective-permute-start = (bf16[4,12,64,128]{3,2,1,0:T(8,128)(2,1)S(1)}, bf16[4,12,64,128]{3,2,1,0:T(8,128)(2,1)S(1)}, u32[]{:S(2)}, u32[]{:S(2)}) collective-permute-start(bf16[4,12,64,128]{3,2,1,0:T(8,128)(2,1)S(1)} %get-tuple-element.94), channel_id=1, source_target_pairs={{1,2},{2,1},{0,4},{3,7},{5,6},{6,5},{4,0},{7,3},{9,10},{10,9},{8,1... | collective-permute-start | bytes 2359304 | tf_op jit(solution)/shard_map/ppermute | solution.py:515
  4.9 10.7 %collective-permute-start.1 = (bf16[4,12,64,128]{3,2,1,0:T(8,128)(2,1)S(1)}, bf16[4,12,64,128]{3,2,1,0:T(8,128)(2,1)S(1)}, u32[]{:S(2)}, u32[]{:S(2)}) collective-permute-start(bf16[4,12,64,128]{3,2,1,0:T(8,128)(2,1)S(1)} %get-tuple-element.95), channel_id=1, source_target_pairs={{0,1},{1,0},{2,3},{3,2},{4,5},{5,4},{6,7},{7,6},{8,9},{9,8},{10,11... | collective-permute-start | bytes 2359304 | tf_op jit(solution)/shard_map/ppermute | solution.py:516
  22.9 1.8 %collective-permute-start.2 = (bf16[8,208,128]{2,1,0:T(8,128)(2,1)S(1)}, bf16[8,208,128]{2,1,0:T(8,128)(2,1)S(1)}, u32[]{:S(2)}, u32[]{:S(2)}) collective-permute-start(bf16[8,208,128]{2,1,0:T(8,128)(2,1)S(1)} %get-tuple-element.115), channel_id=1, source_target_pairs={{0,1},{1,0},{2,3},{3,2},{4,5},{5,4},{6,7},{7,6},{8,9},{9,8},{10,11... | collective-permute-start | bytes 1277960 | tf_op jit(solution)/shard_map/ppermute | solution.py:550
  36.6 6.6 %collective-permute-start.3 = (bf16[208,128]{1,0:T(8,128)(2,1)S(1)}, bf16[208,128]{1,0:T(8,128)(2,1)S(1)}, u32[]{:S(2)}, u32[]{:S(2)}) collective-permute-start(bf16[208,128]{1,0:T(8,128)(2,1)S(1)} %partial.1.own), channel_id=1, source_target_pairs={{0,16},{16,0},{1,17},{17,1},{2,18},{18,2},{3,19},{19,3},{4,20},{20... | collective-permute-start | bytes 159752 | tf_op jit(solution)/shard_map/ppermute | solution.py:563
  39.0 16.4 %copy-start.3 = (f32[192]{0:T(256)S(1)}, f32[192]{0:T(256)}, u32[]{:S(2)}) copy-start(f32[192]{0:T(256)} %param.22) | copy-start | bytes 2308
  39.0 16.4 %copy-start.4 = (f32[192]{0:T(256)S(1)}, f32[192]{0:T(256)}, u32[]{:S(2)}) copy-start(f32[192]{0:T(256)} %param.25) | copy-start | bytes 2308
  52.7 6.3 %collective-permute-start.4 = (bf16[8,208,128]{2,1,0:T(8,128)(2,1)S(1)}, bf16[8,208,128]{2,1,0:T(8,128)(2,1)S(1)}, u32[]{:S(2)}, u32[]{:S(2)}) collective-permute-start(bf16[8,208,128]{2,1,0:T(8,128)(2,1)S(1)} %all_to_all.11.totals), channel_id=1, source_target_pairs={{0,1},{1,0},{2,3},{3,2},{4,5},{5,4},{6,7},{7,6},{8,9},{9,8},{10,11... | collective-permute-start | bytes 1277960 | tf_op jit(solution)/shard_map/ppermute | solution.py:592

commit v5 on v4

--- a/solution.py
+++ b/solution.py
@@ -448,18 +448,21 @@
 
 
 def own_update_kernel(R, totals, *refs):
-    params, small, grads, bias_out, ig, rest, (field, merge_ref, sems) = (
-        refs[:6], refs[6:9], refs[9], refs[10:15], refs[15], refs[16:-3], refs[-3:],
+    params, small, grads, bias_out, ig, rest, (field, merge_ref, sems), bias_ref, bias_sems = (
+        refs[:6], refs[6:9], refs[9], refs[10:15], refs[15], refs[16:32], refs[32:35], refs[35:40], refs[40],
     )
     head = totals[0, :16].astype(F32)
     scale = 1.0 / head[:1]
     wide_scale = jnp.concatenate([scale] * 2, axis=1)
     merge_ref[...] = merge_matrix()
-    copies = merge_field(R, lambda s: (grads[s] * wide_scale).astype(BF16), merge_ref[...], field, ig, sems)
     grad = jnp.concatenate([head[1:2], head[2:3, :64]], axis=1) * scale[:, :1]
     mom, ema, new = advance(grad, *[r[...] for r in small])
-    for ref, v in zip(bias_out, (grad, mom, ema, new, new.astype(BF16).reshape(-1)), strict=True):
-        ref[...] = v
+    copies = []
+    for n, v in enumerate((grad, mom, ema, new, new.astype(BF16).reshape(-1))):
+        bias_ref[n][...] = v
+        copies.append(pltpu.make_async_copy(bias_ref[n], bias_out[n], bias_sems.at[n]))
+        copies[-1].start()
+    copies += merge_field(R, lambda s: (grads[s] * wide_scale).astype(BF16), merge_ref[...], field, ig, sems)
     update_kernel(0, totals, *params, *rest)
     for c in copies:
         c.wait()
@@ -592,13 +595,16 @@
     other = lax.ppermute(mine, "core", swap)
     five = [pltpu.HBM(shape, F32)] * 4 + [pltpu.HBM(shape, BF16)]
     staged = [pltpu.VMEM(v.shape, v.dtype) for v in five] + [pltpu.SemaphoreType.DMA((5 * PARTS,))]
-    bias_shape = [sds(1, latent_ch + C, dtype=F32)] * 4 + [sds(latent_ch + C)]
+    bias_shape = [pltpu.HBM((1, latent_ch + C), F32)] * 4 + [pltpu.HBM((latent_ch + C,), BF16)]
     own = call(
         functools.partial(own_update_kernel, R), "update_own", UPDATE_MB, 1 << 20,
         out_shape=bias_shape + [field] + five * 2,
         in_specs=[vmem] * 11,
-        out_specs=[vmem] * 5 + [hbm] * 11,
-        scratch_shapes=staged + [pltpu.VMEM(snapshots.shape, BF16), pltpu.VMEM((256, 256), BF16), pltpu.SemaphoreType.DMA((4,))],
+        out_specs=[hbm] * 16,
+        scratch_shapes=staged
+        + [pltpu.VMEM(snapshots.shape, BF16), pltpu.VMEM((256, 256), BF16), pltpu.SemaphoreType.DMA((4,))]
+        + [pltpu.VMEM(v.shape, v.dtype) for v in bias_shape]
+        + [pltpu.SemaphoreType.DMA((5,))],
     )(mine, *params, bias_row, bias_mom.reshape(1, -1), bias_ema.reshape(1, -1), grads)
     bias_results, input_grad, begun = own[:5], own[5], own[6:]
     bias_grad, bia_mom, bia_ema, bia_new, bia_copy = [v.reshape(biases.shape) for v in bias_results]

time: 61.4 us -> 60.9 us (level)
  transfers between devices with their start and end apart: 5 -> 5, of which waited for: 0 -> 0; matrix products, arithmetic and copies ran while one was open for 0% -> 0% of each run, Pallas kernels for 31% -> 30%
where the time goes in v5:
time: 60.9 us; the launch traced here: 60.7 us
  Pallas kernels  29.5 us (48%)
  blocking collectives  21.1 us (35%)
  starting transfers between devices  8.24 us (14%)
  between operations  1.63 us (3%)
    all_to_all x1, blocking collectives, on_device(): parts = lax.all_to_all(part, ('snap', 'x'), 0, 0, tiled=True)  11.6 us
    pallas_call x1, Pallas kernels, on_device(): call(functools.partial(inner_kernel, R, U), 'inner', INNER_MB, 2 * conv,...  9.53 us
    all_to_all x1, blocking collectives, on_device(): mine = lax.all_to_all(wide, ('snap', 'x'), 0, 0, tiled=True)  9.5 us
    pallas_call x1, Pallas kernels, on_device(): call(functools.partial(outer_kernel, R), 'outer', OUTER_MB, 4 * conv, out...  7.34 us
    pallas_call x1, Pallas kernels, on_device(): call(functools.partial(scatter_kernel, R, U), 'scatter', FIELD_MB, conv,...  4.16 us
    pallas_call x1, Pallas kernels, on_device(): call(functools.partial(own_update_kernel, R), 'update_own', UPDATE_MB, 1...  3.1 us
    ppermute x1, starting transfers between devices, on_device(): lax.ppermute(far, ('snap', 'x', 'core'), far_pairs(lax.axis_size('snap'),...  2.67 us
    ppermute x1, starting transfers between devices, on_device(): other = lax.ppermute(mine, 'core', swap)  2.64 us
  transfers between devices with their start and end apart: 5, of which 0 were waited for; matrix products, arithmetic and copies ran while one was open for 0% of the time, Pallas kernels for 30%

profile of v5, /device:TPU:1, one launch (start us, length us, event | category | flops | bytes accessed | tf_op | source)
XLA Modules:
  0.0 60.7 jit_solution(12510236976493565428)
XLA Ops:
  0.7 0.0 copy-start.1
  0.7 0.0 copy-start
  0.7 0.0 copy-start.2
  0.7 0.0 copy-start.5
  0.7 1.5 %halo.1 = (bf16[4,12,64,128]{3,2,1,0:T(8,128)(2,1)S(1)}, bf16[4,12,64,128]{3,2,1,0:T(8,128)(2,1)S(1)}) custom-call(bf16[4,32,64,128]{3,2,1,0:T(8,128)(2,1)} %xv.1, bf16[4,32,64,128]{3,2,1,0:T(8,128)(2,1)} %cv.1), custom_call_target="tpu_custom_call" | custom-call | bytes 4194304 | tf_op jit(solution)/shard_map/halo/pallas_call | solution.py:511
  2.2 2.7 %collective-permute-start = (bf16[4,12,64,128]{3,2,1,0:T(8,128)(2,1)S(1)}, bf16[4,12,64,128]{3,2,1,0:T(8,128)(2,1)S(1)}, u32[]{:S(2)}, u32[]{:S(2)}) collective-permute-start(bf16[4,12,64,128]{3,2,1,0:T(8,128)(2,1)S(1)} %get-tuple-element.94), channel_id=1, source_target_pairs={{1,2},{2,1},{0,4},{3,7},{5,6},{6,5},{4,0},{7,3},{9,10},{10,9},{8,1... | collective-permute-start | bytes 2359304 | tf_op jit(solution)/shard_map/ppermute | solution.py:518
  4.9 0.4 collective-permute-start.1
  6.0 0.0 copy-done.1
  6.0 0.0 copy-done
  6.0 0.0 copy-done.2
  6.0 0.0 copy-done.5
  6.0 9.5 %inner.1 = (bf16[48,320,256]{2,1,0:T(8,128)(2,1)S(1)}, bf16[22,384,256]{2,1,0:T(8,128)(2,1)S(1)}, f32[18,128,256]{2,1,0:T(8,128)S(1)}, bf16[40,320,256]{2,1,0:T(...) custom-call(bf16[4,32,64,128]{3,2,1,0:T(8,128)(2,1)S(1)} %copy-done,, ...), custom_call_target="tpu_custom_call" | custom-call | flops 3355443200 | bytes 4194304 | tf_op jit(solution)/shard_map/inner/pallas_call | solution.py:532
  15.6 0.0 collective-permute-done.far
  15.6 0.0 collective-permute-done.1.near
  15.6 7.3 %outer.1 = (bf16[8,208,128]{2,1,0:T(8,128)(2,1)S(1)}, bf16[8,208,128]{2,1,0:T(8,128)(2,1)S(1)}, bf16[48,320,256]{2,1,0:T(8,128)(2,1)S(1)}, bf16[22,384,256]{2,1,...) custom-call(bf16[4,12,64,128]{3,2,1,0:T(8,128)(2,1)S(1)} %collective, ...), custom_call_target="tpu_custom_call", output_to_operand_aliasing={{2}: (9, {}), {3}: (10, {}), {4}: (11, {}), {5}: (12, {}), ... | custom-call | flops 6710886400 | bytes 4194304 | tf_op jit(solution)/shard_map/outer/pallas_call | solution.py:544
  22.9 0.1 collective-permute-start.2
  23.1 1.7 %output.1 = bf16[4,32,64,128]{3,2,1,0:T(8,128)(2,1)} custom-call(bf16[16,256,256]{2,1,0:T(8,128)(2,1)S(1)} %get-tuple-element.116.value), custom_call_target="tpu_custom_call" | custom-call | flops 419430400 | bytes 4194304 | tf_op jit(solution)/shard_map/output/pallas_call | solution.py:554
  24.7 0.0 collective-permute-done.2
  24.8 0.1 add_convert_fusion
  24.9 11.6 %all_to_all.10.parts = bf16[8,208,128]{2,1,0:T(8,128)(2,1)S(1)} all-to-all(bf16[8,208,128]{2,1,0:T(8,128)(2,1)S(1)} %add_convert_fusion), channel_id=1, replica_groups=mesh['side'=2,'snap'=4,'x'=2,'core'=2] {'snap','x'}, dimensions={0} | all-to-all | bytes 851968 | tf_op jit(solution)/shard_map/all_to_all | solution.py:563
  36.5 0.1 partial.1.own
  36.6 2.4 %collective-permute-start.3 = (bf16[208,128]{1,0:T(8,128)(2,1)S(1)}, bf16[208,128]{1,0:T(8,128)(2,1)S(1)}, u32[]{:S(2)}, u32[]{:S(2)}) collective-permute-start(bf16[208,128]{1,0:T(8,128)(2,1)S(1)} %partial.1.own), channel_id=1, source_target_pairs={{0,16},{16,0},{1,17},{17,1},{2,18},{18,2},{3,19},{19,3},{4,20},{20... | collective-permute-start | bytes 159752 | tf_op jit(solution)/shard_map/ppermute | solution.py:566
  39.0 0.0 copy-start.3
  39.0 4.2 %scatter.1 = (f32[16,256,256]{2,1,0:T(8,128)S(1)}, f32[1600,128]{1,0:T(8,128)S(1)}, f32[1600,128]{1,0:T(8,128)S(1)}, f32[1600,128]{1,0:T(8,128)S(1)}, f32[1600,1...) custom-call(bf16[18,128,256]{2,1,0:T(8,128)(2,1)S(1)} %get-tuple-element.121.e_rows, ...), custom_call_target="tpu_custom_call" | custom-call | flops 1677721600 | bytes 4194304 | tf_op jit(solution)/shard_map/scatter/pallas_call | solution.py:579
  43.1 0.0 collective-permute-done.3.other
  43.2 9.5 %all_to_all.11.totals = bf16[8,208,128]{2,1,0:T(8,128)(2,1)S(1)} all-to-all(bf16[8,208,128]{2,1,0:T(8,128)(2,1)S(1)} %total.1), channel_id=1, replica_groups=mesh['side'=2,'snap'=4,'x'=2,'core'=2] {'snap','x'}, dimensions={0} | all-to-all | bytes 851968 | tf_op jit(solution)/shard_map/all_to_all | solution.py:593
  52.7 2.6 %collective-permute-start.4 = (bf16[8,208,128]{2,1,0:T(8,128)(2,1)S(1)}, bf16[8,208,128]{2,1,0:T(8,128)(2,1)S(1)}, u32[]{:S(2)}, u32[]{:S(2)}) collective-permute-start(bf16[8,208,128]{2,1,0:T(8,128)(2,1)S(1)} %all_to_all.11.totals), channel_id=1, source_target_pairs={{0,1},{1,0},{2,3},{3,2},{4,5},{5,4},{6,7},{7,6},{8,9},{9,8},{10,11... | collective-permute-start | bytes 1277960 | tf_op jit(solution)/shard_map/ppermute | solution.py:595
  55.3 0.0 copy-done.3
  55.3 0.0 copy-done.4
  55.3 3.1 %update_own.1 = (f32[1,192]{1,0:T(1,128)}, f32[1,192]{1,0:T(1,128)}, f32[1,192]{1,0:T(1,128)}, f32[1,192]{1,0:T(1,128)}, bf16[192]{0:T(256)(128)(2,1)}, /*index=...) custom-call(bf16[8,208,128]{2,1,0:T(8,128)(2,1)S(1)} %all_to_all.11., ...), custom_call_target="tpu_custom_call" | custom-call | flops 1048576 | bytes 4194304 | tf_op jit(solution)/shard_map/update_own/pallas_call | solution.py:599
  58.5 0.0 collective-permute-done.4.totals
  58.5 2.0 %update_other.1 = (f32[1600,128]{1,0:T(8,128)}, f32[1600,128]{1,0:T(8,128)}, f32[1600,128]{1,0:T(8,128)}, f32[1600,128]{1,0:T(8,128)}, bf16[1600,128]{1,0:T(8,12...) custom-call(bf16[8,208,128]{2,1,0:T(8,128)(2,1)S(1)} %collective-per, ...), custom_call_target="tpu_custom_call", output_to_operand_aliasing={{0}: (7, {}), {1}: (8, {}), {2}: (9, {}), {3}: (10, {}), {4... | custom-call | flops 1048576 | bytes 4194304 | tf_op jit(solution)/shard_map/update_other/pallas_call | solution.py:611
  (2 shorter events, 0.0 us)
Async XLA Ops:
  0.7 5.3 %copy-start.1 = (bf16[4,32,64,128]{3,2,1,0:T(8,128)(2,1)S(1)}, bf16[4,32,64,128]{3,2,1,0:T(8,128)(2,1)}, u32[]{:S(2)}) copy-start(bf16[4,32,64,128]{3,2,1,0:T(8,128)(2,1)} %cv.1) | copy-start | bytes 6291460
  0.7 5.3 %copy-start = (bf16[4,32,64,128]{3,2,1,0:T(8,128)(2,1)S(1)}, bf16[4,32,64,128]{3,2,1,0:T(8,128)(2,1)}, u32[]{:S(2)}) copy-start(bf16[4,32,64,128]{3,2,1,0:T(8,128)(2,1)} %xv.1) | copy-start | bytes 6291460
  0.7 5.3 %copy-start.2 = (f32[192]{0:T(256)S(1)}, f32[192]{0:T(256)}, u32[]{:S(2)}) copy-start(f32[192]{0:T(256)} %param.19) | copy-start | bytes 2308
  0.7 5.3 %copy-start.5 = (s32[4]{0:T(128)S(1)}, s32[4]{0:T(128)}, u32[]{:S(2)}) copy-start(s32[4]{0:T(128)} %param.16) | copy-start | bytes 52
  2.2 13.3 %collective-permute-start = (bf16[4,12,64,128]{3,2,1,0:T(8,128)(2,1)S(1)}, bf16[4,12,64,128]{3,2,1,0:T(8,128)(2,1)S(1)}, u32[]{:S(2)}, u32[]{:S(2)}) collective-permute-start(bf16[4,12,64,128]{3,2,1,0:T(8,128)(2,1)S(1)} %get-tuple-element.94), channel_id=1, source_target_pairs={{1,2},{2,1},{0,4},{3,7},{5,6},{6,5},{4,0},{7,3},{9,10},{10,9},{8,1... | collective-permute-start | bytes 2359304 | tf_op jit(solution)/shard_map/ppermute | solution.py:518
  4.9 10.7 %collective-permute-start.1 = (bf16[4,12,64,128]{3,2,1,0:T(8,128)(2,1)S(1)}, bf16[4,12,64,128]{3,2,1,0:T(8,128)(2,1)S(1)}, u32[]{:S(2)}, u32[]{:S(2)}) collective-permute-start(bf16[4,12,64,128]{3,2,1,0:T(8,128)(2,1)S(1)} %get-tuple-element.95), channel_id=1, source_target_pairs={{0,1},{1,0},{2,3},{3,2},{4,5},{5,4},{6,7},{7,6},{8,9},{9,8},{10,11... | collective-permute-start | bytes 2359304 | tf_op jit(solution)/shard_map/ppermute | solution.py:519
  22.9 1.8 %collective-permute-start.2 = (bf16[8,208,128]{2,1,0:T(8,128)(2,1)S(1)}, bf16[8,208,128]{2,1,0:T(8,128)(2,1)S(1)}, u32[]{:S(2)}, u32[]{:S(2)}) collective-permute-start(bf16[8,208,128]{2,1,0:T(8,128)(2,1)S(1)} %get-tuple-element.115), channel_id=1, source_target_pairs={{0,1},{1,0},{2,3},{3,2},{4,5},{5,4},{6,7},{7,6},{8,9},{9,8},{10,11... | collective-permute-start | bytes 1277960 | tf_op jit(solution)/shard_map/ppermute | solution.py:553
  36.6 6.6 %collective-permute-start.3 = (bf16[208,128]{1,0:T(8,128)(2,1)S(1)}, bf16[208,128]{1,0:T(8,128)(2,1)S(1)}, u32[]{:S(2)}, u32[]{:S(2)}) collective-permute-start(bf16[208,128]{1,0:T(8,128)(2,1)S(1)} %partial.1.own), channel_id=1, source_target_pairs={{0,16},{16,0},{1,17},{17,1},{2,18},{18,2},{3,19},{19,3},{4,20},{20... | collective-permute-start | bytes 159752 | tf_op jit(solution)/shard_map/ppermute | solution.py:566
  39.0 16.4 %copy-start.3 = (f32[192]{0:T(256)S(1)}, f32[192]{0:T(256)}, u32[]{:S(2)}) copy-start(f32[192]{0:T(256)} %param.22) | copy-start | bytes 2308
  39.0 16.4 %copy-start.4 = (f32[192]{0:T(256)S(1)}, f32[192]{0:T(256)}, u32[]{:S(2)}) copy-start(f32[192]{0:T(256)} %param.25) | copy-start | bytes 2308
  52.7 5.8 %collective-permute-start.4 = (bf16[8,208,128]{2,1,0:T(8,128)(2,1)S(1)}, bf16[8,208,128]{2,1,0:T(8,128)(2,1)S(1)}, u32[]{:S(2)}, u32[]{:S(2)}) collective-permute-start(bf16[8,208,128]{2,1,0:T(8,128)(2,1)S(1)} %all_to_all.11.totals), channel_id=1, source_target_pairs={{0,1},{1,0},{2,3},{3,2},{4,5},{5,4},{6,7},{7,6},{8,9},{9,8},{10,11... | collective-permute-start | bytes 1277960 | tf_op jit(solution)/shard_map/ppermute | solution.py:595

commit v6 on v5

--- a/solution.py
+++ b/solution.py
@@ -416,7 +416,7 @@
         wide[p] = both.astype(BF16)
 
 
-PARTS = 4
+PARTS = 2
 
 
 def update_kernel(owner, totals, *refs):

time: 60.9 us -> 60.8 us (level)
  no operation moved by 1% of the time
where the time goes in v6:
time: 60.8 us; the launch traced here: 60.5 us
  Pallas kernels  29.3 us (48%)
  blocking collectives  21.1 us (35%)
  starting transfers between devices  8.24 us (14%)
  between operations  1.63 us (3%)
    all_to_all x1, blocking collectives, on_device(): parts = lax.all_to_all(part, ('snap', 'x'), 0, 0, tiled=True)  11.6 us
    pallas_call x1, Pallas kernels, on_device(): call(functools.partial(inner_kernel, R, U), 'inner', INNER_MB, 2 * conv,...  9.53 us
    all_to_all x1, blocking collectives, on_device(): mine = lax.all_to_all(wide, ('snap', 'x'), 0, 0, tiled=True)  9.5 us
    pallas_call x1, Pallas kernels, on_device(): call(functools.partial(outer_kernel, R), 'outer', OUTER_MB, 4 * conv, out...  7.34 us
    pallas_call x1, Pallas kernels, on_device(): call(functools.partial(scatter_kernel, R, U), 'scatter', FIELD_MB, conv,...  4.16 us
    pallas_call x1, Pallas kernels, on_device(): call(functools.partial(own_update_kernel, R), 'update_own', UPDATE_MB, 1...  3.02 us
    ppermute x1, starting transfers between devices, on_device(): lax.ppermute(far, ('snap', 'x', 'core'), far_pairs(lax.axis_size('snap'),...  2.67 us
    ppermute x1, starting transfers between devices, on_device(): other = lax.ppermute(mine, 'core', swap)  2.64 us
  transfers between devices with their start and end apart: 5, of which 0 were waited for; matrix products, arithmetic and copies ran while one was open for 0% of the time, Pallas kernels for 30%

profile of v6, /device:TPU:1, one launch (start us, length us, event | category | flops | bytes accessed | tf_op | source)
XLA Modules:
  0.0 60.5 jit_solution(17484028661598477056)
XLA Ops:
  0.7 0.0 copy-start.1
  0.7 0.0 copy-start
  0.7 0.0 copy-start.2
  0.7 0.0 copy-start.5
  0.7 1.5 %halo.1 = (bf16[4,12,64,128]{3,2,1,0:T(8,128)(2,1)S(1)}, bf16[4,12,64,128]{3,2,1,0:T(8,128)(2,1)S(1)}) custom-call(bf16[4,32,64,128]{3,2,1,0:T(8,128)(2,1)} %xv.1, bf16[4,32,64,128]{3,2,1,0:T(8,128)(2,1)} %cv.1), custom_call_target="tpu_custom_call" | custom-call | bytes 4194304 | tf_op jit(solution)/shard_map/halo/pallas_call | solution.py:511
  2.2 2.7 %collective-permute-start = (bf16[4,12,64,128]{3,2,1,0:T(8,128)(2,1)S(1)}, bf16[4,12,64,128]{3,2,1,0:T(8,128)(2,1)S(1)}, u32[]{:S(2)}, u32[]{:S(2)}) collective-permute-start(bf16[4,12,64,128]{3,2,1,0:T(8,128)(2,1)S(1)} %get-tuple-element.94), channel_id=1, source_target_pairs={{1,2},{2,1},{0,4},{3,7},{5,6},{6,5},{4,0},{7,3},{9,10},{10,9},{8,1... | collective-permute-start | bytes 2359304 | tf_op jit(solution)/shard_map/ppermute | solution.py:518
  4.9 0.4 collective-permute-start.1
  6.0 0.0 copy-done.1
  6.0 0.0 copy-done
  6.0 0.0 copy-done.2
  6.0 0.0 copy-done.5
  6.0 9.5 %inner.1 = (bf16[48,320,256]{2,1,0:T(8,128)(2,1)S(1)}, bf16[22,384,256]{2,1,0:T(8,128)(2,1)S(1)}, f32[18,128,256]{2,1,0:T(8,128)S(1)}, bf16[40,320,256]{2,1,0:T(...) custom-call(bf16[4,32,64,128]{3,2,1,0:T(8,128)(2,1)S(1)} %copy-done,, ...), custom_call_target="tpu_custom_call" | custom-call | flops 3355443200 | bytes 4194304 | tf_op jit(solution)/shard_map/inner/pallas_call | solution.py:532
  15.6 0.0 collective-permute-done.far
  15.6 0.0 collective-permute-done.1.near
  15.6 7.3 %outer.1 = (bf16[8,208,128]{2,1,0:T(8,128)(2,1)S(1)}, bf16[8,208,128]{2,1,0:T(8,128)(2,1)S(1)}, bf16[48,320,256]{2,1,0:T(8,128)(2,1)S(1)}, bf16[22,384,256]{2,1,...) custom-call(bf16[4,12,64,128]{3,2,1,0:T(8,128)(2,1)S(1)} %collective, ...), custom_call_target="tpu_custom_call", output_to_operand_aliasing={{2}: (9, {}), {3}: (10, {}), {4}: (11, {}), {5}: (12, {}), ... | custom-call | flops 6710886400 | bytes 4194304 | tf_op jit(solution)/shard_map/outer/pallas_call | solution.py:544
  22.9 0.1 collective-permute-start.2
  23.1 1.7 %output.1 = bf16[4,32,64,128]{3,2,1,0:T(8,128)(2,1)} custom-call(bf16[16,256,256]{2,1,0:T(8,128)(2,1)S(1)} %get-tuple-element.116.value), custom_call_target="tpu_custom_call" | custom-call | flops 419430400 | bytes 4194304 | tf_op jit(solution)/shard_map/output/pallas_call | solution.py:554
  24.7 0.0 collective-permute-done.2
  24.8 0.1 add_convert_fusion
  24.9 11.6 %all_to_all.10.parts = bf16[8,208,128]{2,1,0:T(8,128)(2,1)S(1)} all-to-all(bf16[8,208,128]{2,1,0:T(8,128)(2,1)S(1)} %add_convert_fusion), channel_id=1, replica_groups=mesh['side'=2,'snap'=4,'x'=2,'core'=2] {'snap','x'}, dimensions={0} | all-to-all | bytes 851968 | tf_op jit(solution)/shard_map/all_to_all | solution.py:563
  36.5 0.1 partial.1.own
  36.6 2.4 %collective-permute-start.3 = (bf16[208,128]{1,0:T(8,128)(2,1)S(1)}, bf16[208,128]{1,0:T(8,128)(2,1)S(1)}, u32[]{:S(2)}, u32[]{:S(2)}) collective-permute-start(bf16[208,128]{1,0:T(8,128)(2,1)S(1)} %partial.1.own), channel_id=1, source_target_pairs={{0,16},{16,0},{1,17},{17,1},{2,18},{18,2},{3,19},{19,3},{4,20},{20... | collective-permute-start | bytes 159752 | tf_op jit(solution)/shard_map/ppermute | solution.py:566
  39.0 0.0 copy-start.3
  39.0 4.2 %scatter.1 = (f32[16,256,256]{2,1,0:T(8,128)S(1)}, f32[1600,128]{1,0:T(8,128)S(1)}, f32[1600,128]{1,0:T(8,128)S(1)}, f32[1600,128]{1,0:T(8,128)S(1)}, f32[1600,1...) custom-call(bf16[18,128,256]{2,1,0:T(8,128)(2,1)S(1)} %get-tuple-element.121.e_rows, ...), custom_call_target="tpu_custom_call" | custom-call | flops 1677721600 | bytes 4194304 | tf_op jit(solution)/shard_map/scatter/pallas_call | solution.py:579
  43.1 0.0 collective-permute-done.3.other
  43.2 9.5 %all_to_all.11.totals = bf16[8,208,128]{2,1,0:T(8,128)(2,1)S(1)} all-to-all(bf16[8,208,128]{2,1,0:T(8,128)(2,1)S(1)} %total.1), channel_id=1, replica_groups=mesh['side'=2,'snap'=4,'x'=2,'core'=2] {'snap','x'}, dimensions={0} | all-to-all | bytes 851968 | tf_op jit(solution)/shard_map/all_to_all | solution.py:593
  52.7 2.6 %collective-permute-start.4 = (bf16[8,208,128]{2,1,0:T(8,128)(2,1)S(1)}, bf16[8,208,128]{2,1,0:T(8,128)(2,1)S(1)}, u32[]{:S(2)}, u32[]{:S(2)}) collective-permute-start(bf16[8,208,128]{2,1,0:T(8,128)(2,1)S(1)} %all_to_all.11.totals), channel_id=1, source_target_pairs={{0,1},{1,0},{2,3},{3,2},{4,5},{5,4},{6,7},{7,6},{8,9},{9,8},{10,11... | collective-permute-start | bytes 1277960 | tf_op jit(solution)/shard_map/ppermute | solution.py:595
  55.3 0.0 copy-done.3
  55.3 0.0 copy-done.4
  55.3 3.0 %update_own.1 = (f32[1,192]{1,0:T(1,128)}, f32[1,192]{1,0:T(1,128)}, f32[1,192]{1,0:T(1,128)}, f32[1,192]{1,0:T(1,128)}, bf16[192]{0:T(256)(128)(2,1)}, /*index=...) custom-call(bf16[8,208,128]{2,1,0:T(8,128)(2,1)S(1)} %all_to_all.11., ...), custom_call_target="tpu_custom_call" | custom-call | flops 1048576 | bytes 4194304 | tf_op jit(solution)/shard_map/update_own/pallas_call | solution.py:599
  58.4 0.0 collective-permute-done.4.totals
  58.4 2.0 %update_other.1 = (f32[1600,128]{1,0:T(8,128)}, f32[1600,128]{1,0:T(8,128)}, f32[1600,128]{1,0:T(8,128)}, f32[1600,128]{1,0:T(8,128)}, bf16[1600,128]{1,0:T(8,12...) custom-call(bf16[8,208,128]{2,1,0:T(8,128)(2,1)S(1)} %collective-per, ...), custom_call_target="tpu_custom_call", output_to_operand_aliasing={{0}: (7, {}), {1}: (8, {}), {2}: (9, {}), {3}: (10, {}), {4... | custom-call | flops 1048576 | bytes 4194304 | tf_op jit(solution)/shard_map/update_other/pallas_call | solution.py:611
  (2 shorter events, 0.0 us)
Async XLA Ops:
  0.7 5.3 %copy-start.1 = (bf16[4,32,64,128]{3,2,1,0:T(8,128)(2,1)S(1)}, bf16[4,32,64,128]{3,2,1,0:T(8,128)(2,1)}, u32[]{:S(2)}) copy-start(bf16[4,32,64,128]{3,2,1,0:T(8,128)(2,1)} %cv.1) | copy-start | bytes 6291460
  0.7 5.3 %copy-start = (bf16[4,32,64,128]{3,2,1,0:T(8,128)(2,1)S(1)}, bf16[4,32,64,128]{3,2,1,0:T(8,128)(2,1)}, u32[]{:S(2)}) copy-start(bf16[4,32,64,128]{3,2,1,0:T(8,128)(2,1)} %xv.1) | copy-start | bytes 6291460
  0.7 5.3 %copy-start.2 = (f32[192]{0:T(256)S(1)}, f32[192]{0:T(256)}, u32[]{:S(2)}) copy-start(f32[192]{0:T(256)} %param.19) | copy-start | bytes 2308
  0.7 5.3 %copy-start.5 = (s32[4]{0:T(128)S(1)}, s32[4]{0:T(128)}, u32[]{:S(2)}) copy-start(s32[4]{0:T(128)} %param.16) | copy-start | bytes 52
  2.2 13.3 %collective-permute-start = (bf16[4,12,64,128]{3,2,1,0:T(8,128)(2,1)S(1)}, bf16[4,12,64,128]{3,2,1,0:T(8,128)(2,1)S(1)}, u32[]{:S(2)}, u32[]{:S(2)}) collective-permute-start(bf16[4,12,64,128]{3,2,1,0:T(8,128)(2,1)S(1)} %get-tuple-element.94), channel_id=1, source_target_pairs={{1,2},{2,1},{0,4},{3,7},{5,6},{6,5},{4,0},{7,3},{9,10},{10,9},{8,1... | collective-permute-start | bytes 2359304 | tf_op jit(solution)/shard_map/ppermute | solution.py:518
  4.9 10.7 %collective-permute-start.1 = (bf16[4,12,64,128]{3,2,1,0:T(8,128)(2,1)S(1)}, bf16[4,12,64,128]{3,2,1,0:T(8,128)(2,1)S(1)}, u32[]{:S(2)}, u32[]{:S(2)}) collective-permute-start(bf16[4,12,64,128]{3,2,1,0:T(8,128)(2,1)S(1)} %get-tuple-element.95), channel_id=1, source_target_pairs={{0,1},{1,0},{2,3},{3,2},{4,5},{5,4},{6,7},{7,6},{8,9},{9,8},{10,11... | collective-permute-start | bytes 2359304 | tf_op jit(solution)/shard_map/ppermute | solution.py:519
  22.9 1.8 %collective-permute-start.2 = (bf16[8,208,128]{2,1,0:T(8,128)(2,1)S(1)}, bf16[8,208,128]{2,1,0:T(8,128)(2,1)S(1)}, u32[]{:S(2)}, u32[]{:S(2)}) collective-permute-start(bf16[8,208,128]{2,1,0:T(8,128)(2,1)S(1)} %get-tuple-element.115), channel_id=1, source_target_pairs={{0,1},{1,0},{2,3},{3,2},{4,5},{5,4},{6,7},{7,6},{8,9},{9,8},{10,11... | collective-permute-start | bytes 1277960 | tf_op jit(solution)/shard_map/ppermute | solution.py:553
  36.6 6.6 %collective-permute-start.3 = (bf16[208,128]{1,0:T(8,128)(2,1)S(1)}, bf16[208,128]{1,0:T(8,128)(2,1)S(1)}, u32[]{:S(2)}, u32[]{:S(2)}) collective-permute-start(bf16[208,128]{1,0:T(8,128)(2,1)S(1)} %partial.1.own), channel_id=1, source_target_pairs={{0,16},{16,0},{1,17},{17,1},{2,18},{18,2},{3,19},{19,3},{4,20},{20... | collective-permute-start | bytes 159752 | tf_op jit(solution)/shard_map/ppermute | solution.py:566
  39.0 16.4 %copy-start.3 = (f32[192]{0:T(256)S(1)}, f32[192]{0:T(256)}, u32[]{:S(2)}) copy-start(f32[192]{0:T(256)} %param.22) | copy-start | bytes 2308
  39.0 16.4 %copy-start.4 = (f32[192]{0:T(256)S(1)}, f32[192]{0:T(256)}, u32[]{:S(2)}) copy-start(f32[192]{0:T(256)} %param.25) | copy-start | bytes 2308
  52.7 5.7 %collective-permute-start.4 = (bf16[8,208,128]{2,1,0:T(8,128)(2,1)S(1)}, bf16[8,208,128]{2,1,0:T(8,128)(2,1)S(1)}, u32[]{:S(2)}, u32[]{:S(2)}) collective-permute-start(bf16[8,208,128]{2,1,0:T(8,128)(2,1)S(1)} %all_to_all.11.totals), channel_id=1, source_target_pairs={{0,1},{1,0},{2,3},{3,2},{4,5},{5,4},{6,7},{7,6},{8,9},{9,8},{10,11... | collective-permute-start | bytes 1277960 | tf_op jit(solution)/shard_map/ppermute | solution.py:595

commit v7 on v6

--- a/solution.py
+++ b/solution.py
@@ -267,7 +267,7 @@
         for n in range(count):
             decode_row(w + n, True, wd2, bias_dec[...], seeds, l3, d5, value, dsum)
 
-    chunked(0, R, U, columns)
+    columns(0, R)
     copies[0].wait()
     we2[...] = we[...].reshape(KERNEL_ROWS, 128).T.astype(BF16)
     chunked(4, I + 2, U, encode)

time: 60.8 us -> 60.8 us (level)
  transfers between devices with their start and end apart: 5 -> 5, of which waited for: 0 -> 0; matrix products, arithmetic and copies ran while one was open for 0% -> 0% of each run, Pallas kernels for 30% -> 31%
where the time goes in v7:
time: 60.8 us; the launch traced here: 60.5 us
  Pallas kernels  29.6 us (49%)
  blocking collectives  20.9 us (34%)
  starting transfers between devices  8.24 us (14%)
  between operations  1.63 us (3%)
    all_to_all x1, blocking collectives, on_device(): parts = lax.all_to_all(part, ('snap', 'x'), 0, 0, tiled=True)  11.4 us
    pallas_call x1, Pallas kernels, on_device(): call(functools.partial(inner_kernel, R, U), 'inner', INNER_MB, 2 * conv,...  9.75 us
    all_to_all x1, blocking collectives, on_device(): mine = lax.all_to_all(wide, ('snap', 'x'), 0, 0, tiled=True)  9.51 us
    pallas_call x1, Pallas kernels, on_device(): call(functools.partial(outer_kernel, R), 'outer', OUTER_MB, 4 * conv, out...  7.33 us
    pallas_call x1, Pallas kernels, on_device(): call(functools.partial(scatter_kernel, R, U), 'scatter', FIELD_MB, conv,...  4.16 us
    pallas_call x1, Pallas kernels, on_device(): call(functools.partial(own_update_kernel, R), 'update_own', UPDATE_MB, 1...  3.02 us
    ppermute x1, starting transfers between devices, on_device(): lax.ppermute(far, ('snap', 'x', 'core'), far_pairs(lax.axis_size('snap'),...  2.67 us
    ppermute x1, starting transfers between devices, on_device(): other = lax.ppermute(mine, 'core', swap)  2.64 us
  transfers between devices with their start and end apart: 5, of which 0 were waited for; matrix products, arithmetic and copies ran while one was open for 0% of the time, Pallas kernels for 31%

profile of v7, /device:TPU:1, one launch (start us, length us, event | category | flops | bytes accessed | tf_op | source)
XLA Modules:
  0.0 60.5 jit_solution(16752992790714387472)
XLA Ops:
  0.7 0.0 copy-start.1
  0.7 0.0 copy-start
  0.7 0.0 copy-start.2
  0.7 0.0 copy-start.5
  0.7 1.5 %halo.1 = (bf16[4,12,64,128]{3,2,1,0:T(8,128)(2,1)S(1)}, bf16[4,12,64,128]{3,2,1,0:T(8,128)(2,1)S(1)}) custom-call(bf16[4,32,64,128]{3,2,1,0:T(8,128)(2,1)} %xv.1, bf16[4,32,64,128]{3,2,1,0:T(8,128)(2,1)} %cv.1), custom_call_target="tpu_custom_call" | custom-call | bytes 4194304 | tf_op jit(solution)/shard_map/halo/pallas_call | solution.py:511
  2.2 2.7 %collective-permute-start = (bf16[4,12,64,128]{3,2,1,0:T(8,128)(2,1)S(1)}, bf16[4,12,64,128]{3,2,1,0:T(8,128)(2,1)S(1)}, u32[]{:S(2)}, u32[]{:S(2)}) collective-permute-start(bf16[4,12,64,128]{3,2,1,0:T(8,128)(2,1)S(1)} %get-tuple-element.94), channel_id=1, source_target_pairs={{1,2},{2,1},{0,4},{3,7},{5,6},{6,5},{4,0},{7,3},{9,10},{10,9},{8,1... | collective-permute-start | bytes 2359304 | tf_op jit(solution)/shard_map/ppermute | solution.py:518
  4.9 0.4 collective-permute-start.1
  6.0 0.0 copy-done.1
  6.0 0.0 copy-done
  6.0 0.0 copy-done.2
  6.0 0.0 copy-done.5
  6.0 9.8 %inner.1 = (bf16[48,320,256]{2,1,0:T(8,128)(2,1)S(1)}, bf16[22,384,256]{2,1,0:T(8,128)(2,1)S(1)}, f32[18,128,256]{2,1,0:T(8,128)S(1)}, bf16[40,320,256]{2,1,0:T(...) custom-call(bf16[4,32,64,128]{3,2,1,0:T(8,128)(2,1)S(1)} %copy-done,, ...), custom_call_target="tpu_custom_call" | custom-call | flops 3355443200 | bytes 4194304 | tf_op jit(solution)/shard_map/inner/pallas_call | solution.py:532
  15.8 0.0 collective-permute-done.far
  15.8 0.0 collective-permute-done.1.near
  15.8 7.3 %outer.1 = (bf16[8,208,128]{2,1,0:T(8,128)(2,1)S(1)}, bf16[8,208,128]{2,1,0:T(8,128)(2,1)S(1)}, bf16[48,320,256]{2,1,0:T(8,128)(2,1)S(1)}, bf16[22,384,256]{2,1,...) custom-call(bf16[4,12,64,128]{3,2,1,0:T(8,128)(2,1)S(1)} %collective, ...), custom_call_target="tpu_custom_call", output_to_operand_aliasing={{2}: (9, {}), {3}: (10, {}), {4}: (11, {}), {5}: (12, {}), ... | custom-call | flops 6710886400 | bytes 4194304 | tf_op jit(solution)/shard_map/outer/pallas_call | solution.py:544
  23.1 0.1 collective-permute-start.2
  23.3 1.7 %output.1 = bf16[4,32,64,128]{3,2,1,0:T(8,128)(2,1)} custom-call(bf16[16,256,256]{2,1,0:T(8,128)(2,1)S(1)} %get-tuple-element.116.value), custom_call_target="tpu_custom_call" | custom-call | flops 419430400 | bytes 4194304 | tf_op jit(solution)/shard_map/output/pallas_call | solution.py:554
  25.0 0.0 collective-permute-done.2
  25.0 0.1 add_convert_fusion
  25.1 11.4 %all_to_all.10.parts = bf16[8,208,128]{2,1,0:T(8,128)(2,1)S(1)} all-to-all(bf16[8,208,128]{2,1,0:T(8,128)(2,1)S(1)} %add_convert_fusion), channel_id=1, replica_groups=mesh['side'=2,'snap'=4,'x'=2,'core'=2] {'snap','x'}, dimensions={0} | all-to-all | bytes 851968 | tf_op jit(solution)/shard_map/all_to_all | solution.py:563
  36.5 0.1 partial.1.own
  36.6 2.4 %collective-permute-start.3 = (bf16[208,128]{1,0:T(8,128)(2,1)S(1)}, bf16[208,128]{1,0:T(8,128)(2,1)S(1)}, u32[]{:S(2)}, u32[]{:S(2)}) collective-permute-start(bf16[208,128]{1,0:T(8,128)(2,1)S(1)} %partial.1.own), channel_id=1, source_target_pairs={{0,16},{16,0},{1,17},{17,1},{2,18},{18,2},{3,19},{19,3},{4,20},{20... | collective-permute-start | bytes 159752 | tf_op jit(solution)/shard_map/ppermute | solution.py:566
  39.0 0.0 copy-start.3
  39.0 4.2 %scatter.1 = (f32[16,256,256]{2,1,0:T(8,128)S(1)}, f32[1600,128]{1,0:T(8,128)S(1)}, f32[1600,128]{1,0:T(8,128)S(1)}, f32[1600,128]{1,0:T(8,128)S(1)}, f32[1600,1...) custom-call(bf16[18,128,256]{2,1,0:T(8,128)(2,1)S(1)} %get-tuple-element.121.e_rows, ...), custom_call_target="tpu_custom_call" | custom-call | flops 1677721600 | bytes 4194304 | tf_op jit(solution)/shard_map/scatter/pallas_call | solution.py:579
  43.1 0.0 collective-permute-done.3.other
  43.2 9.5 %all_to_all.11.totals = bf16[8,208,128]{2,1,0:T(8,128)(2,1)S(1)} all-to-all(bf16[8,208,128]{2,1,0:T(8,128)(2,1)S(1)} %total.1), channel_id=1, replica_groups=mesh['side'=2,'snap'=4,'x'=2,'core'=2] {'snap','x'}, dimensions={0} | all-to-all | bytes 851968 | tf_op jit(solution)/shard_map/all_to_all | solution.py:593
  52.7 2.6 %collective-permute-start.4 = (bf16[8,208,128]{2,1,0:T(8,128)(2,1)S(1)}, bf16[8,208,128]{2,1,0:T(8,128)(2,1)S(1)}, u32[]{:S(2)}, u32[]{:S(2)}) collective-permute-start(bf16[8,208,128]{2,1,0:T(8,128)(2,1)S(1)} %all_to_all.11.totals), channel_id=1, source_target_pairs={{0,1},{1,0},{2,3},{3,2},{4,5},{5,4},{6,7},{7,6},{8,9},{9,8},{10,11... | collective-permute-start | bytes 1277960 | tf_op jit(solution)/shard_map/ppermute | solution.py:595
  55.3 0.0 copy-done.3
  55.3 0.0 copy-done.4
  55.3 3.0 %update_own.1 = (f32[1,192]{1,0:T(1,128)}, f32[1,192]{1,0:T(1,128)}, f32[1,192]{1,0:T(1,128)}, f32[1,192]{1,0:T(1,128)}, bf16[192]{0:T(256)(128)(2,1)}, /*index=...) custom-call(bf16[8,208,128]{2,1,0:T(8,128)(2,1)S(1)} %all_to_all.11., ...), custom_call_target="tpu_custom_call" | custom-call | flops 1048576 | bytes 4194304 | tf_op jit(solution)/shard_map/update_own/pallas_call | solution.py:599
  58.4 0.0 collective-permute-done.4.totals
  58.4 2.0 %update_other.1 = (f32[1600,128]{1,0:T(8,128)}, f32[1600,128]{1,0:T(8,128)}, f32[1600,128]{1,0:T(8,128)}, f32[1600,128]{1,0:T(8,128)}, bf16[1600,128]{1,0:T(8,12...) custom-call(bf16[8,208,128]{2,1,0:T(8,128)(2,1)S(1)} %collective-per, ...), custom_call_target="tpu_custom_call", output_to_operand_aliasing={{0}: (7, {}), {1}: (8, {}), {2}: (9, {}), {3}: (10, {}), {4... | custom-call | flops 1048576 | bytes 4194304 | tf_op jit(solution)/shard_map/update_other/pallas_call | solution.py:611
  (2 shorter events, 0.0 us)
Async XLA Ops:
  0.7 5.3 %copy-start.1 = (bf16[4,32,64,128]{3,2,1,0:T(8,128)(2,1)S(1)}, bf16[4,32,64,128]{3,2,1,0:T(8,128)(2,1)}, u32[]{:S(2)}) copy-start(bf16[4,32,64,128]{3,2,1,0:T(8,128)(2,1)} %cv.1) | copy-start | bytes 6291460
  0.7 5.3 %copy-start = (bf16[4,32,64,128]{3,2,1,0:T(8,128)(2,1)S(1)}, bf16[4,32,64,128]{3,2,1,0:T(8,128)(2,1)}, u32[]{:S(2)}) copy-start(bf16[4,32,64,128]{3,2,1,0:T(8,128)(2,1)} %xv.1) | copy-start | bytes 6291460
  0.7 5.3 %copy-start.2 = (f32[192]{0:T(256)S(1)}, f32[192]{0:T(256)}, u32[]{:S(2)}) copy-start(f32[192]{0:T(256)} %param.19) | copy-start | bytes 2308
  0.7 5.3 %copy-start.5 = (s32[4]{0:T(128)S(1)}, s32[4]{0:T(128)}, u32[]{:S(2)}) copy-start(s32[4]{0:T(128)} %param.16) | copy-start | bytes 52
  2.2 13.5 %collective-permute-start = (bf16[4,12,64,128]{3,2,1,0:T(8,128)(2,1)S(1)}, bf16[4,12,64,128]{3,2,1,0:T(8,128)(2,1)S(1)}, u32[]{:S(2)}, u32[]{:S(2)}) collective-permute-start(bf16[4,12,64,128]{3,2,1,0:T(8,128)(2,1)S(1)} %get-tuple-element.94), channel_id=1, source_target_pairs={{1,2},{2,1},{0,4},{3,7},{5,6},{6,5},{4,0},{7,3},{9,10},{10,9},{8,1... | collective-permute-start | bytes 2359304 | tf_op jit(solution)/shard_map/ppermute | solution.py:518
  4.9 10.9 %collective-permute-start.1 = (bf16[4,12,64,128]{3,2,1,0:T(8,128)(2,1)S(1)}, bf16[4,12,64,128]{3,2,1,0:T(8,128)(2,1)S(1)}, u32[]{:S(2)}, u32[]{:S(2)}) collective-permute-start(bf16[4,12,64,128]{3,2,1,0:T(8,128)(2,1)S(1)} %get-tuple-element.95), channel_id=1, source_target_pairs={{0,1},{1,0},{2,3},{3,2},{4,5},{5,4},{6,7},{7,6},{8,9},{9,8},{10,11... | collective-permute-start | bytes 2359304 | tf_op jit(solution)/shard_map/ppermute | solution.py:519
  23.1 1.8 %collective-permute-start.2 = (bf16[8,208,128]{2,1,0:T(8,128)(2,1)S(1)}, bf16[8,208,128]{2,1,0:T(8,128)(2,1)S(1)}, u32[]{:S(2)}, u32[]{:S(2)}) collective-permute-start(bf16[8,208,128]{2,1,0:T(8,128)(2,1)S(1)} %get-tuple-element.115), channel_id=1, source_target_pairs={{0,1},{1,0},{2,3},{3,2},{4,5},{5,4},{6,7},{7,6},{8,9},{9,8},{10,11... | collective-permute-start | bytes 1277960 | tf_op jit(solution)/shard_map/ppermute | solution.py:553
  36.6 6.6 %collective-permute-start.3 = (bf16[208,128]{1,0:T(8,128)(2,1)S(1)}, bf16[208,128]{1,0:T(8,128)(2,1)S(1)}, u32[]{:S(2)}, u32[]{:S(2)}) collective-permute-start(bf16[208,128]{1,0:T(8,128)(2,1)S(1)} %partial.1.own), channel_id=1, source_target_pairs={{0,16},{16,0},{1,17},{17,1},{2,18},{18,2},{3,19},{19,3},{4,20},{20... | collective-permute-start | bytes 159752 | tf_op jit(solution)/shard_map/ppermute | solution.py:566
  39.0 16.4 %copy-start.3 = (f32[192]{0:T(256)S(1)}, f32[192]{0:T(256)}, u32[]{:S(2)}) copy-start(f32[192]{0:T(256)} %param.22) | copy-start | bytes 2308
  39.0 16.4 %copy-start.4 = (f32[192]{0:T(256)S(1)}, f32[192]{0:T(256)}, u32[]{:S(2)}) copy-start(f32[192]{0:T(256)} %param.25) | copy-start | bytes 2308
  52.7 5.7 %collective-permute-start.4 = (bf16[8,208,128]{2,1,0:T(8,128)(2,1)S(1)}, bf16[8,208,128]{2,1,0:T(8,128)(2,1)S(1)}, u32[]{:S(2)}, u32[]{:S(2)}) collective-permute-start(bf16[8,208,128]{2,1,0:T(8,128)(2,1)S(1)} %all_to_all.11.totals), channel_id=1, source_target_pairs={{0,1},{1,0},{2,3},{3,2},{4,5},{5,4},{6,7},{7,6},{8,9},{9,8},{10,11... | collective-permute-start | bytes 1277960 | tf_op jit(solution)/shard_map/ppermute | solution.py:595
